TPU v7x, 256 devices: a whole 4x4x8 slice. The times are simulated.
256 devices in a mesh: dp: 16 (over z, core), mp: 16 (over x, y).
Axes of the slice: x: 4, y: 4, z: 8, core: 2. Of those that a mesh axis runs over, the one named last changes fastest.
Arguments:
- gradients: bfloat16 [64, 2, 4096, 512], P('mp', None, 'dp'), may hold values from -50 to 50
- moments: bfloat16 [64, 2, 4096, 512], P('mp', None, 'dp'), may hold values from -6 to 6
- weights: bfloat16 [64, 2, 4096, 512], P('mp', None, 'dp'), may hold values from -6 to 6
- head_logits: float32 [16, 64, 32], P('mp'), may hold values from 10 to 200
Outputs:
- new_weights: bfloat16 [64, 2, 4096, 512], P('mp', None, 'dp')
- new_moments: bfloat16 [64, 2, 4096, 512], P('mp', None, 'dp')
- updates: bfloat16 [64, 2, 4096, 512], P('mp', None, 'dp')
All inputs are finite; a program needn't handle non-finite values.
Results may differ from a plain program's by a relative error of at most 0.0086.
Values may be sent and summed in bfloat16 or wider, within the bound.
No kernel may reach another device: no remote copies, remote signals or barrier semaphores. Data moves between devices by JAX's collectives and lax.ppermute only.
A program may use at most 64 MiB of HBM per device.

v0:
```python
import math

import jax
import jax.numpy as jnp
from jax import lax
from jax.sharding import PartitionSpec as P

DK = 128
ITERS = 3


FIRST_COEFF = 3.4445
SECOND_COEFF = -4.775
THIRD_COEFF = 2.0315
MOMENTUM = 0.95
LEARN_RATE = 0.1
SHRINK = 0.99
CLIP_LIMIT = 100.0
EPSILON = 1e-07


def newton(arrived, combine):
    widened = arrived.astype(jnp.float32)
    squares = combine(jnp.sum(widened * widened))
    current = (widened / (jnp.sqrt(squares) + EPSILON)).astype(jnp.bfloat16)
    for _ in range(ITERS):
        gram_matrix = combine(
            lax.dot_general(
                current, current, (((0,), (0,)), ((), ())), preferred_element_type=jnp.float32
            )
        )
        gram_low = lax.optimization_barrier(gram_matrix.astype(jnp.bfloat16))
        square = jnp.dot(gram_low, gram_low, preferred_element_type=jnp.float32)
        polynomial = (SECOND_COEFF * gram_low.astype(jnp.float32) + THIRD_COEFF * square).astype(
            jnp.bfloat16
        )
        current = (
            FIRST_COEFF * current.astype(jnp.float32)
            + jnp.dot(current, polynomial, preferred_element_type=jnp.float32)
        ).astype(jnp.bfloat16)
    return current


def shards(gradients, moments, weights, head_logits):
    layers, kind_count, row_count, latent_width = gradients.shape
    matrices = layers * kind_count
    parties = lax.axis_size("dp")
    merged = lax.pmax(head_logits, "mp")[0]
    own_peaks = lax.dynamic_slice_in_dim(merged, lax.axis_index("mp") * layers, layers, 0)
    widened = gradients.astype(jnp.float32)
    moment_sum = MOMENTUM * moments.astype(jnp.float32) + widened
    new_moments = moment_sum.astype(jnp.bfloat16)
    advance = (widened + MOMENTUM * moment_sum).astype(jnp.bfloat16)
    splits = 1

    def combine(partial_value):
        return partial_value

    piece_rows = row_count // splits
    outgoing = advance.reshape(matrices * splits, piece_rows, latent_width)
    unused = parties - matrices * splits
    outgoing = jnp.concatenate(
        [outgoing, jnp.zeros((unused, piece_rows, latent_width), jnp.bfloat16)], axis=0
    )
    arrived = lax.all_to_all(outgoing, "dp", split_axis=0, concat_axis=1, tiled=True)
    finished = newton(arrived[0], combine)
    returned = lax.all_to_all(finished[None], "dp", split_axis=1, concat_axis=0, tiled=True)
    ortho_rows = returned[: matrices * splits].reshape(layers, kind_count, row_count, latent_width)
    scaled = (
        0.2 * math.sqrt(max(row_count * parties, latent_width)) * ortho_rows.astype(jnp.float32)
    )
    updates = scaled.astype(jnp.bfloat16)
    clip_ratio = jnp.sqrt(jnp.minimum(1.0, CLIP_LIMIT / own_peaks))
    head_count = clip_ratio.shape[1]
    row_head = (lax.axis_index("dp") * row_count + jnp.arange(row_count, dtype=jnp.int32)) // DK
    head_match = (row_head[:, None] == jnp.arange(head_count, dtype=jnp.int32)[None, :]).astype(
        jnp.float32
    )
    key_factor = jnp.sum(clip_ratio[:, None, :] * head_match[None, :, :], axis=2)
    factor = jnp.stack([key_factor, jnp.ones_like(key_factor)], axis=1)[..., None]
    new_weights = ((weights.astype(jnp.float32) * SHRINK - LEARN_RATE * scaled) * factor).astype(
        jnp.bfloat16
    )
    return (new_weights, new_moments, updates)


def solution(mesh):
    return jax.shard_map(
        shards,
        mesh=mesh,
        in_specs=(
            P("mp", None, "dp", None),
            P("mp", None, "dp", None),
            P("mp", None, "dp", None),
            P("mp", None, None),
        ),
        out_specs=(P("mp", None, "dp", None), P("mp", None, "dp", None), P("mp", None, "dp", None)),
        check_vma=False,
    )
```

profile of v0, /device:TPU:1, one launch (start us, length us, event | category | flops | bytes accessed | tf_op | source)
XLA Modules:
  0.0 324.0 jit_solution(2021136060777418198)
XLA Ops:
  0.6 4.5 %fusion.5 = (bf16[4,2,256,512]{3,2,1,0:T(8,128)(2,1)}, bf16[4,2,256,512]{3,2,1,0:T(8,128)(2,1)S(1)}) fusion(bf16[4,2,256,512]{3,2,1,0:T(8,128)(2,1)} %param.4, bf16[4,2,256,512]{3,2,1,0:T(8,128)(2,1)} %param.5), kind=kLoop, calls=%fused_computation.15 | loop fusion | flops 8388608 | bytes 8388608 | tf_op jit(solution)/shard_map/convert_element_type | solution.py:52
  5.2 0.4 concatenate.3
  5.5 105.7 %all_to_all.21 = bf16[16,256,512]{2,1,0:T(8,128)(2,1)S(1)} all-to-all(bf16[16,256,512]{2,1,0:T(8,128)(2,1)S(1)} %concatenate.3), channel_id=1, replica_groups=mesh['dp'=16,'mp'=16] {'dp'}, dimensions={0} | all-to-all | bytes 8388608 | tf_op jit(solution)/shard_map/all_to_all | solution.py:65
  111.3 0.0 copy-start
  111.3 1.9 copy-done
  113.2 2.8 fusion
  116.7 3.1 fusion.1
  119.8 0.0 copy-start.1
  119.8 2.4 fusion.9
  122.2 0.0 copy-done.1
  122.2 7.6 %add_convert_fusion.2 = bf16[4096,512]{1,0:T(8,128)(2,1)} fusion(bf16[4096,512]{1,0:T(8,128)(2,1)} %bitcast.38, bf16[512,512]{1,0:T(8,128)(2,1)S(1)} %fusion.9), kind=kOutput, calls=%fused_computation.6 | convolution fusion | flops 2425618432 | bytes 8912896 | tf_op jit(solution)/shard_map/dot_general | solution.py:39
  129.8 5.8 %convolution_convert_fusion.1 = bf16[512,512]{1,0:T(8,128)(2,1)S(1)} fusion(bf16[4096,512]{1,0:T(8,128)(2,1)} %add_convert_fusion.2), kind=kOutput, calls=%fused_computation.28 | convolution fusion | flops 2147745792 | bytes 4718592 | tf_op jit(solution)/shard_map/dot_general | solution.py:28
  135.6 7.6 %add_convert_fusion.1 = bf16[4096,512]{1,0:T(8,128)(2,1)} fusion(bf16[4096,512]{1,0:T(8,128)(2,1)} %add_convert_fusion.2, bf16[512,512]{1,0:T(8,128)(2,1)S(1)} %convolution_convert_fusion.1), kind=kOutput, calls=%fused_computation.5 | convolution fusion | flops 2425618432 | bytes 8912896 | tf_op jit(solution)/shard_map/dot_general | solution.py:39
  143.3 5.8 %convolution_convert_fusion = bf16[512,512]{1,0:T(8,128)(2,1)S(1)} fusion(bf16[4096,512]{1,0:T(8,128)(2,1)} %add_convert_fusion.1), kind=kOutput, calls=%fused_computation.27 | convolution fusion | flops 2147745792 | bytes 4718592 | tf_op jit(solution)/shard_map/dot_general | solution.py:28
  149.1 7.6 %fusion.2 = bf16[1,4096,512]{2,1,0:T(8,128)(2,1)} fusion(bf16[4096,512]{1,0:T(8,128)(2,1)} %add_convert_fusion.1, bf16[512,512]{1,0:T(8,128)(2,1)S(1)} %convolution_convert_fusion), kind=kOutput, calls=%fused_computation.7 | convolution fusion | flops 2425618432 | bytes 8912896 | tf_op jit(solution)/shard_map/dot_general | solution.py:39
  156.7 8.6 %copy.32 = bf16[1,4096,512]{2,0,1:T(2,128)(2,1)} copy(bf16[1,4096,512]{2,1,0:T(8,128)(2,1)} %fusion.2) | data formatting | bytes 8388608 | tf_op jit(solution)/shard_map/broadcast_in_dim | solution.py:67
  165.3 0.5 broadcast.120
  165.8 28.7 %reduce.3 = bf16[4096,512]{1,0:T(8,128)(2,1)} reduce(bf16[4096,1,512]{2,1,0:T(2,128)(2,1)} %bitcast.33, bf16[]{:T(256)} %broadcast.120), dimensions={1}, to_apply=%bitcast.32.reduce_sub_computation | reduce | bytes 8388610
  194.5 11.4 %reshape.93 = bf16[16,2,65536]{2,1,0:T(2,128)(2,1)} reshape(bf16[4096,512]{1,0:T(8,128)(2,1)} %reduce.3) | data formatting | bytes 8388608
  205.9 0.0 copy-start.3
  205.9 4.6 %all-to-all-start.1 = ((bf16[16,2,65536]{2,1,0:T(2,128)(2,1)}), bf16[16,2,65536]{2,1,0:T(2,128)(2,1)}, u32[]{:S(2)}, u32[]{:S(2)}) async-start(bf16[16,2,65536]{2,1,0:T(2,128)(2,1)} %reshape.93), calls=%async_computation.1 | async-start | bytes 8388608 | tf_op jit(solution)/shard_map/all_to_all | solution.py:67
  210.5 0.0 copy-done.3
  210.5 0.1 copy.26
  210.6 63.2 %pmax.7 = f32[1,64,32]{2,1,0:T(8,128)S(1)} all-reduce(f32[1,64,32]{2,1,0:T(8,128)S(1)} %copy.26), channel_id=1, replica_groups=mesh['dp'=16,'mp'=16] {'mp'}, use_global_device_ids=true, to_apply=%region_1.0 | all-reduce | flops 2048 | bytes 16384 | tf_op jit(solution)/shard_map/pmax | solution.py:48
  273.9 0.1 multiply_reduce_fusion
  274.0 28.8 %all-to-all-done.1 = bf16[16,2,65536]{2,1,0:T(2,128)(2,1)} async-done(((bf16[16,2,65536]{2,1,0:T(2,128)(2,1)}), bf16[16,2,65536]{2,1,0:T(2,128)(2,1)}, u32[]{:S(2)}, u32[]{:S(2)}) %all-to-all-start.1) | async-done | bytes 4194336 | tf_op jit(solution)/shard_map/all_to_all | solution.py:67
  302.8 12.3 %reshape.94 = bf16[4096,1,512]{2,1,0:T(2,128)(2,1)} reshape(bf16[16,2,65536]{2,1,0:T(2,128)(2,1)} %all-to-all-done.1) | data formatting | bytes 8388608
  315.1 4.6 %copy.29 = bf16[1,4096,512]{2,1,0:T(8,128)(2,1)S(1)} copy(bf16[1,4096,512]{2,0,1:T(2,128)(2,1)} %bitcast.34) | data formatting | bytes 8388608
  319.7 0.0 copy-start.2
  319.7 2.2 fusion.4
  321.9 0.0 copy-done.2
  321.9 2.1 multiply_convert_fusion
  (5 shorter events, 0.0 us)
Async XLA Ops:
  111.3 1.9 copy-start
  119.8 2.4 copy-start.1
  205.9 4.6 %copy-start.3 = (f32[1,64,32]{1,2,0:T(8,128)S(1)}, f32[1,64,32]{1,2,0:T(8,128)}, u32[]{:S(2)}) copy-start(f32[1,64,32]{1,2,0:T(8,128)} %param.7) | copy-start | bytes 24580
  205.9 96.8 %all-to-all-start.1 = ((bf16[16,2,65536]{2,1,0:T(2,128)(2,1)}), bf16[16,2,65536]{2,1,0:T(2,128)(2,1)}, u32[]{:S(2)}, u32[]{:S(2)}) async-start(bf16[16,2,65536]{2,1,0:T(2,128)(2,1)} %reshape.93), calls=%async_computation.1 | async-start | bytes 8388608 | tf_op jit(solution)/shard_map/all_to_all | solution.py:67
  319.7 2.2 copy-start.2
where the time goes:
time: 325 us; the launch traced here: 324 us
  blocking collectives  169 us (52%)
  other arithmetic  43.5 us (13%)
  local copies, waits for them, and re-layouts  39.9 us (12%)
  matrix products  36.9 us (11%)
  waiting for transfers between devices  28.8 us (9%)
  starting transfers between devices  4.57 us (1%)
    all_to_all x1, blocking collectives, shards(): lax.all_to_all(outgoing, 'dp', split_axis=0, concat_axis=1, tiled=True)  106 us
    pmax x1, blocking collectives, shards(): merged = lax.pmax(head_logits, 'mp')[0]  63.2 us
    unnamed x14, local copies, waits for them, and re-layouts  30.9 us
    all_to_all x1, waiting for transfers between devices, shards(): lax.all_to_all(finished[None], 'dp', split_axis=1, concat_axis=0, tiled=T...  28.8 us
    unnamed x1, other arithmetic  28.7 us
    dot_general x3, matrix products, newton(): jnp.dot(current, polynomial, preferred_element_type=jnp.float32)  22.9 us
    dot_general x3, matrix products, newton(): lax.dot_general(current, current, (((0,), (0,)), ((), ())), preferred_ele...  14 us
    broadcast_in_dim x1, local copies, waits for them, and re-layouts, shards(): finished[None]  8.61 us
  transfers between devices with their start and end apart: 1, of which 1 were waited for; matrix products, arithmetic and copies ran while one was open for 0% of the time, Pallas kernels for 0%

commit v1 on v0

v1 whole, which is shorter than its diff:
```python
import math

import jax
import jax.numpy as jnp
from jax import lax
from jax.experimental import pallas as pl
from jax.experimental.pallas import tpu as pltpu
from jax.sharding import PartitionSpec as P

DK = 128
SIDE = 128
EXTRA = 32
PACKED = 8 * SIDE + EXTRA
HALF = PACKED // 2
MEBI = 1024 * 1024

FIRST_COEFF = 3.4445
SECOND_COEFF = -4.775
THIRD_COEFF = 2.0315
MOMENTUM = 0.95
LEARN_RATE = 0.1
SHRINK = 0.99
CLIP_LIMIT = 100.0
EPSILON = 1e-07


def low(value):
    return value.astype(jnp.bfloat16)


def wide(value):
    return value.astype(jnp.float32)


def product(left, right):
    return jnp.dot(low(left), low(right), preferred_element_type=jnp.float32)


def square_iota(dimension):
    return lax.broadcasted_iota(jnp.int32, (SIDE, SIDE), dimension)


def diagonal_row(block):
    return jnp.sum(jnp.where(square_iota(0) == square_iota(1), block, 0.0), axis=0, keepdims=True)


ORDER = ((0, 1), (0, 2), (0, 3)), ((1, 2), (1, 3), (2, 3))


def pack(blocks, residuals=False):
    upper = square_iota(0) <= square_iota(1)
    pieces = []
    for which in range(2):
        even, odd = blocks[2 * which, 2 * which], blocks[2 * which + 1, 2 * which + 1]
        pieces.append(jnp.where(upper, even, odd))
        pieces += [blocks[name] for name in ORDER[which]]
    row = lax.broadcasted_iota(jnp.int32, (EXTRA, SIDE), 0)
    extra = jnp.zeros((EXTRA, SIDE), jnp.float32)
    for i in range(4):
        values = diagonal_row(blocks[i, i])
        extra = jnp.where(row == i, values, extra)
        if residuals:
            extra = jnp.where(row == 4 + i, values - wide(low(values)), extra)
    return jnp.concatenate([low(piece) for piece in pieces + [extra]], axis=0)


def unpack_blocks(packed, dtype):
    rows, columns = square_iota(0), square_iota(1)
    extra = wide(packed[8 * SIDE :])
    blocks = {}
    for which in range(2):
        pieces = [packed[(4 * which + k) * SIDE : (4 * which + k + 1) * SIDE] for k in range(4)]
        both = wide(pieces[0])
        turned = both.T
        first, second = extra[2 * which : 2 * which + 1], extra[2 * which + 1 : 2 * which + 2]
        even = jnp.where(rows < columns, both, jnp.where(rows > columns, turned, first))
        odd = jnp.where(rows > columns, both, jnp.where(rows < columns, turned, second))
        blocks[2 * which, 2 * which] = even.astype(dtype)
        blocks[2 * which + 1, 2 * which + 1] = odd.astype(dtype)
        for name, piece in zip(ORDER[which], pieces[1:]):
            blocks[name] = piece.astype(dtype)
    return blocks, extra


def corner(blocks, i):
    right = blocks[i, i + 1]
    return jnp.concatenate(
        [
            jnp.concatenate([blocks[i, i], right], axis=1),
            jnp.concatenate([wide(right).T.astype(right.dtype), blocks[i + 1, i + 1]], axis=1),
        ],
        axis=0,
    )


def off_corner(blocks):
    return jnp.concatenate(
        [jnp.concatenate([blocks[i, 2], blocks[i, 3]], axis=1) for i in (0, 1)], axis=0
    )


def cut_blocks(matrix):
    return {
        (i, j): matrix[i * SIDE : (i + 1) * SIDE, j * SIDE : (j + 1) * SIDE]
        for i in range(4)
        for j in range(i, 4)
    }


def gram_kernel(
    place_ref, grad_ref, moment_ref, new_moment_ref, advance_ref,
    mine_ref, theirs_ref, far_mine_ref, far_theirs_ref, own_ref,
):
    step = pl.program_id(0)
    widened = wide(grad_ref[0])
    moment_sum = MOMENTUM * wide(moment_ref[0]) + widened
    new_moment_ref[0] = low(moment_sum)
    advance = low(widened + MOMENTUM * moment_sum)
    advance_ref[0] = advance
    middle = 2 * SIDE
    contract = (((0,), (0,)), ((), ()))
    upper = lax.dot_general(
        advance[:, :middle], advance, contract, preferred_element_type=jnp.float32
    )
    lower = lax.dot_general(
        advance[:, middle:], advance[:, middle:], contract, preferred_element_type=jnp.float32
    )
    blocks = {}
    for i in range(2):
        for j in range(i, 4):
            blocks[i, j] = upper[i * SIDE : (i + 1) * SIDE, j * SIDE : (j + 1) * SIDE]
        for j in range(i, 2):
            blocks[i + 2, j + 2] = lower[i * SIDE : (i + 1) * SIDE, j * SIDE : (j + 1) * SIDE]
    packed = pack(blocks)

    @pl.when(step == 0)
    def _():
        on_first = place_ref[1] == 0
        far_mine_ref[...] = jnp.where(on_first, packed[:HALF], packed[HALF:])
        far_theirs_ref[...] = jnp.where(on_first, packed[HALF:], packed[:HALF])

    @pl.when(jnp.logical_and(step % 2 == 1, step < 7))
    def _():
        mine_ref[0] = packed

    @pl.when(jnp.logical_and(step % 2 == 0, step > 0))
    def _():
        theirs_ref[0] = packed

    @pl.when(step == 7)
    def _():
        own_ref[...] = packed


def grams(place, gradients, moments):
    matrices, rows, width = gradients.shape

    def own(step, place):
        distance = 4 - (step + 1) // 2
        carried = (step % 2) == 1
        up = jnp.logical_xor(carried, place[1] == 1)
        signed = jnp.where(up, distance, matrices - distance)
        return (lax.rem(place[0] + signed, matrices), 0, 0)

    def slot(step, place):
        return (jnp.clip((step - 1) // 2, 0, 2), 0, 0)

    full = pl.BlockSpec((1, rows, width), own)
    packed = pl.BlockSpec((1, PACKED, SIDE), slot)
    half = pl.BlockSpec((HALF, SIDE), lambda step, place: (0, 0))
    whole = pl.BlockSpec((PACKED, SIDE), lambda step, place: (0, 0))
    full_shape = jax.ShapeDtypeStruct(gradients.shape, jnp.bfloat16)
    packed_shape = jax.ShapeDtypeStruct((3, PACKED, SIDE), jnp.bfloat16)
    half_shape = jax.ShapeDtypeStruct((HALF, SIDE), jnp.bfloat16)
    whole_shape = jax.ShapeDtypeStruct((PACKED, SIDE), jnp.bfloat16)
    return pl.pallas_call(
        gram_kernel,
        out_shape=(
            full_shape, full_shape, packed_shape, packed_shape, half_shape, half_shape, whole_shape,
        ),
        grid_spec=pltpu.PrefetchScalarGridSpec(
            num_scalar_prefetch=1,
            grid=(matrices,),
            in_specs=[full, full],
            out_specs=(full, full, packed, packed, half, half, whole),
        ),
        compiler_params=pltpu.CompilerParams(vmem_limit_bytes=60 * MEBI),
        cost_estimate=pl.CostEstimate(
            flops=2 * gradients.size * width, bytes_accessed=10 * gradients.size, transcendentals=0
        ),
    )(place, gradients, moments)


def polynomial_kernel(mine_ref, theirs_ref, peaks_ref, out_ref, ratio_ref):
    ratio_ref[...] = jnp.sqrt(jnp.minimum(1.0, CLIP_LIMIT / peaks_ref[...]))
    blocks, _ = unpack_blocks(wide(mine_ref[...]) + wide(theirs_ref[...]), jnp.float32)
    corners = off_corner(blocks)
    gram = jnp.concatenate(
        [
            jnp.concatenate([corner(blocks, 0), corners], axis=1),
            jnp.concatenate([corners.T, corner(blocks, 2)], axis=1),
        ],
        axis=0,
    )
    width = gram.shape[0]
    rows = lax.broadcasted_iota(jnp.int32, (width, width), 0)
    columns = lax.broadcasted_iota(jnp.int32, (width, width), 1)
    diagonal = rows == columns
    norm = jnp.sqrt(jnp.sum(jnp.where(diagonal, gram, 0.0)))
    scale = 1.0 / (norm + EPSILON)
    gram = gram * scale * scale

    def poly(gram):
        return SECOND_COEFF * gram + THIRD_COEFF * product(gram, gram)

    def following(gram, step):
        inner = FIRST_COEFF * gram + product(gram, step)
        return FIRST_COEFF * inner + product(inner, step)

    rest = poly(gram)
    factor = FIRST_COEFF
    gram = following(gram, rest)
    for last in (False, True):
        step = poly(gram)
        if not last:
            gram = following(gram, step)
        rest = FIRST_COEFF * rest + factor * step + product(rest, step)
        factor = factor * FIRST_COEFF
    total = jnp.where(diagonal, rest + factor, rest) * scale
    out_ref[...] = pack(cut_blocks(total), residuals=True)


def polynomial(mine, theirs, peaks):
    width = 4 * SIDE
    whole = pl.BlockSpec(memory_space=pltpu.VMEM)
    return pl.pallas_call(
        polynomial_kernel,
        out_shape=(
            jax.ShapeDtypeStruct((PACKED, SIDE), jnp.bfloat16),
            jax.ShapeDtypeStruct(peaks.shape, jnp.float32),
        ),
        in_specs=[whole, whole, whole],
        out_specs=(whole, whole),
        compiler_params=pltpu.CompilerParams(vmem_limit_bytes=40 * MEBI),
        cost_estimate=pl.CostEstimate(
            flops=9 * 2 * width**3, bytes_accessed=6 * PACKED * SIDE, transcendentals=0
        ),
    )(mine, theirs, peaks)


def finish(place, factors, advance, weights, pieces, distance, results):
    matrices, rows, width = advance.shape
    count = len(pieces)
    middle = width // 2
    scaling = 0.2 * math.sqrt(max(rows * matrices * 2, width))

    def index(step, place):
        below = jnp.logical_xor(step == 1, place[1] == 0)
        signed = jnp.where(below, matrices - distance, distance)
        return lax.rem(place[0] + signed, matrices)

    def kernel(place_ref, factor_ref, advance_ref, weight_ref, *refs):
        new_weight_ref, update_ref, place_out_ref = refs[-4:-1]
        place_out_ref[0] = place_ref[0]
        place_out_ref[1] = place_ref[1]
        matrix_ref = refs[-1]
        step = pl.program_id(0)
        for k in range(count):

            @pl.when(step == k)
            def _():
                blocks, extra = unpack_blocks(refs[k][...], jnp.bfloat16)
                matrix_ref[:middle, :middle] = corner(blocks, 0)
                matrix_ref[:middle, middle:] = off_corner(blocks)
                matrix_ref[middle:width, middle:] = corner(blocks, 2)
                for i in range(4):
                    matrix_ref[width:, i * SIDE : (i + 1) * SIDE] = low(
                        jnp.broadcast_to(extra[4 + i : 5 + i], (16, SIDE))
                    )

        which = index(step, place_ref)
        row = lax.broadcasted_iota(jnp.int32, (rows, 1), 0)
        factor = jnp.where(row < DK, factor_ref[2 * which], factor_ref[2 * which + 1])
        off = matrix_ref[:middle, middle:]
        left, right = advance_ref[0, :, :middle], advance_ref[0, :, middle:]
        halves = (
            jnp.dot(left, matrix_ref[:middle, :middle], preferred_element_type=jnp.float32)
            + lax.dot_general(
                right, off, (((1,), (1,)), ((), ())), preferred_element_type=jnp.float32
            ),
            jnp.dot(left, off, preferred_element_type=jnp.float32)
            + jnp.dot(right, matrix_ref[middle:width, middle:], preferred_element_type=jnp.float32),
        )
        for k, values in enumerate((left, right)):
            columns = slice(k * middle, (k + 1) * middle)
            rest = wide(matrix_ref[width : width + 1, columns])
            scaled = scaling * (halves[k] + wide(values) * rest)
            update_ref[0, :, columns] = low(scaled)
            new_weight = (wide(weight_ref[0, :, columns]) * SHRINK - LEARN_RATE * scaled) * factor
            new_weight_ref[0, :, columns] = low(new_weight)

    full = pl.BlockSpec((1, rows, width), lambda step, place, factors: (index(step, place), 0, 0))
    whole = pl.BlockSpec((PACKED, SIDE), lambda step, place, factors: (0, 0))
    anywhere = pl.BlockSpec(memory_space=pl.ANY)
    shape = jax.ShapeDtypeStruct(advance.shape, jnp.bfloat16)
    carried = [] if results is None else list(results)
    first_carried = 4 + count
    return pl.pallas_call(
        kernel,
        out_shape=(shape, shape, jax.ShapeDtypeStruct((2,), jnp.int32)),
        grid_spec=pltpu.PrefetchScalarGridSpec(
            num_scalar_prefetch=2,
            grid=(count,),
            in_specs=[full, full] + [whole] * count + [anywhere] * len(carried),
            out_specs=(full, full, pl.BlockSpec(memory_space=pltpu.SMEM)),
            scratch_shapes=[pltpu.VMEM((width + 16, width), jnp.bfloat16)],
        ),
        input_output_aliases={first_carried + k: k for k in range(len(carried))},
        compiler_params=pltpu.CompilerParams(vmem_limit_bytes=48 * MEBI),
        cost_estimate=pl.CostEstimate(
            flops=2 * count * rows * width * width,
            bytes_accessed=count * (8 * rows * width + 2 * PACKED * SIDE),
            transcendentals=0,
        ),
    )(place, factors, advance, weights, *pieces, *carried)


def own_peaks_of(logits, observers):
    index = lax.axis_index("mp")
    peaks = logits
    bit = observers // 2
    while bit:
        low_part, high_part = jnp.split(peaks, 2, axis=0)
        upper = (index // bit) % 2 == 1
        sent = jnp.where(upper, low_part, high_part)
        kept = jnp.where(upper, high_part, low_part)
        pairs = [(i, i ^ bit) for i in range(observers)]
        peaks = jnp.maximum(kept, lax.ppermute(sent, "mp", pairs))
        bit //= 2
    return peaks


def shards(gradients, moments, weights, head_logits):
    layers, kind_count, row_count, latent_width = gradients.shape
    matrices = layers * kind_count
    parties = lax.axis_size("dp")
    dp = lax.axis_index("dp")
    core = dp % 2
    place = jnp.stack([dp // 2, core]).astype(jnp.int32)
    stacked = (matrices, row_count, latent_width)

    swap_pairs = [(i, i ^ 1) for i in range(parties)]
    ring_pairs = [(i, (i + 2 - 4 * (i % 2)) % parties) for i in range(parties)]

    def swap(value):
        return lax.ppermute(value, "dp", swap_pairs)

    def onward(value):
        return lax.ppermute(value, "dp", ring_pairs)

    new_moments, advance, mine, theirs, far_mine, far_theirs, own = grams(
        place, gradients.reshape(stacked), moments.reshape(stacked)
    )
    far = onward(low(wide(far_mine) + wide(swap(far_theirs))))
    arrived = swap(theirs)
    blank = jnp.zeros((HALF, SIDE), jnp.float32)
    running = jnp.concatenate(
        [jnp.where(core == 0, wide(far), blank), jnp.where(core == 0, blank, wide(far))], axis=0
    )
    for slot in range(3):
        running = wide(onward(low(wide(mine[slot]) + wide(arrived[slot]) + running)))
    partial = low(wide(own) + running)
    peaks = own_peaks_of(head_logits[0], lax.axis_size("mp"))
    piece, clip_ratio = polynomial(partial, swap(partial), peaks)

    heads = row_count // DK
    key_factor = lax.dynamic_slice_in_dim(clip_ratio, dp * heads, heads, 1)
    factors = jnp.stack([key_factor, jnp.ones_like(key_factor)], axis=1).reshape(-1)

    def final(pieces, distance, results):
        *results, after = finish(
            place, factors, advance, weights.reshape(stacked), pieces, distance, results
        )
        return results, after

    results, _ = final([piece], 0, None)
    piece = onward(piece)
    results, after = final([piece, swap(piece)], 1, results)
    piece = onward(piece)
    results, later = final([piece, swap(piece)], 2, results)
    piece = onward(piece)
    results, _ = final([piece, swap(piece)], 3, results)
    last = onward(jnp.where(after[1] == 0, piece[:HALF], piece[HALF:]))
    last = jnp.where(later[1] < 0, jnp.zeros_like(last), last)
    other = swap(last)
    halves = [jnp.where(core == 0, last, other), jnp.where(core == 0, other, last)]
    (new_weights, updates), _ = final([jnp.concatenate(halves, axis=0)], 4, results)
    whole = gradients.shape
    return (new_weights.reshape(whole), new_moments.reshape(whole), updates.reshape(whole))


def solution(mesh):
    return jax.shard_map(
        shards,
        mesh=mesh,
        in_specs=(
            P("mp", None, "dp", None),
            P("mp", None, "dp", None),
            P("mp", None, "dp", None),
            P("mp", None, None),
        ),
        out_specs=(P("mp", None, "dp", None), P("mp", None, "dp", None), P("mp", None, "dp", None)),
        check_vma=False,
    )
```

time: 325 us -> 91.9 us (0.28)
  blocking collectives: 169 us -> 0 us
  other arithmetic: 43.5 us -> 3.1 us
  starting transfers between devices: 4.57 us -> 42.2 us
  matrix products: 36.9 us -> 0 us
  local copies, waits for them, and re-layouts: 39.9 us -> 3.4 us
  Pallas kernels: 0 us -> 23.7 us
  waiting for transfers between devices: 28.8 us -> 17 us
    all_to_all x1 -> x0, blocking collectives: 106 us -> none  [shards(): lax.all_to_all(outgoing, 'dp', split_axis=0, concat_axis=1, tiled=True)]
    pmax x1 -> x0, blocking collectives: 63.2 us -> none  [shards(): merged = lax.pmax(head_logits, 'mp')[0]]
    ppermute x0 -> x19, starting transfers between devices: none -> 42.2 us  [the longest x8 20.2 us: onward(): return lax.ppermute(value, 'dp', ring_pairs)]
    dot_general x6 -> x0, matrix products: 36.9 us -> none  [the longest x3 22.9 us: newton(): jnp.dot(current, polynomial, preferred_element_type=jnp.float32)]
    unnamed x14 -> x15, local copies, waits for them, and re-layouts: 30.9 us -> 1.85 us
    all_to_all x1 -> x0, waiting for transfers between devices: 28.8 us -> none  [shards(): lax.all_to_all(finished[None], 'dp', split_axis=1, concat_axis=0, tiled=T...]
    unnamed x1 -> x0, other arithmetic: 28.7 us -> none
    pallas_call x0 -> x7, Pallas kernels: none -> 23.7 us  [the longest x5 10.8 us: finish(): pl.pallas_call(kernel, out_shape=(shape, shape, jax.ShapeDtypeStruct((2,)...]
  transfers between devices with their start and end apart: 1 -> 19, of which waited for: 1 -> 11; matrix products, arithmetic and copies ran while one was open for 0% -> 3% of each run, Pallas kernels for 0% -> 7%
where the time goes in v1:
time: 91.9 us; the launch traced here: 91.5 us
  starting transfers between devices  42.2 us (46%)
  Pallas kernels  23.7 us (26%)
  waiting for transfers between devices  17 us (18%)
  local copies, waits for them, and re-layouts  3.4 us (4%)
  other arithmetic  3.1 us (3%)
  between operations  2.19 us (2%)
    ppermute x8, starting transfers between devices, onward(): return lax.ppermute(value, 'dp', ring_pairs)  20.2 us
    ppermute x7, starting transfers between devices, swap(): return lax.ppermute(value, 'dp', swap_pairs)  13.8 us
    pallas_call x5, Pallas kernels, finish(): pl.pallas_call(kernel, out_shape=(shape, shape, jax.ShapeDtypeStruct((2,)...  10.8 us
    ppermute x8, waiting for transfers between devices, onward(): return lax.ppermute(value, 'dp', ring_pairs)  9.87 us
    pallas_call x1, Pallas kernels, grams(): pl.pallas_call(gram_kernel, out_shape=(full_shape, full_shape, packed_sha...  9.29 us
    ppermute x4, starting transfers between devices, own_peaks_of(): peaks = jnp.maximum(kept, lax.ppermute(sent, 'mp', pairs))  8.19 us
    ppermute x4, waiting for transfers between devices, own_peaks_of(): peaks = jnp.maximum(kept, lax.ppermute(sent, 'mp', pairs))  4.83 us
    pallas_call x1, Pallas kernels, polynomial(): pl.pallas_call(polynomial_kernel, out_shape=(jax.ShapeDtypeStruct((PACKED...  3.56 us
  transfers between devices with their start and end apart: 19, of which 11 were waited for; matrix products, arithmetic and copies ran while one was open for 3% of the time, Pallas kernels for 7%

profile of v1, /device:TPU:1, one launch (start us, length us, event | category | flops | bytes accessed | tf_op | source)
XLA Modules:
  0.0 91.5 jit_solution(16036465841067945137)
XLA Ops:
  0.7 0.6 pad_add_fusion.place_ref
  1.3 9.3 %shard_map.67 = (bf16[8,256,512]{2,1,0:T(8,128)(2,1)}, bf16[8,256,512]{2,1,0:T(8,128)(2,1)}, bf16[3,1056,128]{2,1,0:T(8,128)(2,1)}, bf16[3,1056,128]{2,1,0:T(8,1...) custom-call(s32[2]{0:T(128)} %pad_add_fusion.place_ref, ...), custom_call_target="tpu_custom_call" | custom-call | flops 1073741824 | bytes 10485760 | tf_op jit(solution)/shard_map/pallas_call | solution.py:176
  10.6 3.3 %collective-permute-start.1 = (bf16[528,128]{1,0:T(8,128)(2,1)}, bf16[528,128]{1,0:T(8,128)(2,1)S(1)}, u32[]{:S(2)}, u32[]{:S(2)}) collective-permute-start(bf16[528,128]{1,0:T(8,128)(2,1)} %get-tuple-element.28), channel_id=1, source_target_pairs={{0,16},{16,0},{32,48},{48,32},{64,80},{80,64},{96,112},{112,96},{1... | collective-permute-start | bytes 405512 | tf_op jit(solution)/shard_map/ppermute | solution.py:356
  13.9 0.1 collective-permute-start
  14.0 1.1 %collective-permute-done.1 = bf16[528,128]{1,0:T(8,128)(2,1)S(1)} collective-permute-done((bf16[528,128]{1,0:T(8,128)(2,1)}, bf16[528,128]{1,0:T(8,128)(2,1)S(1)}, u32[]{:S(2)}, u32[]{:S(2)}) %collective-permute-start.1) | collective-permute-done | bytes 135200 | tf_op jit(solution)/shard_map/ppermute | solution.py:356
  15.1 0.9 %add_convert_fusion.1 = bf16[528,128]{1,0:T(8,128)(2,1)S(1)} fusion(bf16[528,128]{1,0:T(8,128)(2,1)S(1)} %collective-permute-done.1, bf16[528,128]{1,0:T(8,128)(2,1)} %get-tuple-element.27), kind=kLoop, calls=%fused_computation.10 | loop fusion | flops 270336 | bytes 405504 | tf_op jit(solution)/shard_map/convert_element_type | solution.py:28
  16.0 3.9 %collective-permute-start.2 = (bf16[528,128]{1,0:T(8,128)(2,1)S(1)}, bf16[528,128]{1,0:T(8,128)(2,1)S(1)}, u32[]{:S(2)}, u32[]{:S(2)}) collective-permute-start(bf16[528,128]{1,0:T(8,128)(2,1)S(1)} %add_convert_fusion.1), channel_id=1, source_target_pairs={{0,32},{16,240},{32,64},{48,16},{64,96},{80,48},{96,128},{112,80},... | collective-permute-start | bytes 405512 | tf_op jit(solution)/shard_map/ppermute | solution.py:359
  20.2 1.8 %collective-permute-done.2 = bf16[528,128]{1,0:T(8,128)(2,1)S(1)} collective-permute-done((bf16[528,128]{1,0:T(8,128)(2,1)S(1)}, bf16[528,128]{1,0:T(8,128)(2,1)S(1)}, u32[]{:S(2)}, u32[]{:S(2)}) %collective-permute-start.2) | collective-permute-done | bytes 135200 | tf_op jit(solution)/shard_map/ppermute | solution.py:359
  22.0 1.1 %fusion = bf16[1056,128]{1,0:T(8,128)(2,1)S(1)} fusion(f32[528,128]{1,0:T(8,128)S(1)} %get-tuple-element.48, f32[528,128]{1,0:T(8,128)S(1)} %get-tuple-element.47, bf16[3,1056,128]{2,1,0:T(8,128)(2,1)S(1)} %collective-permute-done, bf16[3,1056,128]{2,1,0:T(8,128)(2,1)} %get-tuple-element.25), kind=kLoop, calls=%fused_computation.1 | loop fusion | flops 811008 | bytes 1351680 | tf_op jit(solution)/shard_map/convert_element_type | solution.py:28
  23.0 3.2 %collective-permute-start.3 = (bf16[1056,128]{1,0:T(8,128)(2,1)S(1)}, bf16[1056,128]{1,0:T(8,128)(2,1)S(1)}, u32[]{:S(2)}, u32[]{:S(2)}) collective-permute-start(bf16[1056,128]{1,0:T(8,128)(2,1)S(1)} %fusion), channel_id=1, source_target_pairs={{0,32},{16,240},{32,64},{48,16},{64,96},{80,48},{96,128},{112,80},... | collective-permute-start | bytes 811016 | tf_op jit(solution)/shard_map/ppermute | solution.py:359
  26.2 2.7 %collective-permute-start.7 = (f32[32,32]{1,0:T(8,128)S(1)}, f32[32,32]{1,0:T(8,128)S(1)}, u32[]{:S(2)}, u32[]{:S(2)}) collective-permute-start(f32[32,32]{1,0:T(8,128)S(1)} %select_bitcast_fusion), channel_id=1, source_target_pairs={{0,8},{1,9},{2,10},{3,11},{4,12},{5,13},{6,14},{7,15},{8,0},{9,1},... | collective-permute-start | bytes 12296 | tf_op jit(solution)/shard_map/ppermute | solution.py:338
  29.0 1.4 %collective-permute-done.7 = f32[32,32]{1,0:T(8,128)S(1)} collective-permute-done((f32[32,32]{1,0:T(8,128)S(1)}, f32[32,32]{1,0:T(8,128)S(1)}, u32[]{:S(2)}, u32[]{:S(2)}) %collective-permute-start.7) | collective-permute-done | bytes 4128 | tf_op jit(solution)/shard_map/ppermute | solution.py:338
  30.3 0.1 fusion.1
  30.5 2.5 %collective-permute-start.4 = (bf16[1056,128]{1,0:T(8,128)(2,1)S(1)}, bf16[1056,128]{1,0:T(8,128)(2,1)S(1)}, u32[]{:S(2)}, u32[]{:S(2)}) collective-permute-start(bf16[1056,128]{1,0:T(8,128)(2,1)S(1)} %fusion.1), channel_id=1, source_target_pairs={{0,32},{16,240},{32,64},{48,16},{64,96},{80,48},{96,128},{112,80},... | collective-permute-start | bytes 811016 | tf_op jit(solution)/shard_map/ppermute | solution.py:359
  33.0 1.2 %collective-permute-start.8 = (f32[16,32]{1,0:T(8,128)S(1)}, f32[16,32]{1,0:T(8,128)S(1)}, u32[]{:S(2)}, u32[]{:S(2)}) collective-permute-start(f32[16,32]{1,0:T(8,128)S(1)} %slice_select_fusion.1), channel_id=1, source_target_pairs={{0,4},{1,5},{2,6},{3,7},{4,0},{5,1},{6,2},{7,3},{8,12},{9,13},{10,... | collective-permute-start | bytes 6152 | tf_op jit(solution)/shard_map/ppermute | solution.py:338
  34.2 1.3 %collective-permute-done.8 = f32[16,32]{1,0:T(8,128)S(1)} collective-permute-done((f32[16,32]{1,0:T(8,128)S(1)}, f32[16,32]{1,0:T(8,128)S(1)}, u32[]{:S(2)}, u32[]{:S(2)}) %collective-permute-start.8) | collective-permute-done | bytes 2080 | tf_op jit(solution)/shard_map/ppermute | solution.py:338
  35.5 0.9 collective-permute-done.4
  36.4 0.1 fusion.2
  36.5 3.2 %collective-permute-start.5 = (bf16[1056,128]{1,0:T(8,128)(2,1)S(1)}, bf16[1056,128]{1,0:T(8,128)(2,1)S(1)}, u32[]{:S(2)}, u32[]{:S(2)}) collective-permute-start(bf16[1056,128]{1,0:T(8,128)(2,1)S(1)} %fusion.2), channel_id=1, source_target_pairs={{0,32},{16,240},{32,64},{48,16},{64,96},{80,48},{96,128},{112,80},... | collective-permute-start | bytes 811016 | tf_op jit(solution)/shard_map/ppermute | solution.py:359
  39.7 2.9 %collective-permute-start.9 = (f32[8,32]{1,0:T(8,128)S(1)}, f32[8,32]{1,0:T(8,128)S(1)}, u32[]{:S(2)}, u32[]{:S(2)}) collective-permute-start(f32[8,32]{1,0:T(8,128)S(1)} %slice_select_fusion.2), channel_id=1, source_target_pairs={{0,2},{1,3},{2,0},{3,1},{4,6},{5,7},{6,4},{7,5},{8,10},{9,11},{10,... | collective-permute-start | bytes 3080 | tf_op jit(solution)/shard_map/ppermute | solution.py:338
  42.6 1.0 %collective-permute-done.9 = f32[8,32]{1,0:T(8,128)S(1)} collective-permute-done((f32[8,32]{1,0:T(8,128)S(1)}, f32[8,32]{1,0:T(8,128)S(1)}, u32[]{:S(2)}, u32[]{:S(2)}) %collective-permute-start.9) | collective-permute-done | bytes 1056 | tf_op jit(solution)/shard_map/ppermute | solution.py:338
  43.7 4.6 %collective-permute-start.6 = (bf16[1056,128]{1,0:T(8,128)(2,1)S(1)}, bf16[1056,128]{1,0:T(8,128)(2,1)S(1)}, u32[]{:S(2)}, u32[]{:S(2)}) collective-permute-start(bf16[1056,128]{1,0:T(8,128)(2,1)S(1)} %add_convert_fusion.mine_ref), channel_id=1, source_target_pairs={{0,16},{16,0},{32,48},{48,32},{64,80},{80,64},{96,112},{112,96},{1... | collective-permute-start | bytes 811016 | tf_op jit(solution)/shard_map/ppermute | solution.py:356
  48.4 1.3 %collective-permute-start.10 = (f32[4,32]{1,0:T(4,128)S(1)}, f32[4,32]{1,0:T(4,128)S(1)}, u32[]{:S(2)}, u32[]{:S(2)}) collective-permute-start(f32[4,32]{1,0:T(4,128)S(1)} %slice_select_fusion.3), channel_id=1, source_target_pairs={{0,1},{1,0},{2,3},{3,2},{4,5},{5,4},{6,7},{7,6},{8,9},{9,8},{10,11... | collective-permute-start | bytes 1544 | tf_op jit(solution)/shard_map/ppermute | solution.py:338
  49.7 1.1 %collective-permute-done.10 = f32[4,32]{1,0:T(4,128)S(1)} collective-permute-done((f32[4,32]{1,0:T(4,128)S(1)}, f32[4,32]{1,0:T(4,128)S(1)}, u32[]{:S(2)}, u32[]{:S(2)}) %collective-permute-start.10) | collective-permute-done | bytes 544 | tf_op jit(solution)/shard_map/ppermute | solution.py:338
  50.9 3.6 %shard_map.68 = (bf16[1056,128]{1,0:T(8,128)(2,1)S(1)}, f32[4,32]{1,0:T(4,128)S(1)}) custom-call(bf16[1056,128]{1,0:T(8,128)(2,1)S(1)} %add_convert_fusion.mine_ref, bf16[1056,128]{1,0:T(8,128)(2,1)S(1)} %collective-permute-done.6.theirs_ref, f32[4,32]{1,0:T(4,128)S(1)} %select_maximum_fusion.2.peaks_ref), custom_call_target="tpu_custom_call" | custom-call | flops 2415919104 | bytes 811008 | tf_op jit(solution)/shard_map/pallas_call | solution.py:236
  54.4 0.5 collective-permute-start.11
  54.9 5.2 %collective-permute-done.11.refs_0_ = bf16[1056,128]{1,0:T(8,128)(2,1)S(1)} collective-permute-done((bf16[1056,128]{1,0:T(8,128)(2,1)S(1)}, bf16[1056,128]{1,0:T(8,128)(2,1)S(1)}, u32[]{:S(2)}, u32[]{:S(2)}) %collective-permute-start.11) | collective-permute-done | bytes 270368 | tf_op jit(solution)/shard_map/ppermute | solution.py:359
  60.1 1.3 %collective-permute-start.12 = (bf16[1056,128]{1,0:T(8,128)(2,1)S(1)}, bf16[1056,128]{1,0:T(8,128)(2,1)S(1)}, u32[]{:S(2)}, u32[]{:S(2)}) collective-permute-start(bf16[1056,128]{1,0:T(8,128)(2,1)S(1)} %collective-permute-done.11.refs_0_), channel_id=1, source_target_pairs={{0,32},{16,240},{32,64},{48,16},{64,96},{80,48},{96,128},{112,80},... | collective-permute-start | bytes 811016 | tf_op jit(solution)/shard_map/ppermute | solution.py:359
  61.4 2.0 %collective-permute-start.14 = (bf16[1056,128]{1,0:T(8,128)(2,1)S(1)}, bf16[1056,128]{1,0:T(8,128)(2,1)S(1)}, u32[]{:S(2)}, u32[]{:S(2)}) collective-permute-start(bf16[1056,128]{1,0:T(8,128)(2,1)S(1)} %collective-permute-done.11.refs_0_), channel_id=1, source_target_pairs={{0,16},{16,0},{32,48},{48,32},{64,80},{80,64},{96,112},{112,96},{1... | collective-permute-start | bytes 811016 | tf_op jit(solution)/shard_map/ppermute | solution.py:356
  63.4 2.0 %collective-permute-done.12.refs_0_ = bf16[1056,128]{1,0:T(8,128)(2,1)S(1)} collective-permute-done((bf16[1056,128]{1,0:T(8,128)(2,1)S(1)}, bf16[1056,128]{1,0:T(8,128)(2,1)S(1)}, u32[]{:S(2)}, u32[]{:S(2)}) %collective-permute-start.12) | collective-permute-done | bytes 270368 | tf_op jit(solution)/shard_map/ppermute | solution.py:359
  65.4 2.5 %collective-permute-start.15 = (bf16[1056,128]{1,0:T(8,128)(2,1)S(1)}, bf16[1056,128]{1,0:T(8,128)(2,1)S(1)}, u32[]{:S(2)}, u32[]{:S(2)}) collective-permute-start(bf16[1056,128]{1,0:T(8,128)(2,1)S(1)} %collective-permute-done.12.refs_0_), channel_id=1, source_target_pairs={{0,32},{16,240},{32,64},{48,16},{64,96},{80,48},{96,128},{112,80},... | collective-permute-start | bytes 811016 | tf_op jit(solution)/shard_map/ppermute | solution.py:359
  68.0 0.1 copy.21
  68.1 0.1 copy.25
  68.2 0.1 reshape.52.factor_ref
  68.3 1.6 %copy-done.1 = bf16[8,256,512]{2,1,0:T(8,128)(2,1)S(1)} copy-done((bf16[8,256,512]{2,1,0:T(8,128)(2,1)S(1)}, bf16[8,256,512]{2,1,0:T(8,128)(2,1)}, u32[]{:S(2)}) %copy-start.1) | copy-done | bytes 2097176
  69.9 1.8 %shard_map.69 = (bf16[8,256,512]{2,1,0:T(8,128)(2,1)}, bf16[8,256,512]{2,1,0:T(8,128)(2,1)}, s32[2]{0:T(128)}) custom-call(s32[2]{0:T(128)S(1)} %copy-done.2, f32[16]{0:T(128)S(1)} %reshape.52.factor_ref, bf16[8,256,512]{2,1,0:T(8,128)(2,1)S(1)} %copy-done.1, bf16[8,256,512]{2,1,0:T(8,128)(2,1)S(1)} %bitcast.25, bf16[1056,128]{1,0:T(8,128)(2,1)S(1)} %get-tuple-element.31.refs_0_), custom_call_target="tpu_custom_call" | custom-call | flops 134217728 | bytes 1318912 | tf_op jit(solution)/shard_map/pallas_call | solution.py:308
  71.7 2.4 %shard_map.70 = (bf16[8,256,512]{2,1,0:T(8,128)(2,1)}, bf16[8,256,512]{2,1,0:T(8,128)(2,1)}, s32[2]{0:T(128)S(1)}) custom-call(s32[2]{0:T(128)S(1)} %copy-done.2, f32[16]{0:T(128)S(1)} %reshape.52.factor_ref, bf16[8,256,512]{2,1,0:T(8,128)(2,1)S(1)} %copy-done.1, bf16[8,256,512]{2,1,0:T(8,128)(2,1)S(1)} %bitcast.26, ...), custom_call_target="tpu_custom_call", output_to_operand_aliasing={{0}: (6, {}), {1}: (7, {})} | custom-call | flops 268435456 | bytes 2637824 | tf_op jit(solution)/shard_map/pallas_call | solution.py:308
  74.1 0.6 slice.39
  75.4 3.2 %collective-permute-start.13 = (bf16[1056,128]{1,0:T(8,128)(2,1)S(1)}, bf16[1056,128]{1,0:T(8,128)(2,1)S(1)}, u32[]{:S(2)}, u32[]{:S(2)}) collective-permute-start(bf16[1056,128]{1,0:T(8,128)(2,1)S(1)} %collective-permute-done.12.refs_0_), channel_id=1, source_target_pairs={{0,16},{16,0},{32,48},{48,32},{64,80},{80,64},{96,112},{112,96},{1... | collective-permute-start | bytes 811016 | tf_op jit(solution)/shard_map/ppermute | solution.py:356
  78.6 3.0 %collective-permute-start.16 = (bf16[528,128]{1,0:T(8,128)(2,1)S(1)}, bf16[528,128]{1,0:T(8,128)(2,1)S(1)}, u32[]{:S(2)}, u32[]{:S(2)}) collective-permute-start(bf16[528,128]{1,0:T(8,128)(2,1)S(1)} %slice_select_fusion), channel_id=1, source_target_pairs={{0,32},{16,240},{32,64},{48,16},{64,96},{80,48},{96,128},{112,80},... | collective-permute-start | bytes 405512 | tf_op jit(solution)/shard_map/ppermute | solution.py:359
  81.6 2.4 %shard_map.71 = (bf16[8,256,512]{2,1,0:T(8,128)(2,1)}, bf16[8,256,512]{2,1,0:T(8,128)(2,1)}, s32[2]{0:T(128)S(1)}) custom-call(s32[2]{0:T(128)S(1)} %copy-done.2, f32[16]{0:T(128)S(1)} %reshape.52.factor_ref, bf16[8,256,512]{2,1,0:T(8,128)(2,1)S(1)} %copy-done.1, bf16[8,256,512]{2,1,0:T(8,128)(2,1)S(1)} %bitcast.27, ...), custom_call_target="tpu_custom_call", output_to_operand_aliasing={{0}: (6, {}), {1}: (7, {})} | custom-call | flops 268435456 | bytes 2637824 | tf_op jit(solution)/shard_map/pallas_call | solution.py:308
  84.0 0.6 slice.38
  85.3 0.1 collective-permute-start.17
  85.4 0.5 collective-permute-start.18
  85.9 0.8 collective-permute-done.17
  86.8 0.3 collective-permute-done.18.refs_1_
  87.1 2.4 %shard_map.72 = (bf16[8,256,512]{2,1,0:T(8,128)(2,1)}, bf16[8,256,512]{2,1,0:T(8,128)(2,1)}, s32[2]{0:T(128)}) custom-call(s32[2]{0:T(128)S(1)} %copy-done.2, f32[16]{0:T(128)S(1)} %reshape.52.factor_ref, bf16[8,256,512]{2,1,0:T(8,128)(2,1)S(1)} %copy-done.1, bf16[8,256,512]{2,1,0:T(8,128)(2,1)S(1)} %bitcast.28, ...), custom_call_target="tpu_custom_call", output_to_operand_aliasing={{0}: (6, {}), {1}: (7, {})} | custom-call | flops 268435456 | bytes 2637824 | tf_op jit(solution)/shard_map/pallas_call | solution.py:308
  89.6 1.8 %shard_map.73 = (bf16[8,256,512]{2,1,0:T(8,128)(2,1)}, bf16[8,256,512]{2,1,0:T(8,128)(2,1)}, s32[2]{0:T(128)}) custom-call(s32[2]{0:T(128)S(1)} %copy-done.2, f32[16]{0:T(128)S(1)} %reshape.52.factor_ref, bf16[8,256,512]{2,1,0:T(8,128)(2,1)S(1)} %copy-done.1, bf16[8,256,512]{2,1,0:T(8,128)(2,1)S(1)} %bitcast.29, ...), custom_call_target="tpu_custom_call", output_to_operand_aliasing={{0}: (5, {}), {1}: (6, {})} | custom-call | flops 134217728 | bytes 1318912 | tf_op jit(solution)/shard_map/pallas_call | solution.py:308
  (38 shorter events, 0.6 us)
Async XLA Ops:
  1.3 18.7 %copy-start.5 = (f32[1,64,32]{1,2,0:T(8,128)S(1)}, f32[1,64,32]{1,2,0:T(8,128)}, u32[]{:S(2)}) copy-start(f32[1,64,32]{1,2,0:T(8,128)} %param.7) | copy-start | bytes 24580
  10.6 19.8 %copy-start.3 = (bf16[3,1056,128]{2,1,0:T(8,128)(2,1)S(1)}, bf16[3,1056,128]{2,1,0:T(8,128)(2,1)}, u32[]{:S(2)}) copy-start(bf16[3,1056,128]{2,1,0:T(8,128)(2,1)} %get-tuple-element.25) | copy-start | bytes 2433028
  10.6 4.5 %collective-permute-start.1 = (bf16[528,128]{1,0:T(8,128)(2,1)}, bf16[528,128]{1,0:T(8,128)(2,1)S(1)}, u32[]{:S(2)}, u32[]{:S(2)}) collective-permute-start(bf16[528,128]{1,0:T(8,128)(2,1)} %get-tuple-element.28), channel_id=1, source_target_pairs={{0,16},{16,0},{32,48},{48,32},{64,80},{80,64},{96,112},{112,96},{1... | collective-permute-start | bytes 405512 | tf_op jit(solution)/shard_map/ppermute | solution.py:356
  13.9 8.1 %collective-permute-start = (bf16[3,1056,128]{2,1,0:T(8,128)(2,1)}, bf16[3,1056,128]{2,1,0:T(8,128)(2,1)S(1)}, u32[]{:S(2)}, u32[]{:S(2)}) collective-permute-start(bf16[3,1056,128]{2,1,0:T(8,128)(2,1)} %get-tuple-element.26), channel_id=1, source_target_pairs={{0,16},{16,0},{32,48},{48,32},{64,80},{80,64},{96,112},{112,96},{1... | collective-permute-start | bytes 2433032 | tf_op jit(solution)/shard_map/ppermute | solution.py:356
  16.0 5.9 %collective-permute-start.2 = (bf16[528,128]{1,0:T(8,128)(2,1)S(1)}, bf16[528,128]{1,0:T(8,128)(2,1)S(1)}, u32[]{:S(2)}, u32[]{:S(2)}) collective-permute-start(bf16[528,128]{1,0:T(8,128)(2,1)S(1)} %add_convert_fusion.1), channel_id=1, source_target_pairs={{0,32},{16,240},{32,64},{48,16},{64,96},{80,48},{96,128},{112,80},... | collective-permute-start | bytes 405512 | tf_op jit(solution)/shard_map/ppermute | solution.py:359
  20.2 23.5 %copy-start.4 = (bf16[1056,128]{1,0:T(8,128)(2,1)S(1)}, bf16[1056,128]{1,0:T(8,128)(2,1)}, u32[]{:S(2)}) copy-start(bf16[1056,128]{1,0:T(8,128)(2,1)} %get-tuple-element.24) | copy-start | bytes 811012
  23.0 7.3 %collective-permute-start.3 = (bf16[1056,128]{1,0:T(8,128)(2,1)S(1)}, bf16[1056,128]{1,0:T(8,128)(2,1)S(1)}, u32[]{:S(2)}, u32[]{:S(2)}) collective-permute-start(bf16[1056,128]{1,0:T(8,128)(2,1)S(1)} %fusion), channel_id=1, source_target_pairs={{0,32},{16,240},{32,64},{48,16},{64,96},{80,48},{96,128},{112,80},... | collective-permute-start | bytes 811016 | tf_op jit(solution)/shard_map/ppermute | solution.py:359
  26.2 4.1 %collective-permute-start.7 = (f32[32,32]{1,0:T(8,128)S(1)}, f32[32,32]{1,0:T(8,128)S(1)}, u32[]{:S(2)}, u32[]{:S(2)}) collective-permute-start(f32[32,32]{1,0:T(8,128)S(1)} %select_bitcast_fusion), channel_id=1, source_target_pairs={{0,8},{1,9},{2,10},{3,11},{4,12},{5,13},{6,14},{7,15},{8,0},{9,1},... | collective-permute-start | bytes 12296 | tf_op jit(solution)/shard_map/ppermute | solution.py:338
  30.5 5.9 %collective-permute-start.4 = (bf16[1056,128]{1,0:T(8,128)(2,1)S(1)}, bf16[1056,128]{1,0:T(8,128)(2,1)S(1)}, u32[]{:S(2)}, u32[]{:S(2)}) collective-permute-start(bf16[1056,128]{1,0:T(8,128)(2,1)S(1)} %fusion.1), channel_id=1, source_target_pairs={{0,32},{16,240},{32,64},{48,16},{64,96},{80,48},{96,128},{112,80},... | collective-permute-start | bytes 811016 | tf_op jit(solution)/shard_map/ppermute | solution.py:359
  33.0 2.5 %collective-permute-start.8 = (f32[16,32]{1,0:T(8,128)S(1)}, f32[16,32]{1,0:T(8,128)S(1)}, u32[]{:S(2)}, u32[]{:S(2)}) collective-permute-start(f32[16,32]{1,0:T(8,128)S(1)} %slice_select_fusion.1), channel_id=1, source_target_pairs={{0,4},{1,5},{2,6},{3,7},{4,0},{5,1},{6,2},{7,3},{8,12},{9,13},{10,... | collective-permute-start | bytes 6152 | tf_op jit(solution)/shard_map/ppermute | solution.py:338
  36.5 7.2 %collective-permute-start.5 = (bf16[1056,128]{1,0:T(8,128)(2,1)S(1)}, bf16[1056,128]{1,0:T(8,128)(2,1)S(1)}, u32[]{:S(2)}, u32[]{:S(2)}) collective-permute-start(bf16[1056,128]{1,0:T(8,128)(2,1)S(1)} %fusion.2), channel_id=1, source_target_pairs={{0,32},{16,240},{32,64},{48,16},{64,96},{80,48},{96,128},{112,80},... | collective-permute-start | bytes 811016 | tf_op jit(solution)/shard_map/ppermute | solution.py:359
  39.7 4.0 %collective-permute-start.9 = (f32[8,32]{1,0:T(8,128)S(1)}, f32[8,32]{1,0:T(8,128)S(1)}, u32[]{:S(2)}, u32[]{:S(2)}) collective-permute-start(f32[8,32]{1,0:T(8,128)S(1)} %slice_select_fusion.2), channel_id=1, source_target_pairs={{0,2},{1,3},{2,0},{3,1},{4,6},{5,7},{6,4},{7,5},{8,10},{9,11},{10,... | collective-permute-start | bytes 3080 | tf_op jit(solution)/shard_map/ppermute | solution.py:338
  43.7 7.1 %collective-permute-start.6 = (bf16[1056,128]{1,0:T(8,128)(2,1)S(1)}, bf16[1056,128]{1,0:T(8,128)(2,1)S(1)}, u32[]{:S(2)}, u32[]{:S(2)}) collective-permute-start(bf16[1056,128]{1,0:T(8,128)(2,1)S(1)} %add_convert_fusion.mine_ref), channel_id=1, source_target_pairs={{0,16},{16,0},{32,48},{48,32},{64,80},{80,64},{96,112},{112,96},{1... | collective-permute-start | bytes 811016 | tf_op jit(solution)/shard_map/ppermute | solution.py:356
  48.4 2.5 %collective-permute-start.10 = (f32[4,32]{1,0:T(4,128)S(1)}, f32[4,32]{1,0:T(4,128)S(1)}, u32[]{:S(2)}, u32[]{:S(2)}) collective-permute-start(f32[4,32]{1,0:T(4,128)S(1)} %slice_select_fusion.3), channel_id=1, source_target_pairs={{0,1},{1,0},{2,3},{3,2},{4,5},{5,4},{6,7},{7,6},{8,9},{9,8},{10,11... | collective-permute-start | bytes 1544 | tf_op jit(solution)/shard_map/ppermute | solution.py:338
  50.8 17.5 %copy-start = (bf16[4,2,256,512]{3,2,1,0:T(8,128)(2,1)S(1)}, bf16[4,2,256,512]{3,2,1,0:T(8,128)(2,1)}, u32[]{:S(2)}) copy-start(bf16[4,2,256,512]{3,2,1,0:T(8,128)(2,1)} %param.6) | copy-start | bytes 6291460
  50.8 17.5 %copy-start.2 = (s32[2]{0:T(128)S(1)}, s32[2]{0:T(128)}, u32[]{:S(2)}) copy-start(s32[2]{0:T(128)} %pad_add_fusion.place_ref) | copy-start | bytes 28
  54.4 5.7 %collective-permute-start.11 = (bf16[1056,128]{1,0:T(8,128)(2,1)S(1)}, bf16[1056,128]{1,0:T(8,128)(2,1)S(1)}, u32[]{:S(2)}, u32[]{:S(2)}) collective-permute-start(bf16[1056,128]{1,0:T(8,128)(2,1)S(1)} %get-tuple-element.31.refs_0_), channel_id=1, source_target_pairs={{0,32},{16,240},{32,64},{48,16},{64,96},{80,48},{96,128},{112,80},... | collective-permute-start | bytes 811016 | tf_op jit(solution)/shard_map/ppermute | solution.py:359
  60.1 5.3 %collective-permute-start.12 = (bf16[1056,128]{1,0:T(8,128)(2,1)S(1)}, bf16[1056,128]{1,0:T(8,128)(2,1)S(1)}, u32[]{:S(2)}, u32[]{:S(2)}) collective-permute-start(bf16[1056,128]{1,0:T(8,128)(2,1)S(1)} %collective-permute-done.11.refs_0_), channel_id=1, source_target_pairs={{0,32},{16,240},{32,64},{48,16},{64,96},{80,48},{96,128},{112,80},... | collective-permute-start | bytes 811016 | tf_op jit(solution)/shard_map/ppermute | solution.py:359
  61.4 10.3 %collective-permute-start.14 = (bf16[1056,128]{1,0:T(8,128)(2,1)S(1)}, bf16[1056,128]{1,0:T(8,128)(2,1)S(1)}, u32[]{:S(2)}, u32[]{:S(2)}) collective-permute-start(bf16[1056,128]{1,0:T(8,128)(2,1)S(1)} %collective-permute-done.11.refs_0_), channel_id=1, source_target_pairs={{0,16},{16,0},{32,48},{48,32},{64,80},{80,64},{96,112},{112,96},{1... | collective-permute-start | bytes 811016 | tf_op jit(solution)/shard_map/ppermute | solution.py:356
  65.4 13.1 %collective-permute-start.15 = (bf16[1056,128]{1,0:T(8,128)(2,1)S(1)}, bf16[1056,128]{1,0:T(8,128)(2,1)S(1)}, u32[]{:S(2)}, u32[]{:S(2)}) collective-permute-start(bf16[1056,128]{1,0:T(8,128)(2,1)S(1)} %collective-permute-done.12.refs_0_), channel_id=1, source_target_pairs={{0,32},{16,240},{32,64},{48,16},{64,96},{80,48},{96,128},{112,80},... | collective-permute-start | bytes 811016 | tf_op jit(solution)/shard_map/ppermute | solution.py:359
  68.3 1.6 %copy-start.1 = (bf16[8,256,512]{2,1,0:T(8,128)(2,1)S(1)}, bf16[8,256,512]{2,1,0:T(8,128)(2,1)}, u32[]{:S(2)}) copy-start(bf16[8,256,512]{2,1,0:T(8,128)(2,1)} %get-tuple-element.30.advance_ref) | copy-start | bytes 6291460
  75.4 6.3 %collective-permute-start.13 = (bf16[1056,128]{1,0:T(8,128)(2,1)S(1)}, bf16[1056,128]{1,0:T(8,128)(2,1)S(1)}, u32[]{:S(2)}, u32[]{:S(2)}) collective-permute-start(bf16[1056,128]{1,0:T(8,128)(2,1)S(1)} %collective-permute-done.12.refs_0_), channel_id=1, source_target_pairs={{0,16},{16,0},{32,48},{48,32},{64,80},{80,64},{96,112},{112,96},{1... | collective-permute-start | bytes 811016 | tf_op jit(solution)/shard_map/ppermute | solution.py:356
  78.6 6.7 %collective-permute-start.16 = (bf16[528,128]{1,0:T(8,128)(2,1)S(1)}, bf16[528,128]{1,0:T(8,128)(2,1)S(1)}, u32[]{:S(2)}, u32[]{:S(2)}) collective-permute-start(bf16[528,128]{1,0:T(8,128)(2,1)S(1)} %slice_select_fusion), channel_id=1, source_target_pairs={{0,32},{16,240},{32,64},{48,16},{64,96},{80,48},{96,128},{112,80},... | collective-permute-start | bytes 405512 | tf_op jit(solution)/shard_map/ppermute | solution.py:359
  85.3 1.4 %collective-permute-start.17 = (bf16[528,128]{1,0:T(8,128)(2,1)S(1)}, bf16[528,128]{1,0:T(8,128)(2,1)S(1)}, u32[]{:S(2)}, u32[]{:S(2)}) collective-permute-start(bf16[528,128]{1,0:T(8,128)(2,1)S(1)} %broadcast_select_fusion), channel_id=1, source_target_pairs={{0,16},{16,0},{32,48},{48,32},{64,80},{80,64},{96,112},{112,96},{1... | collective-permute-start | bytes 405512 | tf_op jit(solution)/shard_map/ppermute | solution.py:356
  85.4 1.7 %collective-permute-start.18 = (bf16[1056,128]{1,0:T(8,128)(2,1)S(1)}, bf16[1056,128]{1,0:T(8,128)(2,1)S(1)}, u32[]{:S(2)}, u32[]{:S(2)}) collective-permute-start(bf16[1056,128]{1,0:T(8,128)(2,1)S(1)} %collective-permute-done.15.refs_0_), channel_id=1, source_target_pairs={{0,16},{16,0},{32,48},{48,32},{64,80},{80,64},{96,112},{112,96},{1... | collective-permute-start | bytes 811016 | tf_op jit(solution)/shard_map/ppermute | solution.py:356

commit v2 on v1

v2 whole, which is shorter than its diff:
```python
import math

import jax
import jax.numpy as jnp
from jax import lax
from jax.experimental import pallas as pl
from jax.experimental.pallas import tpu as pltpu
from jax.sharding import PartitionSpec as P

DK = 128
SIDE = 128
SQUARES = 8 * SIDE
GRAM_ROWS = SQUARES + 64
GRAM_HALF = GRAM_ROWS // 2
PACKED = SQUARES + 32
HALF = PACKED // 2
MEBI = 1024 * 1024

FIRST_COEFF = 3.4445
SECOND_COEFF = -4.775
THIRD_COEFF = 2.0315
MOMENTUM = 0.95
LEARN_RATE = 0.1
SHRINK = 0.99
CLIP_LIMIT = 100.0
EPSILON = 1e-07


def low(value):
    return value.astype(jnp.bfloat16)


def wide(value):
    return value.astype(jnp.float32)


def product(left, right):
    return jnp.dot(low(left), low(right), preferred_element_type=jnp.float32)


def square_iota(dimension):
    return lax.broadcasted_iota(jnp.int32, (SIDE, SIDE), dimension)


def diagonal_row(block):
    return jnp.sum(jnp.where(square_iota(0) == square_iota(1), block, 0.0), axis=0, keepdims=True)


ORDER = ((0, 1), (0, 2), (0, 3)), ((1, 2), (1, 3), (2, 3))


def pack(blocks, rows, residuals=False):
    upper = square_iota(0) <= square_iota(1)
    pieces = []
    for which in range(2):
        even, odd = blocks[2 * which, 2 * which], blocks[2 * which + 1, 2 * which + 1]
        pieces.append(jnp.where(upper, even, odd))
        pieces += [blocks[name] for name in ORDER[which]]
    row = lax.broadcasted_iota(jnp.int32, (rows - SQUARES, SIDE), 0)
    extra = jnp.zeros(row.shape, jnp.float32)
    for i in range(4):
        values = diagonal_row(blocks[i, i])
        extra = jnp.where(row == i, values, extra)
        if residuals:
            extra = jnp.where(row == 4 + i, values - wide(low(values)), extra)
    return jnp.concatenate([low(piece) for piece in pieces + [extra]], axis=0)


def unpack_blocks(packed, dtype):
    rows, columns = square_iota(0), square_iota(1)
    extra = wide(packed[SQUARES:])
    blocks = {}
    for which in range(2):
        pieces = [packed[(4 * which + k) * SIDE : (4 * which + k + 1) * SIDE] for k in range(4)]
        both = wide(pieces[0])
        turned = both.T
        first, second = extra[2 * which : 2 * which + 1], extra[2 * which + 1 : 2 * which + 2]
        even = jnp.where(rows < columns, both, jnp.where(rows > columns, turned, first))
        odd = jnp.where(rows > columns, both, jnp.where(rows < columns, turned, second))
        blocks[2 * which, 2 * which] = even.astype(dtype)
        blocks[2 * which + 1, 2 * which + 1] = odd.astype(dtype)
        for name, piece in zip(ORDER[which], pieces[1:]):
            blocks[name] = piece.astype(dtype)
    return blocks, extra


def corner(blocks, i):
    right = blocks[i, i + 1]
    return jnp.concatenate(
        [
            jnp.concatenate([blocks[i, i], right], axis=1),
            jnp.concatenate([wide(right).T.astype(right.dtype), blocks[i + 1, i + 1]], axis=1),
        ],
        axis=0,
    )


def off_corner(blocks):
    return jnp.concatenate(
        [jnp.concatenate([blocks[i, 2], blocks[i, 3]], axis=1) for i in (0, 1)], axis=0
    )


def cut_blocks(matrix):
    return {
        (i, j): matrix[i * SIDE : (i + 1) * SIDE, j * SIDE : (j + 1) * SIDE]
        for i in range(4)
        for j in range(i, 4)
    }


def carried(step):
    return 4 - (step + 1) // 2, (step % 2) == 1


def gram_kernel(
    grad_hbm, moment_hbm,
    new_moment_hbm, advance_hbm, mine_hbm, theirs_hbm, far_mine_hbm, far_theirs_hbm, own_hbm,
    grad_ref, moment_ref, new_moment_ref, advance_ref, packed_ref, in_sems, out_sems,
):
    matrices, rows, width = grad_ref.shape
    dp = lax.axis_index("dp")
    chip, core = dp // 2, dp % 2
    middle = width // 2
    contract = (((0,), (0,)), ((), ()))

    def place_of(step):
        distance, mine = carried(step)
        up = core == (0 if mine else 1)
        return lax.rem(chip + jnp.where(up, distance, matrices - distance), matrices)

    def incoming(step, which):
        source, target = ((grad_hbm, grad_ref), (moment_hbm, moment_ref))[which]
        return pltpu.make_async_copy(
            source.at[place_of(step)], target.at[step], in_sems.at[which, step]
        )

    def outgoing(step, which):
        source, target = ((new_moment_ref, new_moment_hbm), (advance_ref, advance_hbm))[which]
        return pltpu.make_async_copy(
            source.at[step], target.at[place_of(step)], out_sems.at[which, step]
        )

    def packed_copy(source, target, sem):
        return pltpu.make_async_copy(source, target, sem)

    for step in range(matrices):
        incoming(step, 0).start()
        incoming(step, 1).start()
    copies = []
    for step in range(matrices):
        incoming(step, 0).wait()
        incoming(step, 1).wait()
        widened = wide(grad_ref[step])
        moment_sum = MOMENTUM * wide(moment_ref[step]) + widened
        new_moment_ref[step] = low(moment_sum)
        advance = low(widened + MOMENTUM * moment_sum)
        advance_ref[step] = advance
        for which in range(2):
            copies.append(outgoing(step, which))
            copies[-1].start()
        upper = lax.dot_general(
            advance[:, :middle], advance, contract, preferred_element_type=jnp.float32
        )
        lower = lax.dot_general(
            advance[:, middle:], advance[:, middle:], contract, preferred_element_type=jnp.float32
        )
        blocks = {}
        for i in range(2):
            for j in range(i, 4):
                blocks[i, j] = upper[i * SIDE : (i + 1) * SIDE, j * SIDE : (j + 1) * SIDE]
            for j in range(i, 2):
                blocks[i + 2, j + 2] = lower[i * SIDE : (i + 1) * SIDE, j * SIDE : (j + 1) * SIDE]
        packed = pack(blocks, GRAM_ROWS)
        mine = step in (0, matrices - 1) or carried(step)[1]
        natural = core == (0 if mine else 1)
        packed_ref[step, :GRAM_HALF] = jnp.where(natural, packed[:GRAM_HALF], packed[GRAM_HALF:])
        packed_ref[step, GRAM_HALF:] = jnp.where(natural, packed[GRAM_HALF:], packed[:GRAM_HALF])
        if step == 0:
            first, second = packed_ref.at[0, :GRAM_HALF], packed_ref.at[0, GRAM_HALF:]
            copies.append(packed_copy(first, far_mine_hbm, out_sems.at[2, 0]))
            copies[-1].start()
            copies.append(packed_copy(second, far_theirs_hbm, out_sems.at[3, 0]))
            copies[-1].start()
            continue
        if step == matrices - 1:
            target = own_hbm
        elif mine:
            target = mine_hbm.at[(step - 1) // 2]
        else:
            target = theirs_hbm.at[(step - 1) // 2]
        copies.append(packed_copy(packed_ref.at[step], target, out_sems.at[2, step]))
        copies[-1].start()
    for copy in copies:
        copy.wait()


def grams(gradients, moments):
    matrices, rows, width = gradients.shape
    there = pl.BlockSpec(memory_space=pltpu.HBM)
    anywhere = pl.BlockSpec(memory_space=pl.ANY)

    def shape(*sizes):
        return jax.ShapeDtypeStruct(sizes, jnp.bfloat16)

    full = shape(*gradients.shape)
    return pl.pallas_call(
        gram_kernel,
        out_shape=(
            full, full, shape(3, GRAM_ROWS, SIDE), shape(3, GRAM_ROWS, SIDE),
            shape(GRAM_HALF, SIDE), shape(GRAM_HALF, SIDE), shape(GRAM_ROWS, SIDE),
        ),
        in_specs=[there, there],
        out_specs=(there, there) + (anywhere,) * 5,
        scratch_shapes=[pltpu.VMEM(gradients.shape, jnp.bfloat16)] * 4
        + [
            pltpu.VMEM((matrices, GRAM_ROWS, SIDE), jnp.bfloat16),
            pltpu.SemaphoreType.DMA((2, matrices)),
            pltpu.SemaphoreType.DMA((4, matrices)),
        ],
        compiler_params=pltpu.CompilerParams(vmem_limit_bytes=50 * MEBI),
        cost_estimate=pl.CostEstimate(
            flops=2 * gradients.size * width, bytes_accessed=10 * gradients.size, transcendentals=0
        ),
    )(gradients, moments)


def polynomial_kernel(place_ref, mine_ref, theirs_ref, first_ref, second_ref, ratio_ref):
    natural = place_ref[1] == 0
    mine, theirs = wide(mine_ref[...]), wide(theirs_ref[...])
    first = mine[:GRAM_HALF] + theirs[GRAM_HALF:]
    second = mine[GRAM_HALF:] + theirs[:GRAM_HALF]
    packed = jnp.concatenate(
        [jnp.where(natural, first, second), jnp.where(natural, second, first)], axis=0
    )
    blocks, extra = unpack_blocks(packed, jnp.float32)
    logits = extra[16:32] + extra[32:48] + extra[48:64]
    peaks = jnp.max(logits, axis=0, keepdims=True)
    ratio_ref[...] = jnp.sqrt(jnp.minimum(1.0, CLIP_LIMIT / peaks))
    corners = off_corner(blocks)
    gram = jnp.concatenate(
        [
            jnp.concatenate([corner(blocks, 0), corners], axis=1),
            jnp.concatenate([corners.T, corner(blocks, 2)], axis=1),
        ],
        axis=0,
    )
    width = gram.shape[0]
    rows = lax.broadcasted_iota(jnp.int32, (width, width), 0)
    columns = lax.broadcasted_iota(jnp.int32, (width, width), 1)
    diagonal = rows == columns
    norm = jnp.sqrt(jnp.sum(jnp.where(diagonal, gram, 0.0)))
    scale = 1.0 / (norm + EPSILON)
    gram = gram * scale * scale

    def poly(gram):
        return SECOND_COEFF * gram + THIRD_COEFF * product(gram, gram)

    def following(gram, step):
        inner = FIRST_COEFF * gram + product(gram, step)
        return FIRST_COEFF * inner + product(inner, step)

    rest = poly(gram)
    factor = FIRST_COEFF
    gram = following(gram, rest)
    for last in (False, True):
        step = poly(gram)
        if not last:
            gram = following(gram, step)
        rest = FIRST_COEFF * rest + factor * step + product(rest, step)
        factor = factor * FIRST_COEFF
    total = jnp.where(diagonal, rest + factor, rest) * scale
    packed = pack(cut_blocks(total), PACKED, residuals=True)
    first_ref[...] = jnp.where(natural, packed[:HALF], packed[HALF:])
    second_ref[...] = jnp.where(natural, packed[HALF:], packed[:HALF])


def polynomial(place, mine, theirs):
    width = 4 * SIDE
    whole = pl.BlockSpec(memory_space=pltpu.VMEM)
    return pl.pallas_call(
        polynomial_kernel,
        out_shape=(
            jax.ShapeDtypeStruct((HALF, SIDE), jnp.bfloat16),
            jax.ShapeDtypeStruct((HALF, SIDE), jnp.bfloat16),
            jax.ShapeDtypeStruct((1, SIDE), jnp.float32),
        ),
        in_specs=[pl.BlockSpec(memory_space=pltpu.SMEM), whole, whole],
        out_specs=(whole, whole, whole),
        compiler_params=pltpu.CompilerParams(vmem_limit_bytes=40 * MEBI),
        cost_estimate=pl.CostEstimate(
            flops=9 * 2 * width**3, bytes_accessed=6 * PACKED * SIDE, transcendentals=0
        ),
    )(place, mine, theirs)


def finish(place, ratios, advance, weights, parts, results):
    matrices, rows, width = advance.shape
    pieces = [half for halves, _, _ in parts for half in halves]
    where = [sum(len(halves) for halves, _, _ in parts[:k]) for k in range(len(parts) + 1)]
    count = len(parts)
    middle = width // 2
    scaling = 0.2 * math.sqrt(max(rows * matrices * 2, width))

    def index(step, place):
        chosen = 0
        for k, (_, distance, along) in enumerate(parts):
            below = place[1] == (0 if along else 1)
            signed = jnp.where(below, matrices - distance, distance)
            chosen = jnp.where(step == k, signed, chosen)
        return lax.rem(place[0] + chosen, matrices)

    def kernel(place_ref, ratio_ref, advance_ref, weight_ref, *refs):
        new_weight_ref, update_ref, after_ref = refs[-4:-1]
        after_ref[...] = jnp.zeros_like(after_ref)
        matrix_ref = refs[-1]
        step = pl.program_id(0)
        for k in range(count):

            @pl.when(step == k)
            def _():
                halves = jnp.concatenate([ref[...] for ref in refs[where[k] : where[k + 1]]], axis=0)
                first, second = halves[:HALF], halves[HALF:]
                natural = place_ref[1] == (0 if parts[k][2] else 1)
                packed = jnp.concatenate(
                    [jnp.where(natural, first, second), jnp.where(natural, second, first)], axis=0
                )
                blocks, extra = unpack_blocks(packed, jnp.bfloat16)
                matrix_ref[:middle, :middle] = corner(blocks, 0)
                matrix_ref[:middle, middle:] = off_corner(blocks)
                matrix_ref[middle:width, middle:] = corner(blocks, 2)
                for i in range(4):
                    matrix_ref[width:, i * SIDE : (i + 1) * SIDE] = low(
                        jnp.broadcast_to(extra[4 + i : 5 + i], (16, SIDE))
                    )

        which = index(step, place_ref)
        lane = lax.broadcasted_iota(jnp.int32, (1, SIDE), 1)
        head = (which // 2) * (SIDE * 2 // matrices) + (place_ref[0] * 2 + place_ref[1]) * 2
        row = lax.broadcasted_iota(jnp.int32, (rows, 1), 0)
        factor = jnp.zeros((rows, 1), jnp.float32)
        for k in range(rows // DK):
            ratio = jnp.sum(
                jnp.where(lane == head + k, ratio_ref[...], 0.0), axis=1, keepdims=True
            )
            factor = jnp.where(row // DK == k, ratio, factor)
        factor = jnp.where(which % 2 == 0, factor, 1.0)
        off = matrix_ref[:middle, middle:]
        left, right = advance_ref[0, :, :middle], advance_ref[0, :, middle:]
        halves = (
            jnp.dot(left, matrix_ref[:middle, :middle], preferred_element_type=jnp.float32)
            + lax.dot_general(
                right, off, (((1,), (1,)), ((), ())), preferred_element_type=jnp.float32
            ),
            jnp.dot(left, off, preferred_element_type=jnp.float32)
            + jnp.dot(right, matrix_ref[middle:width, middle:], preferred_element_type=jnp.float32),
        )
        for k, values in enumerate((left, right)):
            columns = slice(k * middle, (k + 1) * middle)
            rest = wide(matrix_ref[width : width + 1, columns])
            scaled = scaling * (halves[k] + wide(values) * rest)
            update_ref[0, :, columns] = low(scaled)
            new_weight = (wide(weight_ref[0, :, columns]) * SHRINK - LEARN_RATE * scaled) * factor
            new_weight_ref[0, :, columns] = low(new_weight)

    full = pl.BlockSpec((1, rows, width), lambda step, place: (index(step, place), 0, 0))
    one_row = pl.BlockSpec((1, SIDE), lambda step, place: (0, 0))
    anywhere = pl.BlockSpec(memory_space=pl.ANY)
    shape = jax.ShapeDtypeStruct(advance.shape, jnp.bfloat16)
    carry = [] if results is None else list(results)
    first_carried = 4 + len(pieces)
    return pl.pallas_call(
        kernel,
        out_shape=(shape, shape, jax.ShapeDtypeStruct((1, SIDE), jnp.bfloat16)),
        grid_spec=pltpu.PrefetchScalarGridSpec(
            num_scalar_prefetch=1,
            grid=(count,),
            in_specs=[one_row, full, full]
            + [pl.BlockSpec(half.shape, lambda step, place: (0, 0)) for half in pieces]
             + [anywhere] * len(carry),
            out_specs=(full, full, one_row),
            scratch_shapes=[pltpu.VMEM((width + 16, width), jnp.bfloat16)],
        ),
        input_output_aliases={first_carried + k: k for k in range(len(carry))},
        compiler_params=pltpu.CompilerParams(vmem_limit_bytes=48 * MEBI),
        cost_estimate=pl.CostEstimate(
            flops=2 * count * rows * width * width,
            bytes_accessed=count * (8 * rows * width + 2 * PACKED * SIDE),
            transcendentals=0,
        ),
    )(place, ratios, advance, weights, *pieces, *carry)


def observed_rows(head_logits, layers):
    parties, observers = lax.axis_size("dp"), lax.axis_size("mp")
    dp = lax.axis_index("dp")
    start = jnp.bitwise_xor(lax.axis_index("mp"), dp) * layers
    pairs = [
        (k * observers + i, k * observers + (i ^ k)) for k in range(parties) for i in range(observers)
    ]
    sent = lax.dynamic_slice_in_dim(head_logits[0], start, layers, 0)
    values = lax.ppermute(sent, ("dp", "mp"), pairs).reshape(1, -1)
    high = lax.reduce_precision(values, 8, 7)
    middle = lax.reduce_precision(values - high, 8, 7)
    rest = values - high - middle
    row = lax.broadcasted_iota(jnp.int32, (GRAM_ROWS - SQUARES, 1), 0)
    kind, slot = row // parties, row % parties
    chosen = jnp.where(kind == 1, high, jnp.where(kind == 2, middle, rest))
    return low(jnp.where(jnp.logical_and(kind > 0, slot == dp), chosen, 0.0))


def shards(gradients, moments, weights, head_logits):
    layers, kind_count, row_count, latent_width = gradients.shape
    matrices = layers * kind_count
    parties = lax.axis_size("dp")
    dp = lax.axis_index("dp")
    core = dp % 2
    place = jnp.stack([dp // 2, core]).astype(jnp.int32)
    stacked = (matrices, row_count, latent_width)

    swap_pairs = [(i, i ^ 1) for i in range(parties)]

    def swap(value):
        return lax.ppermute(value, "dp", swap_pairs)

    def onward(value, distance):
        pairs = [(i, (i + 2 * distance * (1 - 2 * (i % 2))) % parties) for i in range(parties)]
        return lax.ppermute(value, "dp", pairs)

    new_moments, advance, mine, theirs, far_mine, far_theirs, own = grams(
        gradients.reshape(stacked), moments.reshape(stacked)
    )
    rows = observed_rows(head_logits, layers)
    both_rows = wide(rows) + wide(swap(rows))
    far_arrived, arrived = swap(far_theirs), swap(theirs)

    def behind(value, start):
        return jnp.pad(value, ((start, 0), (0, 0)))

    rows_first = behind(jnp.where(core == 0, 0.0, both_rows), SQUARES - GRAM_HALF)
    rows_second = behind(jnp.where(core == 0, both_rows, 0.0), SQUARES - GRAM_HALF)

    def first_half(distance):
        slot = 3 - distance
        return wide(mine[slot, :GRAM_HALF]) + wide(arrived[slot, :GRAM_HALF]) + rows_first

    def second_half(distance):
        slot = 3 - distance
        return wide(mine[slot, GRAM_HALF:]) + wide(arrived[slot, GRAM_HALF:]) + rows_second

    def hop(value):
        return wide(onward(low(value), 1))

    far = low(wide(far_mine) + wide(far_arrived) + rows_first)
    firsts = [first_half(distance) for distance in (3, 2, 1)]
    seconds = [second_half(distance) for distance in (3, 2, 1)]
    firsts[0], seconds[0] = low(firsts[0]), low(seconds[0])
    far, firsts, seconds = lax.optimization_barrier((far, firsts, seconds))
    far = wide(onward(far, 2))
    first, second = wide(onward(firsts[0], 1)), wide(onward(seconds[0], 1))
    first, second = hop(firsts[1] + first + far), hop(seconds[1] + second)
    first, second = hop(firsts[2] + first), hop(seconds[2] + second)
    own_rows = behind(wide(rows), SQUARES - GRAM_HALF)
    first = first + wide(own[:GRAM_HALF]) + jnp.where(core == 0, 0.0, own_rows)
    second = second + wide(own[GRAM_HALF:]) + jnp.where(core == 0, own_rows, 0.0)
    partial = low(jnp.concatenate([first, second], axis=0))

    first, second, ratios = polynomial(place, partial, swap(partial))

    def final(parts, results):
        *results, after = finish(
            place, ratios, advance, weights.reshape(stacked), parts, results
        )
        return results, after

    results, begun = final([((first, second), 0, True)], None)
    parts = []
    for distance in (1, 2, 3):
        first, second = onward(first, 1), onward(second, 1)
        if distance == 2:
            far = onward(first, 2)
        parts.append((first, second))

    def both_ways(halves, distance, before):
        other = swap(jnp.concatenate(halves, axis=0) + before)
        return [(halves, distance, True), ((other,), distance, False)]

    results, after = final(
        both_ways(parts[0], 1, begun) + both_ways(parts[1], 2, begun), results
    )
    far = far + after
    (new_weights, updates), _ = final(
        both_ways(parts[2], 3, after) + [((far, swap(far)), 4, True)], results
    )
    whole = gradients.shape
    return (new_weights.reshape(whole), new_moments.reshape(whole), updates.reshape(whole))


def solution(mesh):
    return jax.shard_map(
        shards,
        mesh=mesh,
        in_specs=(
            P("mp", None, "dp", None),
            P("mp", None, "dp", None),
            P("mp", None, "dp", None),
            P("mp", None, None),
        ),
        out_specs=(P("mp", None, "dp", None), P("mp", None, "dp", None), P("mp", None, "dp", None)),
        check_vma=False,
    )
```

time: 91.9 us -> 82.3 us (0.90)
  starting transfers between devices: 42.2 us -> 48.7 us
  Pallas kernels: 23.7 us -> 18.5 us
  waiting for transfers between devices: 17 us -> 12.2 us
  local copies, waits for them, and re-layouts: 3.4 us -> 0.95 us
  other arithmetic: 3.1 us -> 0.97 us
  between operations: 2.19 us -> 0.82 us
    ppermute x12 -> x15, waiting for transfers between devices: 14.7 us -> 8.51 us  [the longest x14 8.51 us: onward(): return lax.ppermute(value, 'dp', pairs)]
    pallas_call x7 -> x5, Pallas kernels: 23.7 us -> 18.5 us  [the longest x3 8.66 us: finish(): pl.pallas_call(kernel, out_shape=(shape, shape, jax.ShapeDtypeStruct((1,...]
    ppermute x12 -> x15, starting transfers between devices: 28.3 us -> 32.9 us  [the longest x14 28.9 us: onward(): return lax.ppermute(value, 'dp', pairs)]
    convert_element_type x5 -> x6, other arithmetic: 2.33 us -> 0.3 us  [low(): return value.astype(jnp.bfloat16)]
    ppermute x7 -> x8, starting transfers between devices: 13.8 us -> 15.7 us  [swap(): return lax.ppermute(value, 'dp', swap_pairs)]
    ppermute x7 -> x8, waiting for transfers between devices: 2.28 us -> 3.67 us  [swap(): return lax.ppermute(value, 'dp', swap_pairs)]
    slice x2 -> x0, local copies, waits for them, and re-layouts: 1.22 us -> none  [the longest x1 0.61 us: shards(): last = onward(jnp.where(after[1] == 0, piece[:HALF], piece[HALF:]))]
    unnamed x15 -> x6, local copies, waits for them, and re-layouts: 1.85 us -> 0.71 us
  transfers between devices with their start and end apart: 19 -> 23, of which waited for: 11 -> 11; matrix products, arithmetic and copies ran while one was open for 3% -> 1% of each run, Pallas kernels for 7% -> 14%
where the time goes in v2:
time: 82.3 us; the launch traced here: 82.1 us
  starting transfers between devices  48.7 us (59%)
  Pallas kernels  18.5 us (22%)
  waiting for transfers between devices  12.2 us (15%)
  other arithmetic  0.97 us (1%)
  local copies, waits for them, and re-layouts  0.95 us (1%)
    ppermute x14, starting transfers between devices, onward(): return lax.ppermute(value, 'dp', pairs)  28.9 us
    ppermute x8, starting transfers between devices, swap(): return lax.ppermute(value, 'dp', swap_pairs)  15.7 us
    pallas_call x3, Pallas kernels, finish(): pl.pallas_call(kernel, out_shape=(shape, shape, jax.ShapeDtypeStruct((1,...  8.66 us
    ppermute x14, waiting for transfers between devices, onward(): return lax.ppermute(value, 'dp', pairs)  8.51 us
    pallas_call x1, Pallas kernels, grams(): pl.pallas_call(gram_kernel, out_shape=(full, full, shape(3, GRAM_ROWS, SI...  5.69 us
    pallas_call x1, Pallas kernels, polynomial(): pl.pallas_call(polynomial_kernel, out_shape=(jax.ShapeDtypeStruct((HALF,...  4.12 us
    ppermute x1, starting transfers between devices, observed_rows(): values = lax.ppermute(sent, ('dp', 'mp'), pairs).reshape(1, -1)  4.03 us
    ppermute x8, waiting for transfers between devices, swap(): return lax.ppermute(value, 'dp', swap_pairs)  3.67 us
  transfers between devices with their start and end apart: 23, of which 11 were waited for; matrix products, arithmetic and copies ran while one was open for 1% of the time, Pallas kernels for 14%

profile of v2, /device:TPU:1, one launch (start us, length us, event | category | flops | bytes accessed | tf_op | source)
XLA Modules:
  0.0 82.1 jit_solution(6721579004786219886)
XLA Ops:
  0.7 0.7 copy-done
  1.4 0.1 constant_dynamic-slice_fusion
  1.4 0.1 copy.11
  1.5 4.0 %collective-permute-start.1 = (f32[4,32]{1,0:T(4,128)S(1)}, f32[4,32]{1,0:T(4,128)S(1)}, u32[]{:S(2)}, u32[]{:S(2)}) collective-permute-start(f32[4,32]{1,0:T(4,128)S(1)} %bitcast.33), channel_id=1, source_target_pairs={{0,0},{1,1},{2,2},{3,3},{4,4},{5,5},{6,6},{7,7},{8,8},{9,9},{10,10... | collective-permute-start | bytes 1544 | tf_op jit(solution)/shard_map/ppermute | solution.py:402
  5.5 5.7 %shard_map.67 = (bf16[8,256,512]{2,1,0:T(8,128)(2,1)}, bf16[8,256,512]{2,1,0:T(8,128)(2,1)}, bf16[3,1088,128]{2,1,0:T(8,128)(2,1)S(1)}, bf16[3,1088,128]{2,1,0:T...) custom-call(bf16[8,256,512]{2,1,0:T(8,128)(2,1)} %bitcast.31, ...), custom_call_target="tpu_custom_call" | custom-call | flops 1073741824 | bytes 10485760 | tf_op jit(solution)/shard_map/pallas_call | solution.py:207
  11.2 0.1 collective-permute-start.3
  11.4 0.1 reshape.140
  11.5 0.1 select_convert_fusion
  11.6 0.6 collective-permute-start.2
  12.1 0.1 collective-permute-start
  12.2 1.5 %collective-permute-done.2 = bf16[64,128]{1,0:T(8,128)(2,1)S(1)} collective-permute-done((bf16[64,128]{1,0:T(8,128)(2,1)S(1)}, bf16[64,128]{1,0:T(8,128)(2,1)S(1)}, u32[]{:S(2)}, u32[]{:S(2)}) %collective-permute-start.2) | collective-permute-done | bytes 16416 | tf_op jit(solution)/shard_map/ppermute | solution.py:424
  13.7 0.1 fusion.7
  13.8 0.1 collective-permute-done
  14.0 0.2 pad_add_fusion.4
  14.2 10.0 %collective-permute-start.8 = (bf16[544,128]{1,0:T(8,128)(2,1)S(1)}, bf16[544,128]{1,0:T(8,128)(2,1)S(1)}, u32[]{:S(2)}, u32[]{:S(2)}) collective-permute-start(bf16[544,128]{1,0:T(8,128)(2,1)S(1)} %get-tuple-element.39), channel_id=1, source_target_pairs={{0,32},{16,240},{32,64},{48,16},{64,96},{80,48},{96,128},{112,80},... | collective-permute-start | bytes 417800 | tf_op jit(solution)/shard_map/ppermute | solution.py:428
  24.2 0.1 collective-permute-start.4
  24.3 1.4 %collective-permute-start.5 = (bf16[544,128]{1,0:T(8,128)(2,1)S(1)}, bf16[544,128]{1,0:T(8,128)(2,1)S(1)}, u32[]{:S(2)}, u32[]{:S(2)}) collective-permute-start(bf16[544,128]{1,0:T(8,128)(2,1)S(1)} %fusion.5), channel_id=1, source_target_pairs={{0,64},{16,208},{32,96},{48,240},{64,128},{80,16},{96,160},{112,48... | collective-permute-start | bytes 417800 | tf_op jit(solution)/shard_map/ppermute | solution.py:428
  25.7 0.5 collective-permute-done.8
  26.3 3.2 %collective-permute-start.9 = (bf16[544,128]{1,0:T(8,128)(2,1)S(1)}, bf16[544,128]{1,0:T(8,128)(2,1)S(1)}, u32[]{:S(2)}, u32[]{:S(2)}) collective-permute-start(bf16[544,128]{1,0:T(8,128)(2,1)S(1)} %add_convert_fusion.1), channel_id=1, source_target_pairs={{0,32},{16,240},{32,64},{48,16},{64,96},{80,48},{96,128},{112,80},... | collective-permute-start | bytes 417800 | tf_op jit(solution)/shard_map/ppermute | solution.py:428
  29.4 0.2 collective-permute-done.4
  29.7 4.1 %collective-permute-start.6 = (bf16[544,128]{1,0:T(8,128)(2,1)S(1)}, bf16[544,128]{1,0:T(8,128)(2,1)S(1)}, u32[]{:S(2)}, u32[]{:S(2)}) collective-permute-start(bf16[544,128]{1,0:T(8,128)(2,1)S(1)} %add_convert_fusion.3), channel_id=1, source_target_pairs={{0,32},{16,240},{32,64},{48,16},{64,96},{80,48},{96,128},{112,80},... | collective-permute-start | bytes 417800 | tf_op jit(solution)/shard_map/ppermute | solution.py:428
  33.8 1.6 %collective-permute-start.10 = (bf16[544,128]{1,0:T(8,128)(2,1)S(1)}, bf16[544,128]{1,0:T(8,128)(2,1)S(1)}, u32[]{:S(2)}, u32[]{:S(2)}) collective-permute-start(bf16[544,128]{1,0:T(8,128)(2,1)S(1)} %add_convert_fusion), channel_id=1, source_target_pairs={{0,32},{16,240},{32,64},{48,16},{64,96},{80,48},{96,128},{112,80},... | collective-permute-start | bytes 417800 | tf_op jit(solution)/shard_map/ppermute | solution.py:428
  35.4 0.4 collective-permute-done.6
  35.8 3.2 %collective-permute-start.7 = (bf16[544,128]{1,0:T(8,128)(2,1)S(1)}, bf16[544,128]{1,0:T(8,128)(2,1)S(1)}, u32[]{:S(2)}, u32[]{:S(2)}) collective-permute-start(bf16[544,128]{1,0:T(8,128)(2,1)S(1)} %add_convert_fusion.2), channel_id=1, source_target_pairs={{0,32},{16,240},{32,64},{48,16},{64,96},{80,48},{96,128},{112,80},... | collective-permute-start | bytes 417800 | tf_op jit(solution)/shard_map/ppermute | solution.py:428
  39.0 2.0 %collective-permute-done.7 = bf16[544,128]{1,0:T(8,128)(2,1)S(1)} collective-permute-done((bf16[544,128]{1,0:T(8,128)(2,1)S(1)}, bf16[544,128]{1,0:T(8,128)(2,1)S(1)}, u32[]{:S(2)}, u32[]{:S(2)}) %collective-permute-start.7) | collective-permute-done | bytes 139296 | tf_op jit(solution)/shard_map/ppermute | solution.py:428
  41.0 0.1 fusion.1
  41.1 5.7 %collective-permute-start.11 = (bf16[1088,128]{1,0:T(8,128)(2,1)S(1)}, bf16[1088,128]{1,0:T(8,128)(2,1)S(1)}, u32[]{:S(2)}, u32[]{:S(2)}) collective-permute-start(bf16[1088,128]{1,0:T(8,128)(2,1)S(1)} %pad_maximum_fusion.mine_ref), channel_id=1, source_target_pairs={{0,16},{16,0},{32,48},{48,32},{64,80},{80,64},{96,112},{112,96},{1... | collective-permute-start | bytes 835592 | tf_op jit(solution)/shard_map/ppermute | solution.py:424
  46.8 0.1 pad_add_fusion.7.place_ref
  46.9 1.1 %collective-permute-done.11.theirs_ref = bf16[1088,128]{1,0:T(8,128)(2,1)S(1)} collective-permute-done((bf16[1088,128]{1,0:T(8,128)(2,1)S(1)}, bf16[1088,128]{1,0:T(8,128)(2,1)S(1)}, u32[]{:S(2)}, u32[]{:S(2)}) %collective-permute-start.11) | collective-permute-done | bytes 278560 | tf_op jit(solution)/shard_map/ppermute | solution.py:424
  48.0 4.1 %shard_map.68 = (bf16[528,128]{1,0:T(8,128)(2,1)S(1)}, bf16[528,128]{1,0:T(8,128)(2,1)S(1)}, f32[1,128]{1,0:T(1,128)S(1)}) custom-call(s32[2]{0:T(128)S(1)} %pad_add_fusion.7.place_ref, bf16[1088,128]{1,0:T(8,128)(2,1)S(1)} %pad_maximum_fusion.mine_ref, bf16[1088,128]{1,0:T(8,128)(2,1)S(1)} %collective-permute-done.11.theirs_ref), custom_call_target="tpu_custom_call" | custom-call | flops 2415919104 | bytes 811008 | tf_op jit(solution)/shard_map/pallas_call | solution.py:281
  52.2 0.1 collective-permute-start.12
  52.2 0.1 collective-permute-start.15
  52.3 3.8 %collective-permute-done.12.refs_0_ = bf16[528,128]{1,0:T(8,128)(2,1)S(1)} collective-permute-done((bf16[528,128]{1,0:T(8,128)(2,1)S(1)}, bf16[528,128]{1,0:T(8,128)(2,1)S(1)}, u32[]{:S(2)}, u32[]{:S(2)}) %collective-permute-start.12) | collective-permute-done | bytes 135200 | tf_op jit(solution)/shard_map/ppermute | solution.py:428
  56.1 1.2 %collective-permute-start.13 = (bf16[528,128]{1,0:T(8,128)(2,1)S(1)}, bf16[528,128]{1,0:T(8,128)(2,1)S(1)}, u32[]{:S(2)}, u32[]{:S(2)}) collective-permute-start(bf16[528,128]{1,0:T(8,128)(2,1)S(1)} %collective-permute-done.12.refs_0_), channel_id=1, source_target_pairs={{0,32},{16,240},{32,64},{48,16},{64,96},{80,48},{96,128},{112,80},... | collective-permute-start | bytes 405512 | tf_op jit(solution)/shard_map/ppermute | solution.py:428
  57.3 0.5 collective-permute-done.15.refs_1_
  57.8 0.9 %collective-permute-start.16 = (bf16[528,128]{1,0:T(8,128)(2,1)S(1)}, bf16[528,128]{1,0:T(8,128)(2,1)S(1)}, u32[]{:S(2)}, u32[]{:S(2)}) collective-permute-start(bf16[528,128]{1,0:T(8,128)(2,1)S(1)} %collective-permute-done.15.refs_1_), channel_id=1, source_target_pairs={{0,32},{16,240},{32,64},{48,16},{64,96},{80,48},{96,128},{112,80},... | collective-permute-start | bytes 405512 | tf_op jit(solution)/shard_map/ppermute | solution.py:428
  58.8 1.8 %shard_map.69 = (bf16[8,256,512]{2,1,0:T(8,128)(2,1)}, bf16[8,256,512]{2,1,0:T(8,128)(2,1)}, bf16[1,128]{1,0:T(2,128)(2,1)S(1)}) custom-call(s32[2]{0:T(128)S(1)} %pad_add_fusion.7.place_ref, f32[1,128]{1,0:T(1,128)S(1)} %get-tuple-element.40.ratio_ref, bf16[8,256,512]{2,1,0:T(8,128)(2,1)S(1)} %copy-done.2, bf16[8,256,512]{2,1,0:T(8,128)(2,1)S(1)} %bitcast.23, ...), custom_call_target="tpu_custom_call" | custom-call | flops 134217728 | bytes 1318912 | tf_op jit(solution)/shard_map/pallas_call | solution.py:372
  60.5 1.2 %collective-permute-done.16.refs_4_ = bf16[528,128]{1,0:T(8,128)(2,1)S(1)} collective-permute-done((bf16[528,128]{1,0:T(8,128)(2,1)S(1)}, bf16[528,128]{1,0:T(8,128)(2,1)S(1)}, u32[]{:S(2)}, u32[]{:S(2)}) %collective-permute-start.16) | collective-permute-done | bytes 135200 | tf_op jit(solution)/shard_map/ppermute | solution.py:428
  61.7 0.1 maximum_add_fusion.2
  61.8 4.9 %collective-permute-start.18 = (bf16[1056,128]{1,0:T(8,128)(2,1)S(1)}, bf16[1056,128]{1,0:T(8,128)(2,1)S(1)}, u32[]{:S(2)}, u32[]{:S(2)}) collective-permute-start(bf16[1056,128]{1,0:T(8,128)(2,1)S(1)} %get-tuple-element.69), channel_id=1, source_target_pairs={{0,16},{16,0},{32,48},{48,32},{64,80},{80,64},{96,112},{112,96},{1... | collective-permute-start | bytes 811016 | tf_op jit(solution)/shard_map/ppermute | solution.py:424
  66.7 0.1 collective-permute-start.19
  66.8 0.3 collective-permute-start.14
  67.1 2.7 %collective-permute-start.21 = (bf16[528,128]{1,0:T(8,128)(2,1)S(1)}, bf16[528,128]{1,0:T(8,128)(2,1)S(1)}, u32[]{:S(2)}, u32[]{:S(2)}) collective-permute-start(bf16[528,128]{1,0:T(8,128)(2,1)S(1)} %collective-permute-done.13.refs_3_), channel_id=1, source_target_pairs={{0,64},{16,208},{32,96},{48,240},{64,128},{80,16},{96,160},{112,48... | collective-permute-start | bytes 405512 | tf_op jit(solution)/shard_map/ppermute | solution.py:428
  69.8 3.7 %shard_map.70 = (bf16[8,256,512]{2,1,0:T(8,128)(2,1)}, bf16[8,256,512]{2,1,0:T(8,128)(2,1)}, bf16[1,128]{1,0:T(2,128)(2,1)S(1)}) custom-call(s32[2]{0:T(128)S(1)} %pad_add_fusion.7.place_ref, f32[1,128]{1,0:T(1,128)S(1)} %get-tuple-element.40.ratio_ref, bf16[8,256,512]{2,1,0:T(8,128)(2,1)S(1)} %copy-done.2, ...), custom_call_target="tpu_custom_call", output_to_operand_aliasing={{0}: (10, {}), {1}: (11, {})} | custom-call | flops 536870912 | bytes 5275648 | tf_op jit(solution)/shard_map/pallas_call | solution.py:372
  73.6 1.4 %collective-permute-start.20 = (bf16[1056,128]{1,0:T(8,128)(2,1)S(1)}, bf16[1056,128]{1,0:T(8,128)(2,1)S(1)}, u32[]{:S(2)}, u32[]{:S(2)}) collective-permute-start(bf16[1056,128]{1,0:T(8,128)(2,1)S(1)} %maximum_add_fusion), channel_id=1, source_target_pairs={{0,16},{16,0},{32,48},{48,32},{64,80},{80,64},{96,112},{112,96},{1... | collective-permute-start | bytes 811016 | tf_op jit(solution)/shard_map/ppermute | solution.py:424
  75.0 2.8 %collective-permute-start.22 = (bf16[528,128]{1,0:T(8,128)(2,1)S(1)}, bf16[528,128]{1,0:T(8,128)(2,1)S(1)}, u32[]{:S(2)}, u32[]{:S(2)}) collective-permute-start(bf16[528,128]{1,0:T(8,128)(2,1)S(1)} %broadcast_add_fusion.refs_3_), channel_id=1, source_target_pairs={{0,16},{16,0},{32,48},{48,32},{64,80},{80,64},{96,112},{112,96},{1... | collective-permute-start | bytes 405512 | tf_op jit(solution)/shard_map/ppermute | solution.py:424
  77.9 1.0 %collective-permute-done.22.refs_4_ = bf16[528,128]{1,0:T(8,128)(2,1)S(1)} collective-permute-done((bf16[528,128]{1,0:T(8,128)(2,1)S(1)}, bf16[528,128]{1,0:T(8,128)(2,1)S(1)}, u32[]{:S(2)}, u32[]{:S(2)}) %collective-permute-start.22) | collective-permute-done | bytes 135200 | tf_op jit(solution)/shard_map/ppermute | solution.py:424
  78.9 3.2 %shard_map.71 = (bf16[8,256,512]{2,1,0:T(8,128)(2,1)}, bf16[8,256,512]{2,1,0:T(8,128)(2,1)}, bf16[1,128]{1,0:T(2,128)(2,1)}) custom-call(s32[2]{0:T(128)S(1)} %pad_add_fusion.7.place_ref, f32[1,128]{1,0:T(1,128)S(1)} %get-tuple-element.40.ratio_ref, bf16[8,256,512]{2,1,0:T(8,128)(2,1)S(1)} %copy-done.2, ...), custom_call_target="tpu_custom_call", output_to_operand_aliasing={{0}: (9, {}), {1}: (10, {})} | custom-call | flops 402653184 | bytes 3956736 | tf_op jit(solution)/shard_map/pallas_call | solution.py:372
  (29 shorter events, 0.4 us)
Async XLA Ops:
  0.6 0.7 copy-start
  1.5 9.9 %collective-permute-start.1 = (f32[4,32]{1,0:T(4,128)S(1)}, f32[4,32]{1,0:T(4,128)S(1)}, u32[]{:S(2)}, u32[]{:S(2)}) collective-permute-start(f32[4,32]{1,0:T(4,128)S(1)} %bitcast.33), channel_id=1, source_target_pairs={{0,0},{1,1},{2,2},{3,3},{4,4},{5,5},{6,6},{7,7},{8,8},{9,9},{10,10... | collective-permute-start | bytes 1544 | tf_op jit(solution)/shard_map/ppermute | solution.py:402
  11.2 2.7 %collective-permute-start.3 = (bf16[3,1088,128]{2,1,0:T(8,128)(2,1)S(1)}, bf16[3,1088,128]{2,1,0:T(8,128)(2,1)S(1)}, u32[]{:S(2)}, u32[]{:S(2)}) collective-permute-start(bf16[3,1088,128]{2,1,0:T(8,128)(2,1)S(1)} %get-tuple-element.31), channel_id=1, source_target_pairs={{0,16},{16,0},{32,48},{48,32},{64,80},{80,64},{96,112},{112,96},{1... | collective-permute-start | bytes 2506760 | tf_op jit(solution)/shard_map/ppermute | solution.py:424
  11.6 2.1 %collective-permute-start.2 = (bf16[64,128]{1,0:T(8,128)(2,1)S(1)}, bf16[64,128]{1,0:T(8,128)(2,1)S(1)}, u32[]{:S(2)}, u32[]{:S(2)}) collective-permute-start(bf16[64,128]{1,0:T(8,128)(2,1)S(1)} %get-tuple-element.66), channel_id=1, source_target_pairs={{0,16},{16,0},{32,48},{48,32},{64,80},{80,64},{96,112},{112,96},{1... | collective-permute-start | bytes 49160 | tf_op jit(solution)/shard_map/ppermute | solution.py:424
  12.1 1.8 %collective-permute-start = (bf16[544,128]{1,0:T(8,128)(2,1)S(1)}, bf16[544,128]{1,0:T(8,128)(2,1)S(1)}, u32[]{:S(2)}, u32[]{:S(2)}) collective-permute-start(bf16[544,128]{1,0:T(8,128)(2,1)S(1)} %get-tuple-element.29), channel_id=1, source_target_pairs={{0,16},{16,0},{32,48},{48,32},{64,80},{80,64},{96,112},{112,96},{1... | collective-permute-start | bytes 417800 | tf_op jit(solution)/shard_map/ppermute | solution.py:424
  14.2 12.1 %collective-permute-start.8 = (bf16[544,128]{1,0:T(8,128)(2,1)S(1)}, bf16[544,128]{1,0:T(8,128)(2,1)S(1)}, u32[]{:S(2)}, u32[]{:S(2)}) collective-permute-start(bf16[544,128]{1,0:T(8,128)(2,1)S(1)} %get-tuple-element.39), channel_id=1, source_target_pairs={{0,32},{16,240},{32,64},{48,16},{64,96},{80,48},{96,128},{112,80},... | collective-permute-start | bytes 417800 | tf_op jit(solution)/shard_map/ppermute | solution.py:428
  24.2 5.4 %collective-permute-start.4 = (bf16[544,128]{1,0:T(8,128)(2,1)S(1)}, bf16[544,128]{1,0:T(8,128)(2,1)S(1)}, u32[]{:S(2)}, u32[]{:S(2)}) collective-permute-start(bf16[544,128]{1,0:T(8,128)(2,1)S(1)} %get-tuple-element.34), channel_id=1, source_target_pairs={{0,32},{16,240},{32,64},{48,16},{64,96},{80,48},{96,128},{112,80},... | collective-permute-start | bytes 417800 | tf_op jit(solution)/shard_map/ppermute | solution.py:428
  24.3 5.3 %collective-permute-start.5 = (bf16[544,128]{1,0:T(8,128)(2,1)S(1)}, bf16[544,128]{1,0:T(8,128)(2,1)S(1)}, u32[]{:S(2)}, u32[]{:S(2)}) collective-permute-start(bf16[544,128]{1,0:T(8,128)(2,1)S(1)} %fusion.5), channel_id=1, source_target_pairs={{0,64},{16,208},{32,96},{48,240},{64,128},{80,16},{96,160},{112,48... | collective-permute-start | bytes 417800 | tf_op jit(solution)/shard_map/ppermute | solution.py:428
  26.3 7.5 %collective-permute-start.9 = (bf16[544,128]{1,0:T(8,128)(2,1)S(1)}, bf16[544,128]{1,0:T(8,128)(2,1)S(1)}, u32[]{:S(2)}, u32[]{:S(2)}) collective-permute-start(bf16[544,128]{1,0:T(8,128)(2,1)S(1)} %add_convert_fusion.1), channel_id=1, source_target_pairs={{0,32},{16,240},{32,64},{48,16},{64,96},{80,48},{96,128},{112,80},... | collective-permute-start | bytes 417800 | tf_op jit(solution)/shard_map/ppermute | solution.py:428
  29.7 6.1 %collective-permute-start.6 = (bf16[544,128]{1,0:T(8,128)(2,1)S(1)}, bf16[544,128]{1,0:T(8,128)(2,1)S(1)}, u32[]{:S(2)}, u32[]{:S(2)}) collective-permute-start(bf16[544,128]{1,0:T(8,128)(2,1)S(1)} %add_convert_fusion.3), channel_id=1, source_target_pairs={{0,32},{16,240},{32,64},{48,16},{64,96},{80,48},{96,128},{112,80},... | collective-permute-start | bytes 417800 | tf_op jit(solution)/shard_map/ppermute | solution.py:428
  33.8 5.2 %collective-permute-start.10 = (bf16[544,128]{1,0:T(8,128)(2,1)S(1)}, bf16[544,128]{1,0:T(8,128)(2,1)S(1)}, u32[]{:S(2)}, u32[]{:S(2)}) collective-permute-start(bf16[544,128]{1,0:T(8,128)(2,1)S(1)} %add_convert_fusion), channel_id=1, source_target_pairs={{0,32},{16,240},{32,64},{48,16},{64,96},{80,48},{96,128},{112,80},... | collective-permute-start | bytes 417800 | tf_op jit(solution)/shard_map/ppermute | solution.py:428
  35.8 5.2 %collective-permute-start.7 = (bf16[544,128]{1,0:T(8,128)(2,1)S(1)}, bf16[544,128]{1,0:T(8,128)(2,1)S(1)}, u32[]{:S(2)}, u32[]{:S(2)}) collective-permute-start(bf16[544,128]{1,0:T(8,128)(2,1)S(1)} %add_convert_fusion.2), channel_id=1, source_target_pairs={{0,32},{16,240},{32,64},{48,16},{64,96},{80,48},{96,128},{112,80},... | collective-permute-start | bytes 417800 | tf_op jit(solution)/shard_map/ppermute | solution.py:428
  41.1 6.9 %collective-permute-start.11 = (bf16[1088,128]{1,0:T(8,128)(2,1)S(1)}, bf16[1088,128]{1,0:T(8,128)(2,1)S(1)}, u32[]{:S(2)}, u32[]{:S(2)}) collective-permute-start(bf16[1088,128]{1,0:T(8,128)(2,1)S(1)} %pad_maximum_fusion.mine_ref), channel_id=1, source_target_pairs={{0,16},{16,0},{32,48},{48,32},{64,80},{80,64},{96,112},{112,96},{1... | collective-permute-start | bytes 835592 | tf_op jit(solution)/shard_map/ppermute | solution.py:424
  46.9 11.8 %copy-start.1 = (bf16[4,2,256,512]{3,2,1,0:T(8,128)(2,1)S(1)}, bf16[4,2,256,512]{3,2,1,0:T(8,128)(2,1)}, u32[]{:S(2)}) copy-start(bf16[4,2,256,512]{3,2,1,0:T(8,128)(2,1)} %param.6) | copy-start | bytes 6291460
  46.9 11.8 %copy-start.2 = (bf16[8,256,512]{2,1,0:T(8,128)(2,1)S(1)}, bf16[8,256,512]{2,1,0:T(8,128)(2,1)}, u32[]{:S(2)}) copy-start(bf16[8,256,512]{2,1,0:T(8,128)(2,1)} %get-tuple-element.41.advance_ref) | copy-start | bytes 6291460
  52.2 3.9 %collective-permute-start.12 = (bf16[528,128]{1,0:T(8,128)(2,1)S(1)}, bf16[528,128]{1,0:T(8,128)(2,1)S(1)}, u32[]{:S(2)}, u32[]{:S(2)}) collective-permute-start(bf16[528,128]{1,0:T(8,128)(2,1)S(1)} %get-tuple-element.42.refs_0_), channel_id=1, source_target_pairs={{0,32},{16,240},{32,64},{48,16},{64,96},{80,48},{96,128},{112,80},... | collective-permute-start | bytes 405512 | tf_op jit(solution)/shard_map/ppermute | solution.py:428
  52.2 5.6 %collective-permute-start.15 = (bf16[528,128]{1,0:T(8,128)(2,1)S(1)}, bf16[528,128]{1,0:T(8,128)(2,1)S(1)}, u32[]{:S(2)}, u32[]{:S(2)}) collective-permute-start(bf16[528,128]{1,0:T(8,128)(2,1)S(1)} %get-tuple-element.43.refs_1_), channel_id=1, source_target_pairs={{0,32},{16,240},{32,64},{48,16},{64,96},{80,48},{96,128},{112,80},... | collective-permute-start | bytes 405512 | tf_op jit(solution)/shard_map/ppermute | solution.py:428
  56.1 4.4 %collective-permute-start.13 = (bf16[528,128]{1,0:T(8,128)(2,1)S(1)}, bf16[528,128]{1,0:T(8,128)(2,1)S(1)}, u32[]{:S(2)}, u32[]{:S(2)}) collective-permute-start(bf16[528,128]{1,0:T(8,128)(2,1)S(1)} %collective-permute-done.12.refs_0_), channel_id=1, source_target_pairs={{0,32},{16,240},{32,64},{48,16},{64,96},{80,48},{96,128},{112,80},... | collective-permute-start | bytes 405512 | tf_op jit(solution)/shard_map/ppermute | solution.py:428
  57.8 3.9 %collective-permute-start.16 = (bf16[528,128]{1,0:T(8,128)(2,1)S(1)}, bf16[528,128]{1,0:T(8,128)(2,1)S(1)}, u32[]{:S(2)}, u32[]{:S(2)}) collective-permute-start(bf16[528,128]{1,0:T(8,128)(2,1)S(1)} %collective-permute-done.15.refs_1_), channel_id=1, source_target_pairs={{0,32},{16,240},{32,64},{48,16},{64,96},{80,48},{96,128},{112,80},... | collective-permute-start | bytes 405512 | tf_op jit(solution)/shard_map/ppermute | solution.py:428
  61.8 8.0 %collective-permute-start.18 = (bf16[1056,128]{1,0:T(8,128)(2,1)S(1)}, bf16[1056,128]{1,0:T(8,128)(2,1)S(1)}, u32[]{:S(2)}, u32[]{:S(2)}) collective-permute-start(bf16[1056,128]{1,0:T(8,128)(2,1)S(1)} %get-tuple-element.69), channel_id=1, source_target_pairs={{0,16},{16,0},{32,48},{48,32},{64,80},{80,64},{96,112},{112,96},{1... | collective-permute-start | bytes 811016 | tf_op jit(solution)/shard_map/ppermute | solution.py:424
  66.7 3.1 %collective-permute-start.19 = (bf16[1056,128]{1,0:T(8,128)(2,1)S(1)}, bf16[1056,128]{1,0:T(8,128)(2,1)S(1)}, u32[]{:S(2)}, u32[]{:S(2)}) collective-permute-start(bf16[1056,128]{1,0:T(8,128)(2,1)S(1)} %get-tuple-element.68), channel_id=1, source_target_pairs={{0,16},{16,0},{32,48},{48,32},{64,80},{80,64},{96,112},{112,96},{1... | collective-permute-start | bytes 811016 | tf_op jit(solution)/shard_map/ppermute | solution.py:424
  66.8 6.8 %collective-permute-start.14 = (bf16[528,128]{1,0:T(8,128)(2,1)S(1)}, bf16[528,128]{1,0:T(8,128)(2,1)S(1)}, u32[]{:S(2)}, u32[]{:S(2)}) collective-permute-start(bf16[528,128]{1,0:T(8,128)(2,1)S(1)} %collective-permute-done.13.refs_3_), channel_id=1, source_target_pairs={{0,32},{16,240},{32,64},{48,16},{64,96},{80,48},{96,128},{112,80},... | collective-permute-start | bytes 405512 | tf_op jit(solution)/shard_map/ppermute | solution.py:428
  67.1 6.5 %collective-permute-start.17 = (bf16[528,128]{1,0:T(8,128)(2,1)S(1)}, bf16[528,128]{1,0:T(8,128)(2,1)S(1)}, u32[]{:S(2)}, u32[]{:S(2)}) collective-permute-start(bf16[528,128]{1,0:T(8,128)(2,1)S(1)} %collective-permute-done.16.refs_4_), channel_id=1, source_target_pairs={{0,32},{16,240},{32,64},{48,16},{64,96},{80,48},{96,128},{112,80},... | collective-permute-start | bytes 405512 | tf_op jit(solution)/shard_map/ppermute | solution.py:428
  67.1 7.9 %collective-permute-start.21 = (bf16[528,128]{1,0:T(8,128)(2,1)S(1)}, bf16[528,128]{1,0:T(8,128)(2,1)S(1)}, u32[]{:S(2)}, u32[]{:S(2)}) collective-permute-start(bf16[528,128]{1,0:T(8,128)(2,1)S(1)} %collective-permute-done.13.refs_3_), channel_id=1, source_target_pairs={{0,64},{16,208},{32,96},{48,240},{64,128},{80,16},{96,160},{112,48... | collective-permute-start | bytes 405512 | tf_op jit(solution)/shard_map/ppermute | solution.py:428
  73.6 5.3 %collective-permute-start.20 = (bf16[1056,128]{1,0:T(8,128)(2,1)S(1)}, bf16[1056,128]{1,0:T(8,128)(2,1)S(1)}, u32[]{:S(2)}, u32[]{:S(2)}) collective-permute-start(bf16[1056,128]{1,0:T(8,128)(2,1)S(1)} %maximum_add_fusion), channel_id=1, source_target_pairs={{0,16},{16,0},{32,48},{48,32},{64,80},{80,64},{96,112},{112,96},{1... | collective-permute-start | bytes 811016 | tf_op jit(solution)/shard_map/ppermute | solution.py:424
  75.0 3.8 %collective-permute-start.22 = (bf16[528,128]{1,0:T(8,128)(2,1)S(1)}, bf16[528,128]{1,0:T(8,128)(2,1)S(1)}, u32[]{:S(2)}, u32[]{:S(2)}) collective-permute-start(bf16[528,128]{1,0:T(8,128)(2,1)S(1)} %broadcast_add_fusion.refs_3_), channel_id=1, source_target_pairs={{0,16},{16,0},{32,48},{48,32},{64,80},{80,64},{96,112},{112,96},{1... | collective-permute-start | bytes 405512 | tf_op jit(solution)/shard_map/ppermute | solution.py:424

commit v3 on v2

--- a/solution.py
+++ b/solution.py
@@ -49,7 +49,7 @@
 ORDER = ((0, 1), (0, 2), (0, 3)), ((1, 2), (1, 3), (2, 3))
 
 
-def pack(blocks, rows, residuals=False):
+def pack(blocks, rows, residuals=False, peaks=None):
     upper = square_iota(0) <= square_iota(1)
     pieces = []
     for which in range(2):
@@ -63,6 +63,10 @@
         extra = jnp.where(row == i, values, extra)
         if residuals:
             extra = jnp.where(row == 4 + i, values - wide(low(values)), extra)
+    if peaks is not None:
+        for i in range(3):
+            extra = jnp.where(row == 8 + i, peaks, extra)
+            peaks = peaks - wide(low(peaks))
     return jnp.concatenate([low(piece) for piece in pieces + [extra]], axis=0)
 
 
@@ -225,18 +229,18 @@
     )(gradients, moments)
 
 
-def polynomial_kernel(place_ref, mine_ref, theirs_ref, first_ref, second_ref, ratio_ref):
+def polynomial_kernel(
+    place_ref, mine_first, mine_second, theirs_first, theirs_second, first_ref, second_ref
+):
     natural = place_ref[1] == 0
-    mine, theirs = wide(mine_ref[...]), wide(theirs_ref[...])
-    first = mine[:GRAM_HALF] + theirs[GRAM_HALF:]
-    second = mine[GRAM_HALF:] + theirs[:GRAM_HALF]
+    first = wide(mine_first[...]) + wide(theirs_second[...])
+    second = wide(mine_second[...]) + wide(theirs_first[...])
     packed = jnp.concatenate(
         [jnp.where(natural, first, second), jnp.where(natural, second, first)], axis=0
     )
     blocks, extra = unpack_blocks(packed, jnp.float32)
     logits = extra[16:32] + extra[32:48] + extra[48:64]
     peaks = jnp.max(logits, axis=0, keepdims=True)
-    ratio_ref[...] = jnp.sqrt(jnp.minimum(1.0, CLIP_LIMIT / peaks))
     corners = off_corner(blocks)
     gram = jnp.concatenate(
         [
@@ -270,7 +274,7 @@
         rest = FIRST_COEFF * rest + factor * step + product(rest, step)
         factor = factor * FIRST_COEFF
     total = jnp.where(diagonal, rest + factor, rest) * scale
-    packed = pack(cut_blocks(total), PACKED, residuals=True)
+    packed = pack(cut_blocks(total), PACKED, residuals=True, peaks=peaks)
     first_ref[...] = jnp.where(natural, packed[:HALF], packed[HALF:])
     second_ref[...] = jnp.where(natural, packed[HALF:], packed[:HALF])
 
@@ -278,26 +282,30 @@
 def polynomial(place, mine, theirs):
     width = 4 * SIDE
     whole = pl.BlockSpec(memory_space=pltpu.VMEM)
+    half = jax.ShapeDtypeStruct((HALF, SIDE), jnp.bfloat16)
     return pl.pallas_call(
         polynomial_kernel,
-        out_shape=(
-            jax.ShapeDtypeStruct((HALF, SIDE), jnp.bfloat16),
-            jax.ShapeDtypeStruct((HALF, SIDE), jnp.bfloat16),
-            jax.ShapeDtypeStruct((1, SIDE), jnp.float32),
-        ),
-        in_specs=[pl.BlockSpec(memory_space=pltpu.SMEM), whole, whole],
-        out_specs=(whole, whole, whole),
+        out_shape=(half, half),
+        in_specs=[pl.BlockSpec(memory_space=pltpu.SMEM)] + [whole] * 4,
+        out_specs=(whole, whole),
         compiler_params=pltpu.CompilerParams(vmem_limit_bytes=40 * MEBI),
         cost_estimate=pl.CostEstimate(
             flops=9 * 2 * width**3, bytes_accessed=6 * PACKED * SIDE, transcendentals=0
         ),
-    )(place, mine, theirs)
-
-
-def finish(place, ratios, advance, weights, parts, results):
+    )(place, *mine, *theirs)
+
+
+def finish(place, peaks, advance, weights, parts, results):
     matrices, rows, width = advance.shape
-    pieces = [half for halves, _, _ in parts for half in halves]
-    where = [sum(len(halves) for halves, _, _ in parts[:k]) for k in range(len(parts) + 1)]
+    pieces = []
+    for halves, _, _ in parts:
+        for array, _ in halves:
+            if not any(array is piece for piece in pieces):
+                pieces.append(array)
+    places = [
+        [([array is piece for piece in pieces].index(True), row) for array, row in halves]
+        for halves, _, _ in parts
+    ]
     count = len(parts)
     middle = width // 2
     scaling = 0.2 * math.sqrt(max(rows * matrices * 2, width))
@@ -310,17 +318,28 @@
             chosen = jnp.where(step == k, signed, chosen)
         return lax.rem(place[0] + chosen, matrices)
 
-    def kernel(place_ref, ratio_ref, advance_ref, weight_ref, *refs):
-        new_weight_ref, update_ref, after_ref = refs[-4:-1]
-        after_ref[...] = jnp.zeros_like(after_ref)
+    def kernel(place_ref, peaks_ref, advance_ref, weight_ref, *refs):
+        new_weight_ref, update_ref, peaks_out_ref, after_ref = refs[-5:-1]
         matrix_ref = refs[-1]
         step = pl.program_id(0)
+
+        @pl.when(step == 0)
+        def _():
+            after_ref[...] = jnp.zeros_like(after_ref)
+            known = peaks_ref[...]
+            if peaks is None:
+                for k in range(count):
+                    ends = [wide(refs[i][row + HALF - 32 : row + HALF]) for i, row in places[k]]
+                    natural = place_ref[1] == (0 if parts[k][2] else 1)
+                    end = jnp.where(natural, ends[1], ends[0])
+                    known = jnp.maximum(known, end[8:9] + end[9:10] + end[10:11])
+            peaks_out_ref[...] = known
+
         for k in range(count):
 
             @pl.when(step == k)
             def _():
-                halves = jnp.concatenate([ref[...] for ref in refs[where[k] : where[k + 1]]], axis=0)
-                first, second = halves[:HALF], halves[HALF:]
+                first, second = [refs[i][row : row + HALF] for i, row in places[k]]
                 natural = place_ref[1] == (0 if parts[k][2] else 1)
                 packed = jnp.concatenate(
                     [jnp.where(natural, first, second), jnp.where(natural, second, first)], axis=0
@@ -335,13 +354,14 @@
                     )
 
         which = index(step, place_ref)
+        ratios = jnp.sqrt(jnp.minimum(1.0, CLIP_LIMIT / peaks_out_ref[...]))
         lane = lax.broadcasted_iota(jnp.int32, (1, SIDE), 1)
         head = (which // 2) * (SIDE * 2 // matrices) + (place_ref[0] * 2 + place_ref[1]) * 2
         row = lax.broadcasted_iota(jnp.int32, (rows, 1), 0)
         factor = jnp.zeros((rows, 1), jnp.float32)
         for k in range(rows // DK):
             ratio = jnp.sum(
-                jnp.where(lane == head + k, ratio_ref[...], 0.0), axis=1, keepdims=True
+                jnp.where(lane == head + k, ratios, 0.0), axis=1, keepdims=True
             )
             factor = jnp.where(row // DK == k, ratio, factor)
         factor = jnp.where(which % 2 == 0, factor, 1.0)
@@ -371,14 +391,19 @@
     first_carried = 4 + len(pieces)
     return pl.pallas_call(
         kernel,
-        out_shape=(shape, shape, jax.ShapeDtypeStruct((1, SIDE), jnp.bfloat16)),
+        out_shape=(
+            shape,
+            shape,
+            jax.ShapeDtypeStruct((1, SIDE), jnp.float32),
+            jax.ShapeDtypeStruct((1, SIDE), jnp.bfloat16),
+        ),
         grid_spec=pltpu.PrefetchScalarGridSpec(
             num_scalar_prefetch=1,
             grid=(count,),
             in_specs=[one_row, full, full]
             + [pl.BlockSpec(half.shape, lambda step, place: (0, 0)) for half in pieces]
              + [anywhere] * len(carry),
-            out_specs=(full, full, one_row),
+            out_specs=(full, full, one_row, one_row),
             scratch_shapes=[pltpu.VMEM((width + 16, width), jnp.bfloat16)],
         ),
         input_output_aliases={first_carried + k: k for k in range(len(carry))},
@@ -388,10 +413,17 @@
             bytes_accessed=count * (8 * rows * width + 2 * PACKED * SIDE),
             transcendentals=0,
         ),
-    )(place, ratios, advance, weights, *pieces, *carry)
-
-
-def observed_rows(head_logits, layers):
+    )(
+        place,
+        jnp.zeros((1, SIDE), jnp.float32) if peaks is None else peaks,
+        advance,
+        weights,
+        *pieces,
+        *carry,
+    )
+
+
+def observed(head_logits, layers):
     parties, observers = lax.axis_size("dp"), lax.axis_size("mp")
     dp = lax.axis_index("dp")
     start = jnp.bitwise_xor(lax.axis_index("mp"), dp) * layers
@@ -399,7 +431,12 @@
         (k * observers + i, k * observers + (i ^ k)) for k in range(parties) for i in range(observers)
     ]
     sent = lax.dynamic_slice_in_dim(head_logits[0], start, layers, 0)
-    values = lax.ppermute(sent, ("dp", "mp"), pairs).reshape(1, -1)
+    return lax.ppermute(sent, ("dp", "mp"), pairs).reshape(1, -1)
+
+
+def gram_rows(values):
+    parties = lax.axis_size("dp")
+    dp = lax.axis_index("dp")
     high = lax.reduce_precision(values, 8, 7)
     middle = lax.reduce_precision(values - high, 8, 7)
     rest = values - high - middle
@@ -430,67 +467,86 @@
     new_moments, advance, mine, theirs, far_mine, far_theirs, own = grams(
         gradients.reshape(stacked), moments.reshape(stacked)
     )
-    rows = observed_rows(head_logits, layers)
-    both_rows = wide(rows) + wide(swap(rows))
     far_arrived, arrived = swap(far_theirs), swap(theirs)
-
-    def behind(value, start):
-        return jnp.pad(value, ((start, 0), (0, 0)))
-
-    rows_first = behind(jnp.where(core == 0, 0.0, both_rows), SQUARES - GRAM_HALF)
-    rows_second = behind(jnp.where(core == 0, both_rows, 0.0), SQUARES - GRAM_HALF)
 
     def first_half(distance):
         slot = 3 - distance
-        return wide(mine[slot, :GRAM_HALF]) + wide(arrived[slot, :GRAM_HALF]) + rows_first
+        return wide(mine[slot, :GRAM_HALF]) + wide(arrived[slot, :GRAM_HALF])
 
     def second_half(distance):
         slot = 3 - distance
-        return wide(mine[slot, GRAM_HALF:]) + wide(arrived[slot, GRAM_HALF:]) + rows_second
+        return wide(mine[slot, GRAM_HALF:]) + wide(arrived[slot, GRAM_HALF:])
+
+    def in_first(rows):
+        rows = jnp.where(core == 0, 0.0, wide(rows))
+        return jnp.pad(rows, ((SQUARES - GRAM_HALF, 0), (0, 0)))
+
+    def in_second(rows):
+        rows = jnp.where(core == 0, wide(rows), 0.0)
+        return jnp.pad(rows, ((SQUARES - GRAM_HALF, 0), (0, 0)))
 
     def hop(value):
         return wide(onward(low(value), 1))
 
-    far = low(wide(far_mine) + wide(far_arrived) + rows_first)
+    far = low(wide(far_mine) + wide(far_arrived))
     firsts = [first_half(distance) for distance in (3, 2, 1)]
     seconds = [second_half(distance) for distance in (3, 2, 1)]
     firsts[0], seconds[0] = low(firsts[0]), low(seconds[0])
-    far, firsts, seconds = lax.optimization_barrier((far, firsts, seconds))
+    far, firsts, seconds, head_logits = lax.optimization_barrier(
+        (far, firsts, seconds, head_logits)
+    )
+    values = observed(head_logits, layers)
     far = wide(onward(far, 2))
     first, second = wide(onward(firsts[0], 1)), wide(onward(seconds[0], 1))
-    first, second = hop(firsts[1] + first + far), hop(seconds[1] + second)
-    first, second = hop(firsts[2] + first), hop(seconds[2] + second)
-    own_rows = behind(wide(rows), SQUARES - GRAM_HALF)
-    first = first + wide(own[:GRAM_HALF]) + jnp.where(core == 0, 0.0, own_rows)
-    second = second + wide(own[GRAM_HALF:]) + jnp.where(core == 0, own_rows, 0.0)
-    partial = low(jnp.concatenate([first, second], axis=0))
-
-    first, second, ratios = polynomial(place, partial, swap(partial))
-
-    def final(parts, results):
-        *results, after = finish(
-            place, ratios, advance, weights.reshape(stacked), parts, results
+    values, far, first, second = lax.optimization_barrier((values, far, first, second))
+    rows = gram_rows(values)
+    first, second = (
+        hop(firsts[1] + first + far + in_first(rows)),
+        hop(seconds[1] + second + in_second(rows)),
+    )
+    both_rows = lax.optimization_barrier(rows) + lax.optimization_barrier(swap(rows))
+    first, second = (
+        hop(firsts[2] + first + in_first(both_rows)),
+        hop(seconds[2] + second + in_second(both_rows)),
+    )
+    second = low(second + wide(own[GRAM_HALF:]) + in_second(rows))
+    first = low(first + wide(own[:GRAM_HALF]) + in_first(rows))
+    first, second = polynomial(place, (first, second), (swap(first), swap(second)))
+
+    def final(peaks, parts, results):
+        *results, peaks, after = finish(
+            place, peaks, advance, weights.reshape(stacked), parts, results
         )
-        return results, after
-
-    results, begun = final([((first, second), 0, True)], None)
-    parts = []
+        return results, peaks, after
+
+    pieces = [(first, second)]
     for distance in (1, 2, 3):
         first, second = onward(first, 1), onward(second, 1)
         if distance == 2:
             far = onward(first, 2)
-        parts.append((first, second))
-
-    def both_ways(halves, distance, before):
-        other = swap(jnp.concatenate(halves, axis=0) + before)
-        return [(halves, distance, True), ((other,), distance, False)]
-
-    results, after = final(
-        both_ways(parts[0], 1, begun) + both_ways(parts[1], 2, begun), results
-    )
-    far = far + after
-    (new_weights, updates), _ = final(
-        both_ways(parts[2], 3, after) + [((far, swap(far)), 4, True)], results
+        pieces.append((first, second))
+    near = [half for halves in pieces[1:3] for half in halves]
+    other_near = swap(jnp.concatenate(near, axis=0))
+    results, peaks, after = final(
+        None,
+        [
+            ([(half, 0) for half in pieces[0]], 0, True),
+            ([(half, 0) for half in pieces[1]], 1, True),
+            ([(other_near, 0), (other_near, HALF)], 1, False),
+            ([(half, 0) for half in pieces[2]], 2, True),
+            ([(other_near, 2 * HALF), (other_near, 3 * HALF)], 2, False),
+        ],
+        None,
+    )
+    other_remote = swap(jnp.concatenate([*pieces[3], far], axis=0) + after)
+    (new_weights, updates), _, _ = final(
+        peaks,
+        [
+            ([(half, 0) for half in pieces[3]], 3, True),
+            ([(other_remote, 0), (other_remote, HALF)], 3, False),
+            ([(far, 0), (other_remote, 2 * HALF)], 4, True),
+        ],
+        results,
     )
     whole = gradients.shape
     return (new_weights.reshape(whole), new_moments.reshape(whole), updates.reshape(whole))

time: 82.3 us -> 74.9 us (0.910)
  starting transfers between devices: 48.7 us -> 37.7 us
  waiting for transfers between devices: 12.2 us -> 17.6 us
  Pallas kernels: 18.5 us -> 17.5 us
    ppermute x14, starting transfers between devices: 28.9 us -> 21.5 us  [onward(): return lax.ppermute(value, 'dp', pairs)]
    ppermute x14, waiting for transfers between devices: 8.51 us -> 11.8 us  [onward(): return lax.ppermute(value, 'dp', pairs)]
    ppermute x8 -> x7, starting transfers between devices: 15.7 us -> 12.9 us  [swap(): return lax.ppermute(value, 'dp', swap_pairs)]
    ppermute x1, waiting for transfers between devices: 0.01 us -> 1.4 us  [observed(): return lax.ppermute(sent, ('dp', 'mp'), pairs).reshape(1, -1)]
    pallas_call x3 -> x2, Pallas kernels: 8.66 us -> 7.72 us  [finish(): pl.pallas_call(kernel, out_shape=(shape, shape, jax.ShapeDtypeStruct((1,...]
    ppermute x1, starting transfers between devices: 4.03 us -> 3.2 us  [observed(): return lax.ppermute(sent, ('dp', 'mp'), pairs).reshape(1, -1)]
    ppermute x8 -> x7, waiting for transfers between devices: 3.67 us -> 4.45 us  [swap(): return lax.ppermute(value, 'dp', swap_pairs)]
  transfers between devices with their start and end apart: 23 -> 22, of which waited for: 11 -> 14; matrix products, arithmetic and copies ran while one was open for 1% -> 1% of each run, Pallas kernels for 14% -> 6%
where the time goes in v3:
time: 74.9 us; the launch traced here: 74.8 us
  starting transfers between devices  37.7 us (50%)
  waiting for transfers between devices  17.6 us (23%)
  Pallas kernels  17.5 us (23%)
  other arithmetic  0.93 us (1%)
  between operations  0.81 us (1%)
    ppermute x14, starting transfers between devices, onward(): return lax.ppermute(value, 'dp', pairs)  21.5 us
    ppermute x7, starting transfers between devices, swap(): return lax.ppermute(value, 'dp', swap_pairs)  12.9 us
    ppermute x14, waiting for transfers between devices, onward(): return lax.ppermute(value, 'dp', pairs)  11.8 us
    pallas_call x2, Pallas kernels, finish(): pl.pallas_call(kernel, out_shape=(shape, shape, jax.ShapeDtypeStruct((1,...  7.72 us
    pallas_call x1, Pallas kernels, grams(): pl.pallas_call(gram_kernel, out_shape=(full, full, shape(3, GRAM_ROWS, SI...  5.69 us
    ppermute x7, waiting for transfers between devices, swap(): return lax.ppermute(value, 'dp', swap_pairs)  4.45 us
    pallas_call x1, Pallas kernels, polynomial(): pl.pallas_call(polynomial_kernel, out_shape=(half, half), in_specs=[pl.Bl...  4.12 us
    ppermute x1, starting transfers between devices, observed(): return lax.ppermute(sent, ('dp', 'mp'), pairs).reshape(1, -1)  3.2 us
  transfers between devices with their start and end apart: 22, of which 14 were waited for; matrix products, arithmetic and copies ran while one was open for 1% of the time, Pallas kernels for 6%

profile of v3, /device:TPU:1, one launch (start us, length us, event | category | flops | bytes accessed | tf_op | source)
XLA Modules:
  0.0 74.8 jit_solution(1888961921233193928)
XLA Ops:
  0.6 5.7 %shard_map.67 = (bf16[8,256,512]{2,1,0:T(8,128)(2,1)}, bf16[8,256,512]{2,1,0:T(8,128)(2,1)}, bf16[3,1088,128]{2,1,0:T(8,128)(2,1)S(1)}, bf16[3,1088,128]{2,1,0:T...) custom-call(bf16[8,256,512]{2,1,0:T(8,128)(2,1)} %bitcast.31, ...), custom_call_target="tpu_custom_call" | custom-call | flops 1073741824 | bytes 10485760 | tf_op jit(solution)/shard_map/pallas_call | solution.py:211
  6.3 3.3 %collective-permute-start.1 = (bf16[3,1088,128]{2,1,0:T(8,128)(2,1)S(1)}, bf16[3,1088,128]{2,1,0:T(8,128)(2,1)S(1)}, u32[]{:S(2)}, u32[]{:S(2)}) collective-permute-start(bf16[3,1088,128]{2,1,0:T(8,128)(2,1)S(1)} %get-tuple-element.34), channel_id=1, source_target_pairs={{0,16},{16,0},{32,48},{48,32},{64,80},{80,64},{96,112},{112,96},{1... | collective-permute-start | bytes 2506760 | tf_op jit(solution)/shard_map/ppermute | solution.py:461
  9.7 0.1 collective-permute-start
  9.8 2.1 %collective-permute-done = bf16[544,128]{1,0:T(8,128)(2,1)S(1)} collective-permute-done((bf16[544,128]{1,0:T(8,128)(2,1)S(1)}, bf16[544,128]{1,0:T(8,128)(2,1)S(1)}, u32[]{:S(2)}, u32[]{:S(2)}) %collective-permute-start) | collective-permute-done | bytes 139296 | tf_op jit(solution)/shard_map/ppermute | solution.py:461
  11.9 0.2 add_bitcast_fusion
  12.1 4.4 %collective-permute-start.3 = (bf16[544,128]{1,0:T(8,128)(2,1)S(1)}, bf16[544,128]{1,0:T(8,128)(2,1)S(1)}, u32[]{:S(2)}, u32[]{:S(2)}) collective-permute-start(bf16[544,128]{1,0:T(8,128)(2,1)S(1)} %add_convert_fusion.4), channel_id=1, source_target_pairs={{0,64},{16,208},{32,96},{48,240},{64,128},{80,16},{96,160},{112,48... | collective-permute-start | bytes 417800 | tf_op jit(solution)/shard_map/ppermute | solution.py:465
  16.5 0.7 collective-permute-start.4
  17.2 0.7 collective-permute-start.5
  17.9 0.1 constant_dynamic-slice_fusion
  18.0 0.1 copy.9
  18.1 3.2 %collective-permute-start.2 = (f32[4,32]{1,0:T(4,128)S(1)}, f32[4,32]{1,0:T(4,128)S(1)}, u32[]{:S(2)}, u32[]{:S(2)}) collective-permute-start(f32[4,32]{1,0:T(4,128)S(1)} %bitcast.35), channel_id=1, source_target_pairs={{0,0},{1,1},{2,2},{3,3},{4,4},{5,5},{6,6},{7,7},{8,8},{9,9},{10,10... | collective-permute-start | bytes 1544 | tf_op jit(solution)/shard_map/ppermute | solution.py:434
  21.3 1.4 %collective-permute-done.2 = f32[4,32]{1,0:T(4,128)S(1)} collective-permute-done((f32[4,32]{1,0:T(4,128)S(1)}, f32[4,32]{1,0:T(4,128)S(1)}, u32[]{:S(2)}, u32[]{:S(2)}) %collective-permute-start.2) | collective-permute-done | bytes 544 | tf_op jit(solution)/shard_map/ppermute | solution.py:434
  22.7 0.1 reshape.115
  22.9 0.4 collective-permute-done.5
  23.3 0.1 select_convert_fusion
  23.4 1.0 %collective-permute-start.7 = (bf16[64,128]{1,0:T(8,128)(2,1)S(1)}, bf16[64,128]{1,0:T(8,128)(2,1)S(1)}, u32[]{:S(2)}, u32[]{:S(2)}) collective-permute-start(bf16[64,128]{1,0:T(8,128)(2,1)S(1)} %select_convert_fusion), channel_id=1, source_target_pairs={{0,16},{16,0},{32,48},{48,32},{64,80},{80,64},{96,112},{112,96},{1... | collective-permute-start | bytes 49160 | tf_op jit(solution)/shard_map/ppermute | solution.py:461
  24.4 0.1 convert_select_fusion.2
  24.5 4.3 %collective-permute-start.9 = (bf16[544,128]{1,0:T(8,128)(2,1)S(1)}, bf16[544,128]{1,0:T(8,128)(2,1)S(1)}, u32[]{:S(2)}, u32[]{:S(2)}) collective-permute-start(bf16[544,128]{1,0:T(8,128)(2,1)S(1)} %fusion.2), channel_id=1, source_target_pairs={{0,32},{16,240},{32,64},{48,16},{64,96},{80,48},{96,128},{112,80},... | collective-permute-start | bytes 417800 | tf_op jit(solution)/shard_map/ppermute | solution.py:465
  28.9 0.1 collective-permute-start.6
  29.0 1.9 %collective-permute-done.9 = bf16[544,128]{1,0:T(8,128)(2,1)S(1)} collective-permute-done((bf16[544,128]{1,0:T(8,128)(2,1)S(1)}, bf16[544,128]{1,0:T(8,128)(2,1)S(1)}, u32[]{:S(2)}, u32[]{:S(2)}) %collective-permute-start.9) | collective-permute-done | bytes 139296 | tf_op jit(solution)/shard_map/ppermute | solution.py:465
  30.9 3.2 %collective-permute-start.10 = (bf16[544,128]{1,0:T(8,128)(2,1)S(1)}, bf16[544,128]{1,0:T(8,128)(2,1)S(1)}, u32[]{:S(2)}, u32[]{:S(2)}) collective-permute-start(bf16[544,128]{1,0:T(8,128)(2,1)S(1)} %add_convert_fusion), channel_id=1, source_target_pairs={{0,32},{16,240},{32,64},{48,16},{64,96},{80,48},{96,128},{112,80},... | collective-permute-start | bytes 417800 | tf_op jit(solution)/shard_map/ppermute | solution.py:465
  34.1 1.5 %collective-permute-start.8 = (bf16[544,128]{1,0:T(8,128)(2,1)S(1)}, bf16[544,128]{1,0:T(8,128)(2,1)S(1)}, u32[]{:S(2)}, u32[]{:S(2)}) collective-permute-start(bf16[544,128]{1,0:T(8,128)(2,1)S(1)} %add_convert_fusion.1), channel_id=1, source_target_pairs={{0,32},{16,240},{32,64},{48,16},{64,96},{80,48},{96,128},{112,80},... | collective-permute-start | bytes 417800 | tf_op jit(solution)/shard_map/ppermute | solution.py:465
  35.5 0.5 collective-permute-done.10
  36.1 2.1 %collective-permute-done.8 = bf16[544,128]{1,0:T(8,128)(2,1)S(1)} collective-permute-done((bf16[544,128]{1,0:T(8,128)(2,1)S(1)}, bf16[544,128]{1,0:T(8,128)(2,1)S(1)}, u32[]{:S(2)}, u32[]{:S(2)}) %collective-permute-start.8) | collective-permute-done | bytes 139296 | tf_op jit(solution)/shard_map/ppermute | solution.py:465
  38.1 0.1 fusion.3
  38.2 2.6 %collective-permute-start.12 = (bf16[544,128]{1,0:T(8,128)(2,1)S(1)}, bf16[544,128]{1,0:T(8,128)(2,1)S(1)}, u32[]{:S(2)}, u32[]{:S(2)}) collective-permute-start(bf16[544,128]{1,0:T(8,128)(2,1)S(1)} %get-tuple-element.63.mine_second), channel_id=1, source_target_pairs={{0,16},{16,0},{32,48},{48,32},{64,80},{80,64},{96,112},{112,96},{1... | collective-permute-start | bytes 417800 | tf_op jit(solution)/shard_map/ppermute | solution.py:461
  40.9 0.3 collective-permute-start.11
  41.2 0.1 pad_add_fusion.4.place_ref
  41.2 0.6 collective-permute-done.12.theirs_second
  41.9 0.4 collective-permute-done.11.theirs_first
  42.2 4.1 %shard_map.68 = (bf16[528,128]{1,0:T(8,128)(2,1)S(1)}, bf16[528,128]{1,0:T(8,128)(2,1)S(1)}) custom-call(s32[2]{0:T(128)S(1)} %pad_add_fusion.4.place_ref, bf16[544,128]{1,0:T(8,128)(2,1)S(1)} %get-tuple-element.64.mine_first, bf16[544,128]{1,0:T(8,128)(2,1)S(1)} %get-tuple-element.63.mine_second, bf16[544,128]{1,0:T(8,128)(2,1)S(1)} %collective-permute-done.11.theirs_first, ...), custom_call_target="tpu_custom_call" | custom-call | flops 2415919104 | bytes 811008 | tf_op jit(solution)/shard_map/pallas_call | solution.py:286
  46.4 0.3 collective-permute-start.13
  46.7 0.1 collective-permute-start.14
  46.8 3.5 %collective-permute-done.13.refs_2_ = bf16[528,128]{1,0:T(8,128)(2,1)S(1)} collective-permute-done((bf16[528,128]{1,0:T(8,128)(2,1)S(1)}, bf16[528,128]{1,0:T(8,128)(2,1)S(1)}, u32[]{:S(2)}, u32[]{:S(2)}) %collective-permute-start.13) | collective-permute-done | bytes 135200 | tf_op jit(solution)/shard_map/ppermute | solution.py:465
  50.3 1.5 %collective-permute-start.15 = (bf16[528,128]{1,0:T(8,128)(2,1)S(1)}, bf16[528,128]{1,0:T(8,128)(2,1)S(1)}, u32[]{:S(2)}, u32[]{:S(2)}) collective-permute-start(bf16[528,128]{1,0:T(8,128)(2,1)S(1)} %collective-permute-done.13.refs_2_), channel_id=1, source_target_pairs={{0,32},{16,240},{32,64},{48,16},{64,96},{80,48},{96,128},{112,80},... | collective-permute-start | bytes 405512 | tf_op jit(solution)/shard_map/ppermute | solution.py:465
  51.8 0.3 collective-permute-done.14.refs_3_
  52.0 1.2 %collective-permute-start.16 = (bf16[528,128]{1,0:T(8,128)(2,1)S(1)}, bf16[528,128]{1,0:T(8,128)(2,1)S(1)}, u32[]{:S(2)}, u32[]{:S(2)}) collective-permute-start(bf16[528,128]{1,0:T(8,128)(2,1)S(1)} %collective-permute-done.14.refs_3_), channel_id=1, source_target_pairs={{0,32},{16,240},{32,64},{48,16},{64,96},{80,48},{96,128},{112,80},... | collective-permute-start | bytes 405512 | tf_op jit(solution)/shard_map/ppermute | solution.py:465
  53.2 1.0 %collective-permute-done.15.refs_5_ = bf16[528,128]{1,0:T(8,128)(2,1)S(1)} collective-permute-done((bf16[528,128]{1,0:T(8,128)(2,1)S(1)}, bf16[528,128]{1,0:T(8,128)(2,1)S(1)}, u32[]{:S(2)}, u32[]{:S(2)}) %collective-permute-start.15) | collective-permute-done | bytes 135200 | tf_op jit(solution)/shard_map/ppermute | solution.py:465
  54.2 1.7 %collective-permute-done.16.refs_6_ = bf16[528,128]{1,0:T(8,128)(2,1)S(1)} collective-permute-done((bf16[528,128]{1,0:T(8,128)(2,1)S(1)}, bf16[528,128]{1,0:T(8,128)(2,1)S(1)}, u32[]{:S(2)}, u32[]{:S(2)}) %collective-permute-start.16) | collective-permute-done | bytes 135200 | tf_op jit(solution)/shard_map/ppermute | solution.py:465
  55.9 4.8 %collective-permute-start.17 = (bf16[2112,128]{1,0:T(8,128)(2,1)S(1)}, bf16[2112,128]{1,0:T(8,128)(2,1)S(1)}, u32[]{:S(2)}, u32[]{:S(2)}) collective-permute-start(bf16[2112,128]{1,0:T(8,128)(2,1)S(1)} %pad_maximum_fusion), channel_id=1, source_target_pairs={{0,16},{16,0},{32,48},{48,32},{64,80},{80,64},{96,112},{112,96},{1... | collective-permute-start | bytes 1622024 | tf_op jit(solution)/shard_map/ppermute | solution.py:461
  60.7 0.7 collective-permute-start.18
  61.5 3.0 %collective-permute-start.19 = (bf16[528,128]{1,0:T(8,128)(2,1)S(1)}, bf16[528,128]{1,0:T(8,128)(2,1)S(1)}, u32[]{:S(2)}, u32[]{:S(2)}) collective-permute-start(bf16[528,128]{1,0:T(8,128)(2,1)S(1)} %collective-permute-done.16.refs_6_), channel_id=1, source_target_pairs={{0,32},{16,240},{32,64},{48,16},{64,96},{80,48},{96,128},{112,80},... | collective-permute-start | bytes 405512 | tf_op jit(solution)/shard_map/ppermute | solution.py:465
  64.4 4.5 %shard_map.69 = (bf16[8,256,512]{2,1,0:T(8,128)(2,1)}, bf16[8,256,512]{2,1,0:T(8,128)(2,1)}, f32[1,128]{1,0:T(1,128)S(1)}, bf16[1,128]{1,0:T(2,128)(2,1)S(1)}) custom-call(s32[2]{0:T(128)S(1)} %pad_add_fusion.4.place_ref, f32[1,128]{1,0:T(1,128)S(1)} %broadcast_in_dim.69.peaks_ref, bf16[8,256,512]{2,1,0:T(8,128)(2,1)S(1)} %copy-done.2, ...), custom_call_target="tpu_custom_call" | custom-call | flops 671088640 | bytes 6594560 | tf_op jit(solution)/shard_map/pallas_call | solution.py:392
  69.0 0.3 collective-permute-done.19.refs_1_
  69.3 0.1 maximum_add_fusion
  69.4 0.8 %collective-permute-start.21 = (bf16[1584,128]{1,0:T(8,128)(2,1)S(1)}, bf16[1584,128]{1,0:T(8,128)(2,1)S(1)}, u32[]{:S(2)}, u32[]{:S(2)}) collective-permute-start(bf16[1584,128]{1,0:T(8,128)(2,1)S(1)} %maximum_add_fusion), channel_id=1, source_target_pairs={{0,16},{16,0},{32,48},{48,32},{64,80},{80,64},{96,112},{112,96},{1... | collective-permute-start | bytes 1216520 | tf_op jit(solution)/shard_map/ppermute | solution.py:461
  70.2 1.4 %collective-permute-done.21.refs_2_ = bf16[1584,128]{1,0:T(8,128)(2,1)S(1)} collective-permute-done((bf16[1584,128]{1,0:T(8,128)(2,1)S(1)}, bf16[1584,128]{1,0:T(8,128)(2,1)S(1)}, u32[]{:S(2)}, u32[]{:S(2)}) %collective-permute-start.21) | collective-permute-done | bytes 405536 | tf_op jit(solution)/shard_map/ppermute | solution.py:461
  71.6 3.2 %shard_map.70 = (bf16[8,256,512]{2,1,0:T(8,128)(2,1)}, bf16[8,256,512]{2,1,0:T(8,128)(2,1)}, f32[1,128]{1,0:T(1,128)}, bf16[1,128]{1,0:T(2,128)(2,1)}) custom-call(s32[2]{0:T(128)S(1)} %pad_add_fusion.4.place_ref, f32[1,128]{1,0:T(1,128)S(1)} %get-tuple-element.50.peaks_ref, ...), custom_call_target="tpu_custom_call", output_to_operand_aliasing={{0}: (8, {}), {1}: (9, {})} | custom-call | flops 402653184 | bytes 3956736 | tf_op jit(solution)/shard_map/pallas_call | solution.py:392
  (29 shorter events, 0.4 us)
Async XLA Ops:
  0.6 17.3 %copy-start = (f32[1,64,32]{1,2,0:T(8,128)S(1)}, f32[1,64,32]{1,2,0:T(8,128)}, u32[]{:S(2)}) copy-start(f32[1,64,32]{1,2,0:T(8,128)} %param.7) | copy-start | bytes 24580
  6.3 5.6 %collective-permute-start.1 = (bf16[3,1088,128]{2,1,0:T(8,128)(2,1)S(1)}, bf16[3,1088,128]{2,1,0:T(8,128)(2,1)S(1)}, u32[]{:S(2)}, u32[]{:S(2)}) collective-permute-start(bf16[3,1088,128]{2,1,0:T(8,128)(2,1)S(1)} %get-tuple-element.34), channel_id=1, source_target_pairs={{0,16},{16,0},{32,48},{48,32},{64,80},{80,64},{96,112},{112,96},{1... | collective-permute-start | bytes 2506760 | tf_op jit(solution)/shard_map/ppermute | solution.py:461
  9.7 2.2 %collective-permute-start = (bf16[544,128]{1,0:T(8,128)(2,1)S(1)}, bf16[544,128]{1,0:T(8,128)(2,1)S(1)}, u32[]{:S(2)}, u32[]{:S(2)}) collective-permute-start(bf16[544,128]{1,0:T(8,128)(2,1)S(1)} %get-tuple-element.32), channel_id=1, source_target_pairs={{0,16},{16,0},{32,48},{48,32},{64,80},{80,64},{96,112},{112,96},{1... | collective-permute-start | bytes 417800 | tf_op jit(solution)/shard_map/ppermute | solution.py:461
  12.1 10.7 %collective-permute-start.3 = (bf16[544,128]{1,0:T(8,128)(2,1)S(1)}, bf16[544,128]{1,0:T(8,128)(2,1)S(1)}, u32[]{:S(2)}, u32[]{:S(2)}) collective-permute-start(bf16[544,128]{1,0:T(8,128)(2,1)S(1)} %add_convert_fusion.4), channel_id=1, source_target_pairs={{0,64},{16,208},{32,96},{48,240},{64,128},{80,16},{96,160},{112,48... | collective-permute-start | bytes 417800 | tf_op jit(solution)/shard_map/ppermute | solution.py:465
  16.5 6.4 %collective-permute-start.4 = (bf16[544,128]{1,0:T(8,128)(2,1)S(1)}, bf16[544,128]{1,0:T(8,128)(2,1)S(1)}, u32[]{:S(2)}, u32[]{:S(2)}) collective-permute-start(bf16[544,128]{1,0:T(8,128)(2,1)S(1)} %get-tuple-element.39), channel_id=1, source_target_pairs={{0,32},{16,240},{32,64},{48,16},{64,96},{80,48},{96,128},{112,80},... | collective-permute-start | bytes 417800 | tf_op jit(solution)/shard_map/ppermute | solution.py:465
  17.2 6.1 %collective-permute-start.5 = (bf16[544,128]{1,0:T(8,128)(2,1)S(1)}, bf16[544,128]{1,0:T(8,128)(2,1)S(1)}, u32[]{:S(2)}, u32[]{:S(2)}) collective-permute-start(bf16[544,128]{1,0:T(8,128)(2,1)S(1)} %get-tuple-element.40), channel_id=1, source_target_pairs={{0,32},{16,240},{32,64},{48,16},{64,96},{80,48},{96,128},{112,80},... | collective-permute-start | bytes 417800 | tf_op jit(solution)/shard_map/ppermute | solution.py:465
  18.1 4.6 %collective-permute-start.2 = (f32[4,32]{1,0:T(4,128)S(1)}, f32[4,32]{1,0:T(4,128)S(1)}, u32[]{:S(2)}, u32[]{:S(2)}) collective-permute-start(f32[4,32]{1,0:T(4,128)S(1)} %bitcast.35), channel_id=1, source_target_pairs={{0,0},{1,1},{2,2},{3,3},{4,4},{5,5},{6,6},{7,7},{8,8},{9,9},{10,10... | collective-permute-start | bytes 1544 | tf_op jit(solution)/shard_map/ppermute | solution.py:434
  23.4 5.5 %collective-permute-start.7 = (bf16[64,128]{1,0:T(8,128)(2,1)S(1)}, bf16[64,128]{1,0:T(8,128)(2,1)S(1)}, u32[]{:S(2)}, u32[]{:S(2)}) collective-permute-start(bf16[64,128]{1,0:T(8,128)(2,1)S(1)} %select_convert_fusion), channel_id=1, source_target_pairs={{0,16},{16,0},{32,48},{48,32},{64,80},{80,64},{96,112},{112,96},{1... | collective-permute-start | bytes 49160 | tf_op jit(solution)/shard_map/ppermute | solution.py:461
  24.5 6.3 %collective-permute-start.9 = (bf16[544,128]{1,0:T(8,128)(2,1)S(1)}, bf16[544,128]{1,0:T(8,128)(2,1)S(1)}, u32[]{:S(2)}, u32[]{:S(2)}) collective-permute-start(bf16[544,128]{1,0:T(8,128)(2,1)S(1)} %fusion.2), channel_id=1, source_target_pairs={{0,32},{16,240},{32,64},{48,16},{64,96},{80,48},{96,128},{112,80},... | collective-permute-start | bytes 417800 | tf_op jit(solution)/shard_map/ppermute | solution.py:465
  28.9 5.2 %collective-permute-start.6 = (bf16[544,128]{1,0:T(8,128)(2,1)S(1)}, bf16[544,128]{1,0:T(8,128)(2,1)S(1)}, u32[]{:S(2)}, u32[]{:S(2)}) collective-permute-start(bf16[544,128]{1,0:T(8,128)(2,1)S(1)} %fusion), channel_id=1, source_target_pairs={{0,32},{16,240},{32,64},{48,16},{64,96},{80,48},{96,128},{112,80},... | collective-permute-start | bytes 417800 | tf_op jit(solution)/shard_map/ppermute | solution.py:465
  30.9 5.2 %collective-permute-start.10 = (bf16[544,128]{1,0:T(8,128)(2,1)S(1)}, bf16[544,128]{1,0:T(8,128)(2,1)S(1)}, u32[]{:S(2)}, u32[]{:S(2)}) collective-permute-start(bf16[544,128]{1,0:T(8,128)(2,1)S(1)} %add_convert_fusion), channel_id=1, source_target_pairs={{0,32},{16,240},{32,64},{48,16},{64,96},{80,48},{96,128},{112,80},... | collective-permute-start | bytes 417800 | tf_op jit(solution)/shard_map/ppermute | solution.py:465
  34.1 4.0 %collective-permute-start.8 = (bf16[544,128]{1,0:T(8,128)(2,1)S(1)}, bf16[544,128]{1,0:T(8,128)(2,1)S(1)}, u32[]{:S(2)}, u32[]{:S(2)}) collective-permute-start(bf16[544,128]{1,0:T(8,128)(2,1)S(1)} %add_convert_fusion.1), channel_id=1, source_target_pairs={{0,32},{16,240},{32,64},{48,16},{64,96},{80,48},{96,128},{112,80},... | collective-permute-start | bytes 417800 | tf_op jit(solution)/shard_map/ppermute | solution.py:465
  38.2 3.6 %collective-permute-start.12 = (bf16[544,128]{1,0:T(8,128)(2,1)S(1)}, bf16[544,128]{1,0:T(8,128)(2,1)S(1)}, u32[]{:S(2)}, u32[]{:S(2)}) collective-permute-start(bf16[544,128]{1,0:T(8,128)(2,1)S(1)} %get-tuple-element.63.mine_second), channel_id=1, source_target_pairs={{0,16},{16,0},{32,48},{48,32},{64,80},{80,64},{96,112},{112,96},{1... | collective-permute-start | bytes 417800 | tf_op jit(solution)/shard_map/ppermute | solution.py:461
  40.9 1.4 %collective-permute-start.11 = (bf16[544,128]{1,0:T(8,128)(2,1)S(1)}, bf16[544,128]{1,0:T(8,128)(2,1)S(1)}, u32[]{:S(2)}, u32[]{:S(2)}) collective-permute-start(bf16[544,128]{1,0:T(8,128)(2,1)S(1)} %get-tuple-element.64.mine_first), channel_id=1, source_target_pairs={{0,16},{16,0},{32,48},{48,32},{64,80},{80,64},{96,112},{112,96},{1... | collective-permute-start | bytes 417800 | tf_op jit(solution)/shard_map/ppermute | solution.py:461
  42.2 22.2 %copy-start.1 = (bf16[4,2,256,512]{3,2,1,0:T(8,128)(2,1)S(1)}, bf16[4,2,256,512]{3,2,1,0:T(8,128)(2,1)}, u32[]{:S(2)}) copy-start(bf16[4,2,256,512]{3,2,1,0:T(8,128)(2,1)} %param.6) | copy-start | bytes 6291460
  42.2 22.2 %copy-start.2 = (bf16[8,256,512]{2,1,0:T(8,128)(2,1)S(1)}, bf16[8,256,512]{2,1,0:T(8,128)(2,1)}, u32[]{:S(2)}) copy-start(bf16[8,256,512]{2,1,0:T(8,128)(2,1)} %get-tuple-element.30.advance_ref) | copy-start | bytes 6291460
  46.4 3.9 %collective-permute-start.13 = (bf16[528,128]{1,0:T(8,128)(2,1)S(1)}, bf16[528,128]{1,0:T(8,128)(2,1)S(1)}, u32[]{:S(2)}, u32[]{:S(2)}) collective-permute-start(bf16[528,128]{1,0:T(8,128)(2,1)S(1)} %get-tuple-element.48.refs_0_), channel_id=1, source_target_pairs={{0,32},{16,240},{32,64},{48,16},{64,96},{80,48},{96,128},{112,80},... | collective-permute-start | bytes 405512 | tf_op jit(solution)/shard_map/ppermute | solution.py:465
  46.7 5.4 %collective-permute-start.14 = (bf16[528,128]{1,0:T(8,128)(2,1)S(1)}, bf16[528,128]{1,0:T(8,128)(2,1)S(1)}, u32[]{:S(2)}, u32[]{:S(2)}) collective-permute-start(bf16[528,128]{1,0:T(8,128)(2,1)S(1)} %get-tuple-element.49.refs_1_), channel_id=1, source_target_pairs={{0,32},{16,240},{32,64},{48,16},{64,96},{80,48},{96,128},{112,80},... | collective-permute-start | bytes 405512 | tf_op jit(solution)/shard_map/ppermute | solution.py:465
  50.3 3.9 %collective-permute-start.15 = (bf16[528,128]{1,0:T(8,128)(2,1)S(1)}, bf16[528,128]{1,0:T(8,128)(2,1)S(1)}, u32[]{:S(2)}, u32[]{:S(2)}) collective-permute-start(bf16[528,128]{1,0:T(8,128)(2,1)S(1)} %collective-permute-done.13.refs_2_), channel_id=1, source_target_pairs={{0,32},{16,240},{32,64},{48,16},{64,96},{80,48},{96,128},{112,80},... | collective-permute-start | bytes 405512 | tf_op jit(solution)/shard_map/ppermute | solution.py:465
  52.0 3.9 %collective-permute-start.16 = (bf16[528,128]{1,0:T(8,128)(2,1)S(1)}, bf16[528,128]{1,0:T(8,128)(2,1)S(1)}, u32[]{:S(2)}, u32[]{:S(2)}) collective-permute-start(bf16[528,128]{1,0:T(8,128)(2,1)S(1)} %collective-permute-done.14.refs_3_), channel_id=1, source_target_pairs={{0,32},{16,240},{32,64},{48,16},{64,96},{80,48},{96,128},{112,80},... | collective-permute-start | bytes 405512 | tf_op jit(solution)/shard_map/ppermute | solution.py:465
  55.9 8.5 %collective-permute-start.17 = (bf16[2112,128]{1,0:T(8,128)(2,1)S(1)}, bf16[2112,128]{1,0:T(8,128)(2,1)S(1)}, u32[]{:S(2)}, u32[]{:S(2)}) collective-permute-start(bf16[2112,128]{1,0:T(8,128)(2,1)S(1)} %pad_maximum_fusion), channel_id=1, source_target_pairs={{0,16},{16,0},{32,48},{48,32},{64,80},{80,64},{96,112},{112,96},{1... | collective-permute-start | bytes 1622024 | tf_op jit(solution)/shard_map/ppermute | solution.py:461
  60.7 8.2 %collective-permute-start.20 = (bf16[528,128]{1,0:T(8,128)(2,1)S(1)}, bf16[528,128]{1,0:T(8,128)(2,1)S(1)}, u32[]{:S(2)}, u32[]{:S(2)}) collective-permute-start(bf16[528,128]{1,0:T(8,128)(2,1)S(1)} %collective-permute-done.15.refs_5_), channel_id=1, source_target_pairs={{0,64},{16,208},{32,96},{48,240},{64,128},{80,16},{96,160},{112,48... | collective-permute-start | bytes 405512 | tf_op jit(solution)/shard_map/ppermute | solution.py:465
  60.7 8.2 %collective-permute-start.18 = (bf16[528,128]{1,0:T(8,128)(2,1)S(1)}, bf16[528,128]{1,0:T(8,128)(2,1)S(1)}, u32[]{:S(2)}, u32[]{:S(2)}) collective-permute-start(bf16[528,128]{1,0:T(8,128)(2,1)S(1)} %collective-permute-done.15.refs_5_), channel_id=1, source_target_pairs={{0,32},{16,240},{32,64},{48,16},{64,96},{80,48},{96,128},{112,80},... | collective-permute-start | bytes 405512 | tf_op jit(solution)/shard_map/ppermute | solution.py:465
  61.5 7.8 %collective-permute-start.19 = (bf16[528,128]{1,0:T(8,128)(2,1)S(1)}, bf16[528,128]{1,0:T(8,128)(2,1)S(1)}, u32[]{:S(2)}, u32[]{:S(2)}) collective-permute-start(bf16[528,128]{1,0:T(8,128)(2,1)S(1)} %collective-permute-done.16.refs_6_), channel_id=1, source_target_pairs={{0,32},{16,240},{32,64},{48,16},{64,96},{80,48},{96,128},{112,80},... | collective-permute-start | bytes 405512 | tf_op jit(solution)/shard_map/ppermute | solution.py:465
  69.4 2.2 %collective-permute-start.21 = (bf16[1584,128]{1,0:T(8,128)(2,1)S(1)}, bf16[1584,128]{1,0:T(8,128)(2,1)S(1)}, u32[]{:S(2)}, u32[]{:S(2)}) collective-permute-start(bf16[1584,128]{1,0:T(8,128)(2,1)S(1)} %maximum_add_fusion), channel_id=1, source_target_pairs={{0,16},{16,0},{32,48},{48,32},{64,80},{80,64},{96,112},{112,96},{1... | collective-permute-start | bytes 1216520 | tf_op jit(solution)/shard_map/ppermute | solution.py:461

commit v4 on v3

--- a/solution.py
+++ b/solution.py
@@ -1,3 +1,4 @@
+import functools
 import math
 
 import jax
@@ -117,12 +118,11 @@
     return 4 - (step + 1) // 2, (step % 2) == 1
 
 
-def gram_kernel(
-    grad_hbm, moment_hbm,
-    new_moment_hbm, advance_hbm, mine_hbm, theirs_hbm, far_mine_hbm, far_theirs_hbm, own_hbm,
-    grad_ref, moment_ref, new_moment_ref, advance_ref, packed_ref, in_sems, out_sems,
-):
-    matrices, rows, width = grad_ref.shape
+def gram_kernel(steps, matrices, grad_hbm, moment_hbm, *refs):
+    new_moment_hbm, advance_hbm, ours_hbm, theirs_hbm = refs[-11:-7]
+    grad_ref, moment_ref, new_moment_ref, advance_ref, packed_ref, in_sems, out_sems = refs[-7:]
+    own_hbm = ours_hbm.at[pl.ds(2 * GRAM_ROWS, GRAM_ROWS)] if steps[-1] == matrices - 1 else None
+    width = grad_ref.shape[2]
     dp = lax.axis_index("dp")
     chip, core = dp // 2, dp % 2
     middle = width // 2
@@ -133,35 +133,32 @@
         up = core == (0 if mine else 1)
         return lax.rem(chip + jnp.where(up, distance, matrices - distance), matrices)
 
-    def incoming(step, which):
+    def incoming(k, which):
         source, target = ((grad_hbm, grad_ref), (moment_hbm, moment_ref))[which]
         return pltpu.make_async_copy(
-            source.at[place_of(step)], target.at[step], in_sems.at[which, step]
+            source.at[place_of(steps[k])], target.at[k], in_sems.at[which, k]
         )
 
-    def outgoing(step, which):
+    def outgoing(k, which):
         source, target = ((new_moment_ref, new_moment_hbm), (advance_ref, advance_hbm))[which]
         return pltpu.make_async_copy(
-            source.at[step], target.at[place_of(step)], out_sems.at[which, step]
+            source.at[k], target.at[place_of(steps[k])], out_sems.at[which, k]
         )
 
-    def packed_copy(source, target, sem):
-        return pltpu.make_async_copy(source, target, sem)
-
-    for step in range(matrices):
-        incoming(step, 0).start()
-        incoming(step, 1).start()
+    for k in range(len(steps)):
+        incoming(k, 0).start()
+        incoming(k, 1).start()
     copies = []
-    for step in range(matrices):
-        incoming(step, 0).wait()
-        incoming(step, 1).wait()
-        widened = wide(grad_ref[step])
-        moment_sum = MOMENTUM * wide(moment_ref[step]) + widened
-        new_moment_ref[step] = low(moment_sum)
+    for k, step in enumerate(steps):
+        incoming(k, 0).wait()
+        incoming(k, 1).wait()
+        widened = wide(grad_ref[k])
+        moment_sum = MOMENTUM * wide(moment_ref[k]) + widened
+        new_moment_ref[k] = low(moment_sum)
         advance = low(widened + MOMENTUM * moment_sum)
-        advance_ref[step] = advance
+        advance_ref[k] = advance
         for which in range(2):
-            copies.append(outgoing(step, which))
+            copies.append(outgoing(k, which))
             copies[-1].start()
         upper = lax.dot_general(
             advance[:, :middle], advance, contract, preferred_element_type=jnp.float32
@@ -176,57 +173,62 @@
             for j in range(i, 2):
                 blocks[i + 2, j + 2] = lower[i * SIDE : (i + 1) * SIDE, j * SIDE : (j + 1) * SIDE]
         packed = pack(blocks, GRAM_ROWS)
-        mine = step in (0, matrices - 1) or carried(step)[1]
+        distance, mine = carried(step)
+        mine = mine or step == 0
         natural = core == (0 if mine else 1)
-        packed_ref[step, :GRAM_HALF] = jnp.where(natural, packed[:GRAM_HALF], packed[GRAM_HALF:])
-        packed_ref[step, GRAM_HALF:] = jnp.where(natural, packed[GRAM_HALF:], packed[:GRAM_HALF])
+        packed_ref[k, :GRAM_HALF] = jnp.where(natural, packed[:GRAM_HALF], packed[GRAM_HALF:])
+        packed_ref[k, GRAM_HALF:] = jnp.where(natural, packed[GRAM_HALF:], packed[:GRAM_HALF])
         if step == 0:
-            first, second = packed_ref.at[0, :GRAM_HALF], packed_ref.at[0, GRAM_HALF:]
-            copies.append(packed_copy(first, far_mine_hbm, out_sems.at[2, 0]))
+            moves = [
+                (packed_ref.at[k, :GRAM_HALF], ours_hbm.at[pl.ds(0, GRAM_HALF)]),
+                (packed_ref.at[k, GRAM_HALF:], theirs_hbm.at[pl.ds(0, GRAM_HALF)]),
+            ]
+        elif step == matrices - 1:
+            moves = [(packed_ref.at[k], own_hbm)]
+        else:
+            start = {3: GRAM_HALF, 2: 0, 1: GRAM_ROWS}[distance]
+            target = ours_hbm if mine else theirs_hbm
+            moves = [(packed_ref.at[k], target.at[pl.ds(start, GRAM_ROWS)])]
+        for i, (source, target) in enumerate(moves):
+            copies.append(pltpu.make_async_copy(source, target, out_sems.at[2 + i, k]))
             copies[-1].start()
-            copies.append(packed_copy(second, far_theirs_hbm, out_sems.at[3, 0]))
-            copies[-1].start()
-            continue
-        if step == matrices - 1:
-            target = own_hbm
-        elif mine:
-            target = mine_hbm.at[(step - 1) // 2]
-        else:
-            target = theirs_hbm.at[(step - 1) // 2]
-        copies.append(packed_copy(packed_ref.at[step], target, out_sems.at[2, step]))
-        copies[-1].start()
     for copy in copies:
         copy.wait()
 
 
-def grams(gradients, moments):
+def grams(gradients, moments, steps, earlier=None, before=None):
     matrices, rows, width = gradients.shape
-    there = pl.BlockSpec(memory_space=pltpu.HBM)
     anywhere = pl.BlockSpec(memory_space=pl.ANY)
-
-    def shape(*sizes):
-        return jax.ShapeDtypeStruct(sizes, jnp.bfloat16)
-
-    full = shape(*gradients.shape)
+    last = steps[-1] == matrices - 1
+    our_rows = 3 * GRAM_ROWS if last else GRAM_HALF + GRAM_ROWS
+    their_rows = 2 * GRAM_ROWS if last else GRAM_HALF + GRAM_ROWS
+    full = jax.ShapeDtypeStruct(gradients.shape, jnp.bfloat16)
+    some = pltpu.VMEM((len(steps), rows, width), jnp.bfloat16)
+    given = [] if earlier is None else [before, *earlier]
     return pl.pallas_call(
-        gram_kernel,
+        functools.partial(gram_kernel, steps, matrices),
         out_shape=(
-            full, full, shape(3, GRAM_ROWS, SIDE), shape(3, GRAM_ROWS, SIDE),
-            shape(GRAM_HALF, SIDE), shape(GRAM_HALF, SIDE), shape(GRAM_ROWS, SIDE),
-        ),
-        in_specs=[there, there],
-        out_specs=(there, there) + (anywhere,) * 5,
-        scratch_shapes=[pltpu.VMEM(gradients.shape, jnp.bfloat16)] * 4
+            full,
+            full,
+            jax.ShapeDtypeStruct((our_rows, SIDE), jnp.bfloat16),
+            jax.ShapeDtypeStruct((their_rows, SIDE), jnp.bfloat16),
+        ),
+        in_specs=[anywhere] * (2 + len(given)),
+        out_specs=(anywhere,) * 4,
+        input_output_aliases={3: 0, 4: 1} if given else {},
+        scratch_shapes=[some] * 4
         + [
-            pltpu.VMEM((matrices, GRAM_ROWS, SIDE), jnp.bfloat16),
-            pltpu.SemaphoreType.DMA((2, matrices)),
-            pltpu.SemaphoreType.DMA((4, matrices)),
+            pltpu.VMEM((len(steps), GRAM_ROWS, SIDE), jnp.bfloat16),
+            pltpu.SemaphoreType.DMA((2, len(steps))),
+            pltpu.SemaphoreType.DMA((4, len(steps))),
         ],
         compiler_params=pltpu.CompilerParams(vmem_limit_bytes=50 * MEBI),
         cost_estimate=pl.CostEstimate(
-            flops=2 * gradients.size * width, bytes_accessed=10 * gradients.size, transcendentals=0
-        ),
-    )(gradients, moments)
+            flops=2 * len(steps) * rows * width * width,
+            bytes_accessed=10 * len(steps) * rows * width,
+            transcendentals=0,
+        ),
+    )(gradients, moments, *given)
 
 
 def polynomial_kernel(
@@ -366,7 +368,7 @@
             factor = jnp.where(row // DK == k, ratio, factor)
         factor = jnp.where(which % 2 == 0, factor, 1.0)
         off = matrix_ref[:middle, middle:]
-        left, right = advance_ref[0, :, :middle], advance_ref[0, :, middle:]
+        left, right = advance_ref[which, :, :middle], advance_ref[which, :, middle:]
         halves = (
             jnp.dot(left, matrix_ref[:middle, :middle], preferred_element_type=jnp.float32)
             + lax.dot_general(
@@ -380,10 +382,11 @@
             rest = wide(matrix_ref[width : width + 1, columns])
             scaled = scaling * (halves[k] + wide(values) * rest)
             update_ref[0, :, columns] = low(scaled)
-            new_weight = (wide(weight_ref[0, :, columns]) * SHRINK - LEARN_RATE * scaled) * factor
+            new_weight = (wide(weight_ref[which, :, columns]) * SHRINK - LEARN_RATE * scaled) * factor
             new_weight_ref[0, :, columns] = low(new_weight)
 
     full = pl.BlockSpec((1, rows, width), lambda step, place: (index(step, place), 0, 0))
+    held = pl.BlockSpec(memory_space=pltpu.VMEM)
     one_row = pl.BlockSpec((1, SIDE), lambda step, place: (0, 0))
     anywhere = pl.BlockSpec(memory_space=pl.ANY)
     shape = jax.ShapeDtypeStruct(advance.shape, jnp.bfloat16)
@@ -400,7 +403,7 @@
         grid_spec=pltpu.PrefetchScalarGridSpec(
             num_scalar_prefetch=1,
             grid=(count,),
-            in_specs=[one_row, full, full]
+            in_specs=[one_row, held, held]
             + [pl.BlockSpec(half.shape, lambda step, place: (0, 0)) for half in pieces]
              + [anywhere] * len(carry),
             out_specs=(full, full, one_row, one_row),
@@ -464,18 +467,16 @@
         pairs = [(i, (i + 2 * distance * (1 - 2 * (i % 2))) % parties) for i in range(parties)]
         return lax.ppermute(value, "dp", pairs)
 
-    new_moments, advance, mine, theirs, far_mine, far_theirs, own = grams(
-        gradients.reshape(stacked), moments.reshape(stacked)
-    )
-    far_arrived, arrived = swap(far_theirs), swap(theirs)
-
-    def first_half(distance):
-        slot = 3 - distance
-        return wide(mine[slot, :GRAM_HALF]) + wide(arrived[slot, :GRAM_HALF])
-
-    def second_half(distance):
-        slot = 3 - distance
-        return wide(mine[slot, GRAM_HALF:]) + wide(arrived[slot, GRAM_HALF:])
+    gradients, moments = gradients.reshape(stacked), moments.reshape(stacked)
+    *earlier, ours, theirs = grams(gradients, moments, (0, 1, 2))
+    summed = wide(ours) + wide(swap(theirs))
+    far = low(summed[:GRAM_HALF])
+    first = low(summed[GRAM_HALF : 2 * GRAM_HALF])
+    second = low(summed[2 * GRAM_HALF :])
+    far, first, second, head_logits = lax.optimization_barrier((far, first, second, head_logits))
+    new_moments, advance, ours, theirs = grams(
+        gradients, moments, (3, 4, 5, 6, 7), earlier, far
+    )
 
     def in_first(rows):
         rows = jnp.where(core == 0, 0.0, wide(rows))
@@ -488,29 +489,26 @@
     def hop(value):
         return wide(onward(low(value), 1))
 
-    far = low(wide(far_mine) + wide(far_arrived))
-    firsts = [first_half(distance) for distance in (3, 2, 1)]
-    seconds = [second_half(distance) for distance in (3, 2, 1)]
-    firsts[0], seconds[0] = low(firsts[0]), low(seconds[0])
-    far, firsts, seconds, head_logits = lax.optimization_barrier(
-        (far, firsts, seconds, head_logits)
-    )
     values = observed(head_logits, layers)
     far = wide(onward(far, 2))
-    first, second = wide(onward(firsts[0], 1)), wide(onward(seconds[0], 1))
+    first, second = wide(onward(first, 1)), wide(onward(second, 1))
+    summed = wide(ours[: 2 * GRAM_ROWS]) + wide(swap(theirs))
+    own = wide(ours[2 * GRAM_ROWS :])
+    halves = [summed[k * GRAM_HALF : (k + 1) * GRAM_HALF] for k in range(4)]
+    halves = lax.optimization_barrier(halves)
     values, far, first, second = lax.optimization_barrier((values, far, first, second))
     rows = gram_rows(values)
     first, second = (
-        hop(firsts[1] + first + far + in_first(rows)),
-        hop(seconds[1] + second + in_second(rows)),
+        hop(halves[0] + first + far + in_first(rows)),
+        hop(halves[1] + second + in_second(rows)),
     )
     both_rows = lax.optimization_barrier(rows) + lax.optimization_barrier(swap(rows))
     first, second = (
-        hop(firsts[2] + first + in_first(both_rows)),
-        hop(seconds[2] + second + in_second(both_rows)),
-    )
-    second = low(second + wide(own[GRAM_HALF:]) + in_second(rows))
-    first = low(first + wide(own[:GRAM_HALF]) + in_first(rows))
+        hop(halves[2] + first + in_first(both_rows)),
+        hop(halves[3] + second + in_second(both_rows)),
+    )
+    second = low(second + own[GRAM_HALF:] + in_second(rows))
+    first = low(first + own[:GRAM_HALF] + in_first(rows))
     first, second = polynomial(place, (first, second), (swap(first), swap(second)))
 
     def final(peaks, parts, results):
@@ -539,16 +537,16 @@
         None,
     )
     other_remote = swap(jnp.concatenate([*pieces[3], far], axis=0) + after)
+    results, _, _ = final(peaks, [([(half, 0) for half in pieces[3]], 3, True)], results)
     (new_weights, updates), _, _ = final(
         peaks,
         [
-            ([(half, 0) for half in pieces[3]], 3, True),
             ([(other_remote, 0), (other_remote, HALF)], 3, False),
             ([(far, 0), (other_remote, 2 * HALF)], 4, True),
         ],
         results,
     )
-    whole = gradients.shape
+    whole = weights.shape
     return (new_weights.reshape(whole), new_moments.reshape(whole), updates.reshape(whole))
 
 

time: 74.9 us -> 79.5 us (1.061)
  waiting for transfers between devices: 17.6 us -> 14.7 us
  other arithmetic: 0.93 us -> 3.82 us
  Pallas kernels: 17.5 us -> 20.3 us
  starting transfers between devices: 37.7 us -> 39.3 us
    convert_element_type x3 -> x4, other arithmetic: 0.06 us -> 1.92 us  [wide(): return value.astype(jnp.float32)]
    pallas_call x1 -> x2, Pallas kernels: 5.69 us -> 7.51 us  [grams(): pl.pallas_call(functools.partial(gram_kernel, steps, matrices), out_shape...]
    ppermute x1, waiting for transfers between devices: 1.4 us -> 0.01 us  [observed(): return lax.ppermute(sent, ('dp', 'mp'), pairs).reshape(1, -1)]
    ppermute x7, waiting for transfers between devices: 4.45 us -> 3.3 us  [swap(): return lax.ppermute(value, 'dp', swap_pairs)]
    ppermute x7, starting transfers between devices: 12.9 us -> 14 us  [swap(): return lax.ppermute(value, 'dp', swap_pairs)]
    add x1, other arithmetic: 0.18 us -> 1.16 us  [shards(): summed = wide(ours[:2 * GRAM_ROWS]) + wide(swap(theirs))]
    pallas_call x2 -> x3, Pallas kernels: 7.72 us -> 8.66 us  [finish(): pl.pallas_call(kernel, out_shape=(shape, shape, jax.ShapeDtypeStruct((1,...]
  transfers between devices with their start and end apart: 22 -> 22, of which waited for: 14 -> 11; matrix products, arithmetic and copies ran while one was open for 1% -> 3% of each run, Pallas kernels for 6% -> 13%
where the time goes in v4:
time: 79.5 us; the launch traced here: 79.3 us
  starting transfers between devices  39.3 us (49%)
  Pallas kernels  20.3 us (26%)
  waiting for transfers between devices  14.7 us (18%)
  other arithmetic  3.82 us (5%)
  between operations  0.84 us (1%)
    ppermute x14, starting transfers between devices, onward(): return lax.ppermute(value, 'dp', pairs)  22.1 us
    ppermute x7, starting transfers between devices, swap(): return lax.ppermute(value, 'dp', swap_pairs)  14 us
    ppermute x14, waiting for transfers between devices, onward(): return lax.ppermute(value, 'dp', pairs)  11.4 us
    pallas_call x3, Pallas kernels, finish(): pl.pallas_call(kernel, out_shape=(shape, shape, jax.ShapeDtypeStruct((1,...  8.66 us
    pallas_call x2, Pallas kernels, grams(): pl.pallas_call(functools.partial(gram_kernel, steps, matrices), out_shape...  7.51 us
    pallas_call x1, Pallas kernels, polynomial(): pl.pallas_call(polynomial_kernel, out_shape=(half, half), in_specs=[pl.Bl...  4.12 us
    ppermute x7, waiting for transfers between devices, swap(): return lax.ppermute(value, 'dp', swap_pairs)  3.3 us
    ppermute x1, starting transfers between devices, observed(): return lax.ppermute(sent, ('dp', 'mp'), pairs).reshape(1, -1)  3.2 us
  transfers between devices with their start and end apart: 22, of which 11 were waited for; matrix products, arithmetic and copies ran while one was open for 3% of the time, Pallas kernels for 13%

profile of v4, /device:TPU:1, one launch (start us, length us, event | category | flops | bytes accessed | tf_op | source)
XLA Modules:
  0.0 79.3 jit_solution(7454469768666929720)
XLA Ops:
  0.6 3.4 %shard_map.67 = (bf16[8,256,512]{2,1,0:T(8,128)(2,1)}, bf16[8,256,512]{2,1,0:T(8,128)(2,1)S(1)}, bf16[1632,128]{1,0:T(8,128)(2,1)S(1)}, bf16[1632,128]{1,0:T(8,128)(2,1)S(1)}) custom-call(bf16[8,256,512]{2,1,0:T(8,128)(2,1)} %bitcast.20, bf16[8,256,512]{2,1,0:T(8,128)(2,1)} %bitcast.22), custom_call_target="tpu_custom_call" | custom-call | flops 402653184 | bytes 3932160 | tf_op jit(solution)/shard_map/pallas_call | solution.py:208
  4.0 3.3 %collective-permute-start = (bf16[1632,128]{1,0:T(8,128)(2,1)S(1)}, bf16[1632,128]{1,0:T(8,128)(2,1)S(1)}, u32[]{:S(2)}, u32[]{:S(2)}) collective-permute-start(bf16[1632,128]{1,0:T(8,128)(2,1)S(1)} %get-tuple-element.34), channel_id=1, source_target_pairs={{0,16},{16,0},{32,48},{48,32},{64,80},{80,64},{96,112},{112,96},{1... | collective-permute-start | bytes 1253384 | tf_op jit(solution)/shard_map/ppermute | solution.py:464
  7.3 1.4 %collective-permute-done = bf16[1632,128]{1,0:T(8,128)(2,1)S(1)} collective-permute-done((bf16[1632,128]{1,0:T(8,128)(2,1)S(1)}, bf16[1632,128]{1,0:T(8,128)(2,1)S(1)}, u32[]{:S(2)}, u32[]{:S(2)}) %collective-permute-start) | collective-permute-done | bytes 417824 | tf_op jit(solution)/shard_map/ppermute | solution.py:464
  8.7 0.1 add_convert_fusion
  8.9 4.4 %collective-permute-start.3 = (bf16[544,128]{1,0:T(8,128)(2,1)S(1)}, bf16[544,128]{1,0:T(8,128)(2,1)}, u32[]{:S(2)}, u32[]{:S(2)}) collective-permute-start(bf16[544,128]{1,0:T(8,128)(2,1)S(1)} %get-tuple-element.35.refs_0_), channel_id=1, source_target_pairs={{0,64},{16,208},{32,96},{48,240},{64,128},{80,16},{96,160},{112,48... | collective-permute-start | bytes 417800 | tf_op jit(solution)/shard_map/ppermute | solution.py:468
  13.2 0.7 collective-permute-start.4
  14.0 0.7 collective-permute-start.5
  14.8 0.1 copy.13
  14.8 3.2 %collective-permute-start.2 = (f32[4,32]{1,0:T(4,128)S(1)}, f32[4,32]{1,0:T(4,128)S(1)}, u32[]{:S(2)}, u32[]{:S(2)}) collective-permute-start(f32[4,32]{1,0:T(4,128)S(1)} %bitcast.27), channel_id=1, source_target_pairs={{0,0},{1,1},{2,2},{3,3},{4,4},{5,5},{6,6},{7,7},{8,8},{9,9},{10,10... | collective-permute-start | bytes 1544 | tf_op jit(solution)/shard_map/ppermute | solution.py:437
  18.1 4.2 %shard_map.68 = (bf16[8,256,512]{2,1,0:T(8,128)(2,1)}, bf16[8,256,512]{2,1,0:T(8,128)(2,1)S(1)}, bf16[3264,128]{1,0:T(8,128)(2,1)S(1)}, bf16[2176,128]{1,0:T(8,128)(2,1)}) custom-call(bf16[8,256,512]{2,1,0:T(8,128)(2,1)} %bitcast.21, bf16[8,256,512]{2,1,0:T(8,128)(2,1)} %bitcast.23, ...), custom_call_target="tpu_custom_call", output_to_operand_aliasing={{0}: (3, {}), {1}: (4, {})} | custom-call | flops 671088640 | bytes 6553600 | tf_op jit(solution)/shard_map/pallas_call | solution.py:208
  22.2 0.1 collective-permute-start.1
  22.3 0.1 reshape.96
  22.4 0.9 %convert_element_type.81 = f32[544,128]{1,0:T(8,128)S(1)} convert(bf16[544,128]{1,0:T(8,128)(2,1)} %collective-permute-done.3) | non-fusion elementwise | flops 69632 | bytes 417792 | tf_op jit(solution)/shard_map/convert_element_type | solution.py:35
  23.4 0.9 %convert_element_type.82 = f32[544,128]{1,0:T(8,128)S(1)} convert(bf16[544,128]{1,0:T(8,128)(2,1)} %collective-permute-done.4) | non-fusion elementwise | flops 69632 | bytes 417792 | tf_op jit(solution)/shard_map/convert_element_type | solution.py:35
  24.3 0.1 select_convert_fusion
  24.4 0.6 collective-permute-start.7
  25.0 0.1 convert_select_fusion.2
  25.1 0.7 collective-permute-done.7
  25.9 1.2 %convert_add_fusion = f32[2176,128]{1,0:T(8,128)S(1)} fusion(bf16[2176,128]{1,0:T(8,128)(2,1)} %collective-permute-done.1, bf16[3264,128]{1,0:T(8,128)(2,1)S(1)} %get-tuple-element.39), kind=kLoop, calls=%fused_computation | loop fusion | flops 835584 | bytes 2228224 | tf_op jit(solution)/shard_map/add | solution.py:495
  27.0 0.1 fusion.5
  27.2 5.0 %collective-permute-start.6 = (bf16[544,128]{1,0:T(8,128)(2,1)S(1)}, bf16[544,128]{1,0:T(8,128)(2,1)S(1)}, u32[]{:S(2)}, u32[]{:S(2)}) collective-permute-start(bf16[544,128]{1,0:T(8,128)(2,1)S(1)} %fusion), channel_id=1, source_target_pairs={{0,32},{16,240},{32,64},{48,16},{64,96},{80,48},{96,128},{112,80},... | collective-permute-start | bytes 417800 | tf_op jit(solution)/shard_map/ppermute | solution.py:468
  32.3 0.1 collective-permute-start.9
  32.4 1.9 %collective-permute-done.6 = bf16[544,128]{1,0:T(8,128)(2,1)S(1)} collective-permute-done((bf16[544,128]{1,0:T(8,128)(2,1)S(1)}, bf16[544,128]{1,0:T(8,128)(2,1)S(1)}, u32[]{:S(2)}, u32[]{:S(2)}) %collective-permute-start.6) | collective-permute-done | bytes 139296 | tf_op jit(solution)/shard_map/ppermute | solution.py:468
  34.3 3.2 %collective-permute-start.8 = (bf16[544,128]{1,0:T(8,128)(2,1)S(1)}, bf16[544,128]{1,0:T(8,128)(2,1)S(1)}, u32[]{:S(2)}, u32[]{:S(2)}) collective-permute-start(bf16[544,128]{1,0:T(8,128)(2,1)S(1)} %add_convert_fusion.2), channel_id=1, source_target_pairs={{0,32},{16,240},{32,64},{48,16},{64,96},{80,48},{96,128},{112,80},... | collective-permute-start | bytes 417800 | tf_op jit(solution)/shard_map/ppermute | solution.py:468
  37.5 1.5 %collective-permute-start.10 = (bf16[544,128]{1,0:T(8,128)(2,1)S(1)}, bf16[544,128]{1,0:T(8,128)(2,1)S(1)}, u32[]{:S(2)}, u32[]{:S(2)}) collective-permute-start(bf16[544,128]{1,0:T(8,128)(2,1)S(1)} %add_convert_fusion.1), channel_id=1, source_target_pairs={{0,32},{16,240},{32,64},{48,16},{64,96},{80,48},{96,128},{112,80},... | collective-permute-start | bytes 417800 | tf_op jit(solution)/shard_map/ppermute | solution.py:468
  39.0 0.5 collective-permute-done.8
  39.5 2.2 %collective-permute-done.10 = bf16[544,128]{1,0:T(8,128)(2,1)S(1)} collective-permute-done((bf16[544,128]{1,0:T(8,128)(2,1)S(1)}, bf16[544,128]{1,0:T(8,128)(2,1)S(1)}, u32[]{:S(2)}, u32[]{:S(2)}) %collective-permute-start.10) | collective-permute-done | bytes 139296 | tf_op jit(solution)/shard_map/ppermute | solution.py:468
  41.8 2.7 %collective-permute-start.11 = (bf16[544,128]{1,0:T(8,128)(2,1)S(1)}, bf16[544,128]{1,0:T(8,128)(2,1)S(1)}, u32[]{:S(2)}, u32[]{:S(2)}) collective-permute-start(bf16[544,128]{1,0:T(8,128)(2,1)S(1)} %get-tuple-element.68.mine_first), channel_id=1, source_target_pairs={{0,16},{16,0},{32,48},{48,32},{64,80},{80,64},{96,112},{112,96},{1... | collective-permute-start | bytes 417800 | tf_op jit(solution)/shard_map/ppermute | solution.py:464
  44.5 0.1 collective-permute-start.12
  44.7 0.8 %collective-permute-done.11.theirs_first = bf16[544,128]{1,0:T(8,128)(2,1)S(1)} collective-permute-done((bf16[544,128]{1,0:T(8,128)(2,1)S(1)}, bf16[544,128]{1,0:T(8,128)(2,1)S(1)}, u32[]{:S(2)}, u32[]{:S(2)}) %collective-permute-start.11) | collective-permute-done | bytes 139296 | tf_op jit(solution)/shard_map/ppermute | solution.py:464
  45.5 0.4 collective-permute-done.12.theirs_second
  45.9 4.1 %shard_map.69 = (bf16[528,128]{1,0:T(8,128)(2,1)S(1)}, bf16[528,128]{1,0:T(8,128)(2,1)S(1)}) custom-call(s32[2]{0:T(128)S(1)} %pad_add_fusion.4.place_ref, bf16[544,128]{1,0:T(8,128)(2,1)S(1)} %get-tuple-element.68.mine_first, bf16[544,128]{1,0:T(8,128)(2,1)S(1)} %get-tuple-element.67.mine_second, bf16[544,128]{1,0:T(8,128)(2,1)S(1)} %collective-permute-done.11.theirs_first, ...), custom_call_target="tpu_custom_call" | custom-call | flops 2415919104 | bytes 811008 | tf_op jit(solution)/shard_map/pallas_call | solution.py:288
  50.0 0.2 collective-permute-start.13
  50.2 0.2 collective-permute-start.14
  50.4 3.5 %collective-permute-done.13.refs_2_ = bf16[528,128]{1,0:T(8,128)(2,1)S(1)} collective-permute-done((bf16[528,128]{1,0:T(8,128)(2,1)S(1)}, bf16[528,128]{1,0:T(8,128)(2,1)S(1)}, u32[]{:S(2)}, u32[]{:S(2)}) %collective-permute-start.13) | collective-permute-done | bytes 135200 | tf_op jit(solution)/shard_map/ppermute | solution.py:468
  53.9 1.3 %collective-permute-start.15 = (bf16[528,128]{1,0:T(8,128)(2,1)S(1)}, bf16[528,128]{1,0:T(8,128)(2,1)S(1)}, u32[]{:S(2)}, u32[]{:S(2)}) collective-permute-start(bf16[528,128]{1,0:T(8,128)(2,1)S(1)} %collective-permute-done.13.refs_2_), channel_id=1, source_target_pairs={{0,32},{16,240},{32,64},{48,16},{64,96},{80,48},{96,128},{112,80},... | collective-permute-start | bytes 405512 | tf_op jit(solution)/shard_map/ppermute | solution.py:468
  55.2 0.4 collective-permute-done.14.refs_3_
  55.7 1.0 %collective-permute-start.16 = (bf16[528,128]{1,0:T(8,128)(2,1)S(1)}, bf16[528,128]{1,0:T(8,128)(2,1)S(1)}, u32[]{:S(2)}, u32[]{:S(2)}) collective-permute-start(bf16[528,128]{1,0:T(8,128)(2,1)S(1)} %collective-permute-done.14.refs_3_), channel_id=1, source_target_pairs={{0,32},{16,240},{32,64},{48,16},{64,96},{80,48},{96,128},{112,80},... | collective-permute-start | bytes 405512 | tf_op jit(solution)/shard_map/ppermute | solution.py:468
  56.7 1.1 %collective-permute-done.15.refs_5_ = bf16[528,128]{1,0:T(8,128)(2,1)S(1)} collective-permute-done((bf16[528,128]{1,0:T(8,128)(2,1)S(1)}, bf16[528,128]{1,0:T(8,128)(2,1)S(1)}, u32[]{:S(2)}, u32[]{:S(2)}) %collective-permute-start.15) | collective-permute-done | bytes 135200 | tf_op jit(solution)/shard_map/ppermute | solution.py:468
  57.8 1.7 %collective-permute-done.16.refs_6_ = bf16[528,128]{1,0:T(8,128)(2,1)S(1)} collective-permute-done((bf16[528,128]{1,0:T(8,128)(2,1)S(1)}, bf16[528,128]{1,0:T(8,128)(2,1)S(1)}, u32[]{:S(2)}, u32[]{:S(2)}) %collective-permute-start.16) | collective-permute-done | bytes 135200 | tf_op jit(solution)/shard_map/ppermute | solution.py:468
  59.6 4.7 %collective-permute-start.17 = (bf16[2112,128]{1,0:T(8,128)(2,1)S(1)}, bf16[2112,128]{1,0:T(8,128)(2,1)S(1)}, u32[]{:S(2)}, u32[]{:S(2)}) collective-permute-start(bf16[2112,128]{1,0:T(8,128)(2,1)S(1)} %pad_maximum_fusion), channel_id=1, source_target_pairs={{0,16},{16,0},{32,48},{48,32},{64,80},{80,64},{96,112},{112,96},{1... | collective-permute-start | bytes 1622024 | tf_op jit(solution)/shard_map/ppermute | solution.py:464
  64.3 0.3 collective-permute-start.18
  64.6 3.4 %collective-permute-start.20 = (bf16[528,128]{1,0:T(8,128)(2,1)S(1)}, bf16[528,128]{1,0:T(8,128)(2,1)S(1)}, u32[]{:S(2)}, u32[]{:S(2)}) collective-permute-start(bf16[528,128]{1,0:T(8,128)(2,1)S(1)} %collective-permute-done.15.refs_5_), channel_id=1, source_target_pairs={{0,64},{16,208},{32,96},{48,240},{64,128},{80,16},{96,160},{112,48... | collective-permute-start | bytes 405512 | tf_op jit(solution)/shard_map/ppermute | solution.py:468
  68.0 4.5 %shard_map.70 = (bf16[8,256,512]{2,1,0:T(8,128)(2,1)}, bf16[8,256,512]{2,1,0:T(8,128)(2,1)}, f32[1,128]{1,0:T(1,128)S(1)}, bf16[1,128]{1,0:T(2,128)(2,1)S(1)}) custom-call(s32[2]{0:T(128)S(1)} %pad_add_fusion.4.place_ref, f32[1,128]{1,0:T(1,128)S(1)} %broadcast_in_dim.69.peaks_ref, bf16[8,256,512]{2,1,0:T(8,128)(2,1)S(1)} %get-tuple-element.38.advance_ref, ...), custom_call_target="tpu_custom_call" | custom-call | flops 671088640 | bytes 6594560 | tf_op jit(solution)/shard_map/pallas_call | solution.py:395
  72.5 0.1 maximum_add_fusion
  72.6 2.5 %collective-permute-start.21 = (bf16[1584,128]{1,0:T(8,128)(2,1)S(1)}, bf16[1584,128]{1,0:T(8,128)(2,1)S(1)}, u32[]{:S(2)}, u32[]{:S(2)}) collective-permute-start(bf16[1584,128]{1,0:T(8,128)(2,1)S(1)} %maximum_add_fusion), channel_id=1, source_target_pairs={{0,16},{16,0},{32,48},{48,32},{64,80},{80,64},{96,112},{112,96},{1... | collective-permute-start | bytes 1216520 | tf_op jit(solution)/shard_map/ppermute | solution.py:464
  75.1 1.8 %shard_map.71 = (bf16[8,256,512]{2,1,0:T(8,128)(2,1)}, bf16[8,256,512]{2,1,0:T(8,128)(2,1)}, f32[1,128]{1,0:T(1,128)}, bf16[1,128]{1,0:T(2,128)(2,1)}) custom-call(s32[2]{0:T(128)S(1)} %pad_add_fusion.4.place_ref, f32[1,128]{1,0:T(1,128)S(1)} %get-tuple-element.54.peaks_ref, ...), custom_call_target="tpu_custom_call", output_to_operand_aliasing={{0}: (6, {}), {1}: (7, {})} | custom-call | flops 134217728 | bytes 1318912 | tf_op jit(solution)/shard_map/pallas_call | solution.py:395
  76.9 2.4 %shard_map.72 = (bf16[8,256,512]{2,1,0:T(8,128)(2,1)}, bf16[8,256,512]{2,1,0:T(8,128)(2,1)}, f32[1,128]{1,0:T(1,128)}, bf16[1,128]{1,0:T(2,128)(2,1)}) custom-call(s32[2]{0:T(128)S(1)} %pad_add_fusion.4.place_ref, f32[1,128]{1,0:T(1,128)S(1)} %get-tuple-element.54.peaks_ref, ...), custom_call_target="tpu_custom_call", output_to_operand_aliasing={{0}: (6, {}), {1}: (7, {})} | custom-call | flops 268435456 | bytes 2637824 | tf_op jit(solution)/shard_map/pallas_call | solution.py:395
  (32 shorter events, 0.6 us)
Async XLA Ops:
  0.6 14.1 %copy-start = (f32[1,64,32]{1,2,0:T(8,128)S(1)}, f32[1,64,32]{1,2,0:T(8,128)}, u32[]{:S(2)}) copy-start(f32[1,64,32]{1,2,0:T(8,128)} %param.7) | copy-start | bytes 24580
  4.0 4.7 %collective-permute-start = (bf16[1632,128]{1,0:T(8,128)(2,1)S(1)}, bf16[1632,128]{1,0:T(8,128)(2,1)S(1)}, u32[]{:S(2)}, u32[]{:S(2)}) collective-permute-start(bf16[1632,128]{1,0:T(8,128)(2,1)S(1)} %get-tuple-element.34), channel_id=1, source_target_pairs={{0,16},{16,0},{32,48},{48,32},{64,80},{80,64},{96,112},{112,96},{1... | collective-permute-start | bytes 1253384 | tf_op jit(solution)/shard_map/ppermute | solution.py:464
  8.9 13.5 %collective-permute-start.3 = (bf16[544,128]{1,0:T(8,128)(2,1)S(1)}, bf16[544,128]{1,0:T(8,128)(2,1)}, u32[]{:S(2)}, u32[]{:S(2)}) collective-permute-start(bf16[544,128]{1,0:T(8,128)(2,1)S(1)} %get-tuple-element.35.refs_0_), channel_id=1, source_target_pairs={{0,64},{16,208},{32,96},{48,240},{64,128},{80,16},{96,160},{112,48... | collective-permute-start | bytes 417800 | tf_op jit(solution)/shard_map/ppermute | solution.py:468
  13.2 10.1 %collective-permute-start.4 = (bf16[544,128]{1,0:T(8,128)(2,1)S(1)}, bf16[544,128]{1,0:T(8,128)(2,1)}, u32[]{:S(2)}, u32[]{:S(2)}) collective-permute-start(bf16[544,128]{1,0:T(8,128)(2,1)S(1)} %get-tuple-element.44), channel_id=1, source_target_pairs={{0,32},{16,240},{32,64},{48,16},{64,96},{80,48},{96,128},{112,80},... | collective-permute-start | bytes 417800 | tf_op jit(solution)/shard_map/ppermute | solution.py:468
  14.0 10.3 %collective-permute-start.5 = (bf16[544,128]{1,0:T(8,128)(2,1)S(1)}, bf16[544,128]{1,0:T(8,128)(2,1)S(1)}, u32[]{:S(2)}, u32[]{:S(2)}) collective-permute-start(bf16[544,128]{1,0:T(8,128)(2,1)S(1)} %get-tuple-element.45), channel_id=1, source_target_pairs={{0,32},{16,240},{32,64},{48,16},{64,96},{80,48},{96,128},{112,80},... | collective-permute-start | bytes 417800 | tf_op jit(solution)/shard_map/ppermute | solution.py:468
  14.8 7.5 %collective-permute-start.2 = (f32[4,32]{1,0:T(4,128)S(1)}, f32[4,32]{1,0:T(4,128)S(1)}, u32[]{:S(2)}, u32[]{:S(2)}) collective-permute-start(f32[4,32]{1,0:T(4,128)S(1)} %bitcast.27), channel_id=1, source_target_pairs={{0,0},{1,1},{2,2},{3,3},{4,4},{5,5},{6,6},{7,7},{8,8},{9,9},{10,10... | collective-permute-start | bytes 1544 | tf_op jit(solution)/shard_map/ppermute | solution.py:437
  22.2 3.7 %collective-permute-start.1 = (bf16[2176,128]{1,0:T(8,128)(2,1)}, bf16[2176,128]{1,0:T(8,128)(2,1)}, u32[]{:S(2)}, u32[]{:S(2)}) collective-permute-start(bf16[2176,128]{1,0:T(8,128)(2,1)} %get-tuple-element.40), channel_id=1, source_target_pairs={{0,16},{16,0},{32,48},{48,32},{64,80},{80,64},{96,112},{112,96},{1... | collective-permute-start | bytes 1671176 | tf_op jit(solution)/shard_map/ppermute | solution.py:464
  24.4 1.4 %collective-permute-start.7 = (bf16[64,128]{1,0:T(8,128)(2,1)S(1)}, bf16[64,128]{1,0:T(8,128)(2,1)S(1)}, u32[]{:S(2)}, u32[]{:S(2)}) collective-permute-start(bf16[64,128]{1,0:T(8,128)(2,1)S(1)} %select_convert_fusion), channel_id=1, source_target_pairs={{0,16},{16,0},{32,48},{48,32},{64,80},{80,64},{96,112},{112,96},{1... | collective-permute-start | bytes 49160 | tf_op jit(solution)/shard_map/ppermute | solution.py:464
  27.2 7.1 %collective-permute-start.6 = (bf16[544,128]{1,0:T(8,128)(2,1)S(1)}, bf16[544,128]{1,0:T(8,128)(2,1)S(1)}, u32[]{:S(2)}, u32[]{:S(2)}) collective-permute-start(bf16[544,128]{1,0:T(8,128)(2,1)S(1)} %fusion), channel_id=1, source_target_pairs={{0,32},{16,240},{32,64},{48,16},{64,96},{80,48},{96,128},{112,80},... | collective-permute-start | bytes 417800 | tf_op jit(solution)/shard_map/ppermute | solution.py:468
  32.3 5.2 %collective-permute-start.9 = (bf16[544,128]{1,0:T(8,128)(2,1)S(1)}, bf16[544,128]{1,0:T(8,128)(2,1)S(1)}, u32[]{:S(2)}, u32[]{:S(2)}) collective-permute-start(bf16[544,128]{1,0:T(8,128)(2,1)S(1)} %fusion.2), channel_id=1, source_target_pairs={{0,32},{16,240},{32,64},{48,16},{64,96},{80,48},{96,128},{112,80},... | collective-permute-start | bytes 417800 | tf_op jit(solution)/shard_map/ppermute | solution.py:468
  34.3 5.2 %collective-permute-start.8 = (bf16[544,128]{1,0:T(8,128)(2,1)S(1)}, bf16[544,128]{1,0:T(8,128)(2,1)S(1)}, u32[]{:S(2)}, u32[]{:S(2)}) collective-permute-start(bf16[544,128]{1,0:T(8,128)(2,1)S(1)} %add_convert_fusion.2), channel_id=1, source_target_pairs={{0,32},{16,240},{32,64},{48,16},{64,96},{80,48},{96,128},{112,80},... | collective-permute-start | bytes 417800 | tf_op jit(solution)/shard_map/ppermute | solution.py:468
  37.5 4.2 %collective-permute-start.10 = (bf16[544,128]{1,0:T(8,128)(2,1)S(1)}, bf16[544,128]{1,0:T(8,128)(2,1)S(1)}, u32[]{:S(2)}, u32[]{:S(2)}) collective-permute-start(bf16[544,128]{1,0:T(8,128)(2,1)S(1)} %add_convert_fusion.1), channel_id=1, source_target_pairs={{0,32},{16,240},{32,64},{48,16},{64,96},{80,48},{96,128},{112,80},... | collective-permute-start | bytes 417800 | tf_op jit(solution)/shard_map/ppermute | solution.py:468
  41.8 3.7 %collective-permute-start.11 = (bf16[544,128]{1,0:T(8,128)(2,1)S(1)}, bf16[544,128]{1,0:T(8,128)(2,1)S(1)}, u32[]{:S(2)}, u32[]{:S(2)}) collective-permute-start(bf16[544,128]{1,0:T(8,128)(2,1)S(1)} %get-tuple-element.68.mine_first), channel_id=1, source_target_pairs={{0,16},{16,0},{32,48},{48,32},{64,80},{80,64},{96,112},{112,96},{1... | collective-permute-start | bytes 417800 | tf_op jit(solution)/shard_map/ppermute | solution.py:464
  44.5 1.4 %collective-permute-start.12 = (bf16[544,128]{1,0:T(8,128)(2,1)S(1)}, bf16[544,128]{1,0:T(8,128)(2,1)S(1)}, u32[]{:S(2)}, u32[]{:S(2)}) collective-permute-start(bf16[544,128]{1,0:T(8,128)(2,1)S(1)} %get-tuple-element.67.mine_second), channel_id=1, source_target_pairs={{0,16},{16,0},{32,48},{48,32},{64,80},{80,64},{96,112},{112,96},{1... | collective-permute-start | bytes 417800 | tf_op jit(solution)/shard_map/ppermute | solution.py:464
  45.9 22.2 %copy-start.1 = (bf16[4,2,256,512]{3,2,1,0:T(8,128)(2,1)S(1)}, bf16[4,2,256,512]{3,2,1,0:T(8,128)(2,1)}, u32[]{:S(2)}) copy-start(bf16[4,2,256,512]{3,2,1,0:T(8,128)(2,1)} %param.6) | copy-start | bytes 6291460
  50.0 3.9 %collective-permute-start.13 = (bf16[528,128]{1,0:T(8,128)(2,1)S(1)}, bf16[528,128]{1,0:T(8,128)(2,1)S(1)}, u32[]{:S(2)}, u32[]{:S(2)}) collective-permute-start(bf16[528,128]{1,0:T(8,128)(2,1)S(1)} %get-tuple-element.52.refs_0_), channel_id=1, source_target_pairs={{0,32},{16,240},{32,64},{48,16},{64,96},{80,48},{96,128},{112,80},... | collective-permute-start | bytes 405512 | tf_op jit(solution)/shard_map/ppermute | solution.py:468
  50.2 5.5 %collective-permute-start.14 = (bf16[528,128]{1,0:T(8,128)(2,1)S(1)}, bf16[528,128]{1,0:T(8,128)(2,1)S(1)}, u32[]{:S(2)}, u32[]{:S(2)}) collective-permute-start(bf16[528,128]{1,0:T(8,128)(2,1)S(1)} %get-tuple-element.53.refs_1_), channel_id=1, source_target_pairs={{0,32},{16,240},{32,64},{48,16},{64,96},{80,48},{96,128},{112,80},... | collective-permute-start | bytes 405512 | tf_op jit(solution)/shard_map/ppermute | solution.py:468
  53.9 3.9 %collective-permute-start.15 = (bf16[528,128]{1,0:T(8,128)(2,1)S(1)}, bf16[528,128]{1,0:T(8,128)(2,1)S(1)}, u32[]{:S(2)}, u32[]{:S(2)}) collective-permute-start(bf16[528,128]{1,0:T(8,128)(2,1)S(1)} %collective-permute-done.13.refs_2_), channel_id=1, source_target_pairs={{0,32},{16,240},{32,64},{48,16},{64,96},{80,48},{96,128},{112,80},... | collective-permute-start | bytes 405512 | tf_op jit(solution)/shard_map/ppermute | solution.py:468
  55.7 3.9 %collective-permute-start.16 = (bf16[528,128]{1,0:T(8,128)(2,1)S(1)}, bf16[528,128]{1,0:T(8,128)(2,1)S(1)}, u32[]{:S(2)}, u32[]{:S(2)}) collective-permute-start(bf16[528,128]{1,0:T(8,128)(2,1)S(1)} %collective-permute-done.14.refs_3_), channel_id=1, source_target_pairs={{0,32},{16,240},{32,64},{48,16},{64,96},{80,48},{96,128},{112,80},... | collective-permute-start | bytes 405512 | tf_op jit(solution)/shard_map/ppermute | solution.py:468
  59.6 8.5 %collective-permute-start.17 = (bf16[2112,128]{1,0:T(8,128)(2,1)S(1)}, bf16[2112,128]{1,0:T(8,128)(2,1)S(1)}, u32[]{:S(2)}, u32[]{:S(2)}) collective-permute-start(bf16[2112,128]{1,0:T(8,128)(2,1)S(1)} %pad_maximum_fusion), channel_id=1, source_target_pairs={{0,16},{16,0},{32,48},{48,32},{64,80},{80,64},{96,112},{112,96},{1... | collective-permute-start | bytes 1622024 | tf_op jit(solution)/shard_map/ppermute | solution.py:464
  64.3 8.2 %collective-permute-start.18 = (bf16[528,128]{1,0:T(8,128)(2,1)S(1)}, bf16[528,128]{1,0:T(8,128)(2,1)S(1)}, u32[]{:S(2)}, u32[]{:S(2)}) collective-permute-start(bf16[528,128]{1,0:T(8,128)(2,1)S(1)} %collective-permute-done.15.refs_5_), channel_id=1, source_target_pairs={{0,32},{16,240},{32,64},{48,16},{64,96},{80,48},{96,128},{112,80},... | collective-permute-start | bytes 405512 | tf_op jit(solution)/shard_map/ppermute | solution.py:468
  64.6 7.9 %collective-permute-start.19 = (bf16[528,128]{1,0:T(8,128)(2,1)S(1)}, bf16[528,128]{1,0:T(8,128)(2,1)S(1)}, u32[]{:S(2)}, u32[]{:S(2)}) collective-permute-start(bf16[528,128]{1,0:T(8,128)(2,1)S(1)} %collective-permute-done.16.refs_6_), channel_id=1, source_target_pairs={{0,32},{16,240},{32,64},{48,16},{64,96},{80,48},{96,128},{112,80},... | collective-permute-start | bytes 405512 | tf_op jit(solution)/shard_map/ppermute | solution.py:468
  64.6 7.9 %collective-permute-start.20 = (bf16[528,128]{1,0:T(8,128)(2,1)S(1)}, bf16[528,128]{1,0:T(8,128)(2,1)S(1)}, u32[]{:S(2)}, u32[]{:S(2)}) collective-permute-start(bf16[528,128]{1,0:T(8,128)(2,1)S(1)} %collective-permute-done.15.refs_5_), channel_id=1, source_target_pairs={{0,64},{16,208},{32,96},{48,240},{64,128},{80,16},{96,160},{112,48... | collective-permute-start | bytes 405512 | tf_op jit(solution)/shard_map/ppermute | solution.py:468
  72.6 4.3 %collective-permute-start.21 = (bf16[1584,128]{1,0:T(8,128)(2,1)S(1)}, bf16[1584,128]{1,0:T(8,128)(2,1)S(1)}, u32[]{:S(2)}, u32[]{:S(2)}) collective-permute-start(bf16[1584,128]{1,0:T(8,128)(2,1)S(1)} %maximum_add_fusion), channel_id=1, source_target_pairs={{0,16},{16,0},{32,48},{48,32},{64,80},{80,64},{96,112},{112,96},{1... | collective-permute-start | bytes 1216520 | tf_op jit(solution)/shard_map/ppermute | solution.py:464

commit v5 on v4

--- a/solution.py
+++ b/solution.py
@@ -50,7 +50,7 @@
 ORDER = ((0, 1), (0, 2), (0, 3)), ((1, 2), (1, 3), (2, 3))
 
 
-def pack(blocks, rows, residuals=False, peaks=None):
+def pack(blocks, rows, residuals=False):
     upper = square_iota(0) <= square_iota(1)
     pieces = []
     for which in range(2):
@@ -64,10 +64,6 @@
         extra = jnp.where(row == i, values, extra)
         if residuals:
             extra = jnp.where(row == 4 + i, values - wide(low(values)), extra)
-    if peaks is not None:
-        for i in range(3):
-            extra = jnp.where(row == 8 + i, peaks, extra)
-            peaks = peaks - wide(low(peaks))
     return jnp.concatenate([low(piece) for piece in pieces + [extra]], axis=0)
 
 
@@ -118,10 +114,9 @@
     return 4 - (step + 1) // 2, (step % 2) == 1
 
 
-def gram_kernel(steps, matrices, grad_hbm, moment_hbm, *refs):
-    new_moment_hbm, advance_hbm, ours_hbm, theirs_hbm = refs[-11:-7]
-    grad_ref, moment_ref, new_moment_ref, advance_ref, packed_ref, in_sems, out_sems = refs[-7:]
-    own_hbm = ours_hbm.at[pl.ds(2 * GRAM_ROWS, GRAM_ROWS)] if steps[-1] == matrices - 1 else None
+def gram_kernel(matrices, grad_hbm, moment_hbm, *refs):
+    new_moment_hbm, advance_hbm, ours_hbm, theirs_hbm = refs[:4]
+    grad_ref, moment_ref, new_moment_ref, advance_ref, packed_ref, in_sems, out_sems = refs[4:]
     width = grad_ref.shape[2]
     dp = lax.axis_index("dp")
     chip, core = dp // 2, dp % 2
@@ -136,20 +131,20 @@
     def incoming(k, which):
         source, target = ((grad_hbm, grad_ref), (moment_hbm, moment_ref))[which]
         return pltpu.make_async_copy(
-            source.at[place_of(steps[k])], target.at[k], in_sems.at[which, k]
+            source.at[place_of(k)], target.at[k], in_sems.at[which, k]
         )
 
     def outgoing(k, which):
         source, target = ((new_moment_ref, new_moment_hbm), (advance_ref, advance_hbm))[which]
         return pltpu.make_async_copy(
-            source.at[k], target.at[place_of(steps[k])], out_sems.at[which, k]
+            source.at[k], target.at[place_of(k)], out_sems.at[which, k]
         )
 
-    for k in range(len(steps)):
+    for k in range(matrices):
         incoming(k, 0).start()
         incoming(k, 1).start()
     copies = []
-    for k, step in enumerate(steps):
+    for k in range(matrices):
         incoming(k, 0).wait()
         incoming(k, 1).wait()
         widened = wide(grad_ref[k])
@@ -173,21 +168,19 @@
             for j in range(i, 2):
                 blocks[i + 2, j + 2] = lower[i * SIDE : (i + 1) * SIDE, j * SIDE : (j + 1) * SIDE]
         packed = pack(blocks, GRAM_ROWS)
-        distance, mine = carried(step)
-        mine = mine or step == 0
+        distance, mine = carried(k)
+        mine = mine or k == 0
         natural = core == (0 if mine else 1)
         packed_ref[k, :GRAM_HALF] = jnp.where(natural, packed[:GRAM_HALF], packed[GRAM_HALF:])
         packed_ref[k, GRAM_HALF:] = jnp.where(natural, packed[GRAM_HALF:], packed[:GRAM_HALF])
-        if step == 0:
+        if k == 0:
             moves = [
                 (packed_ref.at[k, :GRAM_HALF], ours_hbm.at[pl.ds(0, GRAM_HALF)]),
                 (packed_ref.at[k, GRAM_HALF:], theirs_hbm.at[pl.ds(0, GRAM_HALF)]),
             ]
-        elif step == matrices - 1:
-            moves = [(packed_ref.at[k], own_hbm)]
         else:
-            start = {3: GRAM_HALF, 2: 0, 1: GRAM_ROWS}[distance]
             target = ours_hbm if mine else theirs_hbm
+            start = GRAM_HALF + (3 - distance) * GRAM_ROWS
             moves = [(packed_ref.at[k], target.at[pl.ds(start, GRAM_ROWS)])]
         for i, (source, target) in enumerate(moves):
             copies.append(pltpu.make_async_copy(source, target, out_sems.at[2 + i, k]))
@@ -196,43 +189,36 @@
         copy.wait()
 
 
-def grams(gradients, moments, steps, earlier=None, before=None):
+def grams(gradients, moments):
     matrices, rows, width = gradients.shape
     anywhere = pl.BlockSpec(memory_space=pl.ANY)
-    last = steps[-1] == matrices - 1
-    our_rows = 3 * GRAM_ROWS if last else GRAM_HALF + GRAM_ROWS
-    their_rows = 2 * GRAM_ROWS if last else GRAM_HALF + GRAM_ROWS
     full = jax.ShapeDtypeStruct(gradients.shape, jnp.bfloat16)
-    some = pltpu.VMEM((len(steps), rows, width), jnp.bfloat16)
-    given = [] if earlier is None else [before, *earlier]
     return pl.pallas_call(
-        functools.partial(gram_kernel, steps, matrices),
+        functools.partial(gram_kernel, matrices),
         out_shape=(
             full,
             full,
-            jax.ShapeDtypeStruct((our_rows, SIDE), jnp.bfloat16),
-            jax.ShapeDtypeStruct((their_rows, SIDE), jnp.bfloat16),
-        ),
-        in_specs=[anywhere] * (2 + len(given)),
+            jax.ShapeDtypeStruct((GRAM_HALF + 4 * GRAM_ROWS, SIDE), jnp.bfloat16),
+            jax.ShapeDtypeStruct((GRAM_HALF + 3 * GRAM_ROWS, SIDE), jnp.bfloat16),
+        ),
+        in_specs=[anywhere] * 2,
         out_specs=(anywhere,) * 4,
-        input_output_aliases={3: 0, 4: 1} if given else {},
-        scratch_shapes=[some] * 4
+        scratch_shapes=[pltpu.VMEM(gradients.shape, jnp.bfloat16)] * 4
         + [
-            pltpu.VMEM((len(steps), GRAM_ROWS, SIDE), jnp.bfloat16),
-            pltpu.SemaphoreType.DMA((2, len(steps))),
-            pltpu.SemaphoreType.DMA((4, len(steps))),
+            pltpu.VMEM((matrices, GRAM_ROWS, SIDE), jnp.bfloat16),
+            pltpu.SemaphoreType.DMA((2, matrices)),
+            pltpu.SemaphoreType.DMA((4, matrices)),
         ],
         compiler_params=pltpu.CompilerParams(vmem_limit_bytes=50 * MEBI),
         cost_estimate=pl.CostEstimate(
-            flops=2 * len(steps) * rows * width * width,
-            bytes_accessed=10 * len(steps) * rows * width,
-            transcendentals=0,
-        ),
-    )(gradients, moments, *given)
+            flops=2 * gradients.size * width, bytes_accessed=10 * gradients.size, transcendentals=0
+        ),
+    )(gradients, moments)
 
 
 def polynomial_kernel(
-    place_ref, mine_first, mine_second, theirs_first, theirs_second, first_ref, second_ref
+    place_ref, mine_first, mine_second, theirs_first, theirs_second,
+    first_ref, second_ref, ratio_ref,
 ):
     natural = place_ref[1] == 0
     first = wide(mine_first[...]) + wide(theirs_second[...])
@@ -243,6 +229,7 @@
     blocks, extra = unpack_blocks(packed, jnp.float32)
     logits = extra[16:32] + extra[32:48] + extra[48:64]
     peaks = jnp.max(logits, axis=0, keepdims=True)
+    ratio_ref[...] = jnp.sqrt(jnp.minimum(1.0, CLIP_LIMIT / peaks))
     corners = off_corner(blocks)
     gram = jnp.concatenate(
         [
@@ -276,7 +263,7 @@
         rest = FIRST_COEFF * rest + factor * step + product(rest, step)
         factor = factor * FIRST_COEFF
     total = jnp.where(diagonal, rest + factor, rest) * scale
-    packed = pack(cut_blocks(total), PACKED, residuals=True, peaks=peaks)
+    packed = pack(cut_blocks(total), PACKED, residuals=True)
     first_ref[...] = jnp.where(natural, packed[:HALF], packed[HALF:])
     second_ref[...] = jnp.where(natural, packed[HALF:], packed[:HALF])
 
@@ -287,9 +274,9 @@
     half = jax.ShapeDtypeStruct((HALF, SIDE), jnp.bfloat16)
     return pl.pallas_call(
         polynomial_kernel,
-        out_shape=(half, half),
+        out_shape=(half, half, jax.ShapeDtypeStruct((1, SIDE), jnp.float32)),
         in_specs=[pl.BlockSpec(memory_space=pltpu.SMEM)] + [whole] * 4,
-        out_specs=(whole, whole),
+        out_specs=(whole, whole, whole),
         compiler_params=pltpu.CompilerParams(vmem_limit_bytes=40 * MEBI),
         cost_estimate=pl.CostEstimate(
             flops=9 * 2 * width**3, bytes_accessed=6 * PACKED * SIDE, transcendentals=0
@@ -297,7 +284,7 @@
     )(place, *mine, *theirs)
 
 
-def finish(place, peaks, advance, weights, parts, results):
+def finish(place, ratios, advance, weights, parts, results):
     matrices, rows, width = advance.shape
     pieces = []
     for halves, _, _ in parts:
@@ -320,22 +307,11 @@
             chosen = jnp.where(step == k, signed, chosen)
         return lax.rem(place[0] + chosen, matrices)
 
-    def kernel(place_ref, peaks_ref, advance_ref, weight_ref, *refs):
-        new_weight_ref, update_ref, peaks_out_ref, after_ref = refs[-5:-1]
+    def kernel(place_ref, ratio_ref, advance_ref, weight_ref, *refs):
+        new_weight_ref, update_ref, after_ref = refs[-4:-1]
+        after_ref[...] = jnp.zeros_like(after_ref)
         matrix_ref = refs[-1]
         step = pl.program_id(0)
-
-        @pl.when(step == 0)
-        def _():
-            after_ref[...] = jnp.zeros_like(after_ref)
-            known = peaks_ref[...]
-            if peaks is None:
-                for k in range(count):
-                    ends = [wide(refs[i][row + HALF - 32 : row + HALF]) for i, row in places[k]]
-                    natural = place_ref[1] == (0 if parts[k][2] else 1)
-                    end = jnp.where(natural, ends[1], ends[0])
-                    known = jnp.maximum(known, end[8:9] + end[9:10] + end[10:11])
-            peaks_out_ref[...] = known
 
         for k in range(count):
 
@@ -356,14 +332,13 @@
                     )
 
         which = index(step, place_ref)
-        ratios = jnp.sqrt(jnp.minimum(1.0, CLIP_LIMIT / peaks_out_ref[...]))
         lane = lax.broadcasted_iota(jnp.int32, (1, SIDE), 1)
         head = (which // 2) * (SIDE * 2 // matrices) + (place_ref[0] * 2 + place_ref[1]) * 2
         row = lax.broadcasted_iota(jnp.int32, (rows, 1), 0)
         factor = jnp.zeros((rows, 1), jnp.float32)
         for k in range(rows // DK):
             ratio = jnp.sum(
-                jnp.where(lane == head + k, ratios, 0.0), axis=1, keepdims=True
+                jnp.where(lane == head + k, ratio_ref[...], 0.0), axis=1, keepdims=True
             )
             factor = jnp.where(row // DK == k, ratio, factor)
         factor = jnp.where(which % 2 == 0, factor, 1.0)
@@ -397,7 +372,6 @@
         out_shape=(
             shape,
             shape,
-            jax.ShapeDtypeStruct((1, SIDE), jnp.float32),
             jax.ShapeDtypeStruct((1, SIDE), jnp.bfloat16),
         ),
         grid_spec=pltpu.PrefetchScalarGridSpec(
@@ -406,7 +380,7 @@
             in_specs=[one_row, held, held]
             + [pl.BlockSpec(half.shape, lambda step, place: (0, 0)) for half in pieces]
              + [anywhere] * len(carry),
-            out_specs=(full, full, one_row, one_row),
+            out_specs=(full, full, one_row),
             scratch_shapes=[pltpu.VMEM((width + 16, width), jnp.bfloat16)],
         ),
         input_output_aliases={first_carried + k: k for k in range(len(carry))},
@@ -418,7 +392,7 @@
         ),
     )(
         place,
-        jnp.zeros((1, SIDE), jnp.float32) if peaks is None else peaks,
+        ratios,
         advance,
         weights,
         *pieces,
@@ -428,10 +402,15 @@
 
 def observed(head_logits, layers):
     parties, observers = lax.axis_size("dp"), lax.axis_size("mp")
+    hops = (0, 1, 2, 1)
+    flips = sorted(range(observers), key=lambda flip: -hops[flip // 4] - hops[flip % 4])
     dp = lax.axis_index("dp")
-    start = jnp.bitwise_xor(lax.axis_index("mp"), dp) * layers
+    flip = sum(jnp.where(dp == k, flips[k], 0) for k in range(parties))
+    start = jnp.bitwise_xor(lax.axis_index("mp"), flip) * layers
     pairs = [
-        (k * observers + i, k * observers + (i ^ k)) for k in range(parties) for i in range(observers)
+        (k * observers + i, k * observers + (i ^ flips[k]))
+        for k in range(parties)
+        for i in range(observers)
     ]
     sent = lax.dynamic_slice_in_dim(head_logits[0], start, layers, 0)
     return lax.ppermute(sent, ("dp", "mp"), pairs).reshape(1, -1)
@@ -467,16 +446,14 @@
         pairs = [(i, (i + 2 * distance * (1 - 2 * (i % 2))) % parties) for i in range(parties)]
         return lax.ppermute(value, "dp", pairs)
 
-    gradients, moments = gradients.reshape(stacked), moments.reshape(stacked)
-    *earlier, ours, theirs = grams(gradients, moments, (0, 1, 2))
-    summed = wide(ours) + wide(swap(theirs))
-    far = low(summed[:GRAM_HALF])
-    first = low(summed[GRAM_HALF : 2 * GRAM_HALF])
-    second = low(summed[2 * GRAM_HALF :])
-    far, first, second, head_logits = lax.optimization_barrier((far, first, second, head_logits))
+    values = observed(head_logits, layers)
     new_moments, advance, ours, theirs = grams(
-        gradients, moments, (3, 4, 5, 6, 7), earlier, far
-    )
+        gradients.reshape(stacked), moments.reshape(stacked)
+    )
+    values, theirs = lax.optimization_barrier((values, theirs))
+    rows = gram_rows(values)
+    both_rows = rows + swap(rows)
+    arrived = swap(theirs)
 
     def in_first(rows):
         rows = jnp.where(core == 0, 0.0, wide(rows))
@@ -486,36 +463,31 @@
         rows = jnp.where(core == 0, wide(rows), 0.0)
         return jnp.pad(rows, ((SQUARES - GRAM_HALF, 0), (0, 0)))
 
+    def half(k):
+        part = slice(k * GRAM_HALF, (k + 1) * GRAM_HALF)
+        end = in_first(both_rows) if k == 0 or k % 2 else in_second(both_rows)
+        return wide(ours[part]) + wide(arrived[part]) + end
+
+    halves = [low(half(k)) for k in range(3)] + [half(k) for k in range(3, 7)]
+    own = [wide(ours[k * GRAM_HALF : (k + 1) * GRAM_HALF]) for k in (7, 8)]
+    halves = lax.optimization_barrier(halves)
+
     def hop(value):
         return wide(onward(low(value), 1))
 
-    values = observed(head_logits, layers)
-    far = wide(onward(far, 2))
-    first, second = wide(onward(first, 1)), wide(onward(second, 1))
-    summed = wide(ours[: 2 * GRAM_ROWS]) + wide(swap(theirs))
-    own = wide(ours[2 * GRAM_ROWS :])
-    halves = [summed[k * GRAM_HALF : (k + 1) * GRAM_HALF] for k in range(4)]
-    halves = lax.optimization_barrier(halves)
-    values, far, first, second = lax.optimization_barrier((values, far, first, second))
-    rows = gram_rows(values)
-    first, second = (
-        hop(halves[0] + first + far + in_first(rows)),
-        hop(halves[1] + second + in_second(rows)),
-    )
-    both_rows = lax.optimization_barrier(rows) + lax.optimization_barrier(swap(rows))
-    first, second = (
-        hop(halves[2] + first + in_first(both_rows)),
-        hop(halves[3] + second + in_second(both_rows)),
-    )
-    second = low(second + own[GRAM_HALF:] + in_second(rows))
-    first = low(first + own[:GRAM_HALF] + in_first(rows))
-    first, second = polynomial(place, (first, second), (swap(first), swap(second)))
-
-    def final(peaks, parts, results):
-        *results, peaks, after = finish(
-            place, peaks, advance, weights.reshape(stacked), parts, results
+    far = wide(onward(halves[0], 2))
+    first, second = wide(onward(halves[1], 1)), wide(onward(halves[2], 1))
+    first, second = hop(halves[3] + first + far), hop(halves[4] + second)
+    first, second = hop(halves[5] + first), hop(halves[6] + second)
+    second = low(second + own[1] + in_second(rows))
+    first = low(first + own[0] + in_first(rows))
+    first, second, ratios = polynomial(place, (first, second), (swap(first), swap(second)))
+
+    def final(parts, results):
+        *results, after = finish(
+            place, ratios, advance, weights.reshape(stacked), parts, results
         )
-        return results, peaks, after
+        return results, after
 
     pieces = [(first, second)]
     for distance in (1, 2, 3):
@@ -523,23 +495,22 @@
         if distance == 2:
             far = onward(first, 2)
         pieces.append((first, second))
+    along = [([(half, 0) for half in pieces[k]], k, True) for k in range(4)]
+    results, _ = final(along[:1], None)
+    results, after = final(along[1:2], results)
     near = [half for halves in pieces[1:3] for half in halves]
-    other_near = swap(jnp.concatenate(near, axis=0))
-    results, peaks, after = final(
-        None,
+    other_near = swap(jnp.concatenate(near, axis=0) + after)
+    results, after = final(
         [
-            ([(half, 0) for half in pieces[0]], 0, True),
-            ([(half, 0) for half in pieces[1]], 1, True),
             ([(other_near, 0), (other_near, HALF)], 1, False),
-            ([(half, 0) for half in pieces[2]], 2, True),
+            along[2],
             ([(other_near, 2 * HALF), (other_near, 3 * HALF)], 2, False),
         ],
-        None,
+        results,
     )
     other_remote = swap(jnp.concatenate([*pieces[3], far], axis=0) + after)
-    results, _, _ = final(peaks, [([(half, 0) for half in pieces[3]], 3, True)], results)
-    (new_weights, updates), _, _ = final(
-        peaks,
+    results, _ = final(along[3:], results)
+    (new_weights, updates), _ = final(
         [
             ([(other_remote, 0), (other_remote, HALF)], 3, False),
             ([(far, 0), (other_remote, 2 * HALF)], 4, True),

time: 79.5 us -> 79.7 us (level)
  starting transfers between devices: 39.3 us -> 45.5 us
  waiting for transfers between devices: 14.7 us -> 10.7 us
  other arithmetic: 3.82 us -> 0.96 us
    ppermute x14, waiting for transfers between devices: 11.4 us -> 7.68 us  [onward(): return lax.ppermute(value, 'dp', pairs)]
    ppermute x1, starting transfers between devices: 3.2 us -> 6.57 us  [observed(): return lax.ppermute(sent, ('dp', 'mp'), pairs).reshape(1, -1)]
    ppermute x14, starting transfers between devices: 22.1 us -> 25.1 us  [onward(): return lax.ppermute(value, 'dp', pairs)]
    pallas_call x3 -> x5, Pallas kernels: 8.66 us -> 10.9 us  [finish(): pl.pallas_call(kernel, out_shape=(shape, shape, jax.ShapeDtypeStruct((1,...]
    convert_element_type x4 -> x0, other arithmetic: 1.92 us -> none  [wide(): return value.astype(jnp.float32)]
    pallas_call x3 -> x2, Pallas kernels: 11.6 us -> 9.8 us  [the longest x1 5.68 us: grams(): pl.pallas_call(functools.partial(gram_kernel, matrices), out_shape=(full,...]
    add x1 -> x3, other arithmetic: 1.16 us -> 0.34 us  [the longest x2 0.23 us: half(): return wide(ours[part]) + wide(arrived[part]) + end]
    ppermute x7 -> x6, waiting for transfers between devices: 3.3 us -> 2.97 us  [swap(): return lax.ppermute(value, 'dp', swap_pairs)]
  transfers between devices with their start and end apart: 22 -> 21, of which waited for: 11 -> 7; matrix products, arithmetic and copies ran while one was open for 3% -> 1% of each run, Pallas kernels for 13% -> 18%
where the time goes in v5:
time: 79.7 us; the launch traced here: 79.6 us
  starting transfers between devices  45.5 us (57%)
  Pallas kernels  20.7 us (26%)
  waiting for transfers between devices  10.7 us (13%)
  other arithmetic  0.96 us (1%)
  local copies, waits for them, and re-layouts  0.89 us (1%)
  between operations  0.85 us (1%)
    ppermute x14, starting transfers between devices, onward(): return lax.ppermute(value, 'dp', pairs)  25.1 us
    ppermute x6, starting transfers between devices, swap(): return lax.ppermute(value, 'dp', swap_pairs)  13.9 us
    pallas_call x5, Pallas kernels, finish(): pl.pallas_call(kernel, out_shape=(shape, shape, jax.ShapeDtypeStruct((1,...  10.9 us
    ppermute x14, waiting for transfers between devices, onward(): return lax.ppermute(value, 'dp', pairs)  7.68 us
    ppermute x1, starting transfers between devices, observed(): return lax.ppermute(sent, ('dp', 'mp'), pairs).reshape(1, -1)  6.57 us
    pallas_call x1, Pallas kernels, grams(): pl.pallas_call(functools.partial(gram_kernel, matrices), out_shape=(full,...  5.68 us
    pallas_call x1, Pallas kernels, polynomial(): pl.pallas_call(polynomial_kernel, out_shape=(half, half, jax.ShapeDtypeSt...  4.12 us
    ppermute x6, waiting for transfers between devices, swap(): return lax.ppermute(value, 'dp', swap_pairs)  2.97 us
  transfers between devices with their start and end apart: 21, of which 7 were waited for; matrix products, arithmetic and copies ran while one was open for 1% of the time, Pallas kernels for 18%

profile of v5, /device:TPU:1, one launch (start us, length us, event | category | flops | bytes accessed | tf_op | source)
XLA Modules:
  0.0 79.6 jit_solution(13470695295615156148)
XLA Ops:
  0.7 0.6 copy-done
  1.4 0.1 constant_dynamic-slice_fusion
  1.4 0.1 copy.15
  1.5 6.6 %collective-permute-start = (f32[4,32]{1,0:T(4,128)S(1)}, f32[4,32]{1,0:T(4,128)S(1)}, u32[]{:S(2)}, u32[]{:S(2)}) collective-permute-start(f32[4,32]{1,0:T(4,128)S(1)} %bitcast.28), channel_id=1, source_target_pairs={{0,10},{1,11},{2,8},{3,9},{4,14},{5,15},{6,12},{7,13},{8,2},{9,3},... | collective-permute-start | bytes 1544 | tf_op jit(solution)/shard_map/ppermute | solution.py:416
  8.1 5.7 %shard_map.67 = (bf16[8,256,512]{2,1,0:T(8,128)(2,1)}, bf16[8,256,512]{2,1,0:T(8,128)(2,1)}, bf16[4896,128]{1,0:T(8,128)(2,1)S(1)}, bf16[3808,128]{1,0:T(8,128)(2,1)S(1)}) custom-call(bf16[8,256,512]{2,1,0:T(8,128)(2,1)} %bitcast.26, bf16[8,256,512]{2,1,0:T(8,128)(2,1)} %bitcast.27), custom_call_target="tpu_custom_call" | custom-call | flops 1073741824 | bytes 10485760 | tf_op jit(solution)/shard_map/pallas_call | solution.py:196
  13.8 0.1 reshape.97
  13.9 2.5 %collective-permute-start.1 = (bf16[3808,128]{1,0:T(8,128)(2,1)S(1)}, bf16[3808,128]{1,0:T(8,128)(2,1)S(1)}, u32[]{:S(2)}, u32[]{:S(2)}) collective-permute-start(bf16[3808,128]{1,0:T(8,128)(2,1)S(1)} %get-tuple-element.33), channel_id=1, source_target_pairs={{0,16},{16,0},{32,48},{48,32},{64,80},{80,64},{96,112},{112,96},{1... | collective-permute-start | bytes 2924552 | tf_op jit(solution)/shard_map/ppermute | solution.py:443
  16.4 0.1 select_convert_fusion
  16.5 0.1 collective-permute-start.2
  16.6 2.0 %collective-permute-done.2 = bf16[64,128]{1,0:T(8,128)(2,1)S(1)} collective-permute-done((bf16[64,128]{1,0:T(8,128)(2,1)S(1)}, bf16[64,128]{1,0:T(8,128)(2,1)S(1)}, u32[]{:S(2)}, u32[]{:S(2)}) %collective-permute-start.2) | collective-permute-done | bytes 16416 | tf_op jit(solution)/shard_map/ppermute | solution.py:443
  18.6 0.1 convert_select_fusion.2
  18.7 0.1 pad_add_fusion.4
  18.8 0.1 pad_add_fusion
  18.9 2.8 %collective-permute-start.3 = (bf16[544,128]{1,0:T(8,128)(2,1)S(1)}, bf16[544,128]{1,0:T(8,128)(2,1)S(1)}, u32[]{:S(2)}, u32[]{:S(2)}) collective-permute-start(bf16[544,128]{1,0:T(8,128)(2,1)S(1)} %get-tuple-element.37), channel_id=1, source_target_pairs={{0,32},{16,240},{32,64},{48,16},{64,96},{80,48},{96,128},{112,80},... | collective-permute-start | bytes 417800 | tf_op jit(solution)/shard_map/ppermute | solution.py:447
  21.7 3.6 %collective-permute-start.4 = (bf16[544,128]{1,0:T(8,128)(2,1)S(1)}, bf16[544,128]{1,0:T(8,128)(2,1)S(1)}, u32[]{:S(2)}, u32[]{:S(2)}) collective-permute-start(bf16[544,128]{1,0:T(8,128)(2,1)S(1)} %get-tuple-element.38), channel_id=1, source_target_pairs={{0,64},{16,208},{32,96},{48,240},{64,128},{80,16},{96,160},{112,48... | collective-permute-start | bytes 417800 | tf_op jit(solution)/shard_map/ppermute | solution.py:447
  25.3 0.1 collective-permute-start.7
  25.4 2.3 %collective-permute-done.4 = bf16[544,128]{1,0:T(8,128)(2,1)S(1)} collective-permute-done((bf16[544,128]{1,0:T(8,128)(2,1)S(1)}, bf16[544,128]{1,0:T(8,128)(2,1)S(1)}, u32[]{:S(2)}, u32[]{:S(2)}) %collective-permute-start.4) | collective-permute-done | bytes 139296 | tf_op jit(solution)/shard_map/ppermute | solution.py:447
  27.7 0.1 add_convert_fusion.5
  27.8 2.7 %collective-permute-start.5 = (bf16[544,128]{1,0:T(8,128)(2,1)S(1)}, bf16[544,128]{1,0:T(8,128)(2,1)S(1)}, u32[]{:S(2)}, u32[]{:S(2)}) collective-permute-start(bf16[544,128]{1,0:T(8,128)(2,1)S(1)} %add_convert_fusion.5), channel_id=1, source_target_pairs={{0,32},{16,240},{32,64},{48,16},{64,96},{80,48},{96,128},{112,80},... | collective-permute-start | bytes 417800 | tf_op jit(solution)/shard_map/ppermute | solution.py:447
  30.5 2.0 %collective-permute-start.8 = (bf16[544,128]{1,0:T(8,128)(2,1)S(1)}, bf16[544,128]{1,0:T(8,128)(2,1)S(1)}, u32[]{:S(2)}, u32[]{:S(2)}) collective-permute-start(bf16[544,128]{1,0:T(8,128)(2,1)S(1)} %add_convert_fusion.2), channel_id=1, source_target_pairs={{0,32},{16,240},{32,64},{48,16},{64,96},{80,48},{96,128},{112,80},... | collective-permute-start | bytes 417800 | tf_op jit(solution)/shard_map/ppermute | solution.py:447
  32.5 3.2 %collective-permute-start.6 = (bf16[544,128]{1,0:T(8,128)(2,1)S(1)}, bf16[544,128]{1,0:T(8,128)(2,1)S(1)}, u32[]{:S(2)}, u32[]{:S(2)}) collective-permute-start(bf16[544,128]{1,0:T(8,128)(2,1)S(1)} %add_convert_fusion.4), channel_id=1, source_target_pairs={{0,32},{16,240},{32,64},{48,16},{64,96},{80,48},{96,128},{112,80},... | collective-permute-start | bytes 417800 | tf_op jit(solution)/shard_map/ppermute | solution.py:447
  35.7 1.9 %collective-permute-start.9 = (bf16[544,128]{1,0:T(8,128)(2,1)S(1)}, bf16[544,128]{1,0:T(8,128)(2,1)S(1)}, u32[]{:S(2)}, u32[]{:S(2)}) collective-permute-start(bf16[544,128]{1,0:T(8,128)(2,1)S(1)} %add_convert_fusion.1), channel_id=1, source_target_pairs={{0,32},{16,240},{32,64},{48,16},{64,96},{80,48},{96,128},{112,80},... | collective-permute-start | bytes 417800 | tf_op jit(solution)/shard_map/ppermute | solution.py:447
  37.7 2.3 %collective-permute-done.9 = bf16[544,128]{1,0:T(8,128)(2,1)S(1)} collective-permute-done((bf16[544,128]{1,0:T(8,128)(2,1)S(1)}, bf16[544,128]{1,0:T(8,128)(2,1)S(1)}, u32[]{:S(2)}, u32[]{:S(2)}) %collective-permute-start.9) | collective-permute-done | bytes 139296 | tf_op jit(solution)/shard_map/ppermute | solution.py:447
  40.0 0.1 add_convert_fusion
  40.1 4.4 %collective-permute-start.10 = (bf16[544,128]{1,0:T(8,128)(2,1)S(1)}, bf16[544,128]{1,0:T(8,128)(2,1)S(1)}, u32[]{:S(2)}, u32[]{:S(2)}) collective-permute-start(bf16[544,128]{1,0:T(8,128)(2,1)S(1)} %get-tuple-element.67.mine_first), channel_id=1, source_target_pairs={{0,16},{16,0},{32,48},{48,32},{64,80},{80,64},{96,112},{112,96},{1... | collective-permute-start | bytes 417800 | tf_op jit(solution)/shard_map/ppermute | solution.py:443
  44.5 0.3 collective-permute-start.11
  44.8 0.1 pad_add_fusion.7.place_ref
  44.8 0.6 collective-permute-done.10.theirs_first
  45.5 0.4 collective-permute-done.11.theirs_second
  45.8 4.1 %shard_map.68 = (bf16[528,128]{1,0:T(8,128)(2,1)S(1)}, bf16[528,128]{1,0:T(8,128)(2,1)S(1)}, f32[1,128]{1,0:T(1,128)S(1)}) custom-call(s32[2]{0:T(128)S(1)} %pad_add_fusion.7.place_ref, bf16[544,128]{1,0:T(8,128)(2,1)S(1)} %get-tuple-element.67.mine_first, bf16[544,128]{1,0:T(8,128)(2,1)S(1)} %get-tuple-element.66.mine_second, ...), custom_call_target="tpu_custom_call" | custom-call | flops 2415919104 | bytes 811008 | tf_op jit(solution)/shard_map/pallas_call | solution.py:275
  50.0 0.1 collective-permute-start.12
  50.1 1.4 %collective-permute-start.15 = (bf16[528,128]{1,0:T(8,128)(2,1)S(1)}, bf16[528,128]{1,0:T(8,128)(2,1)S(1)}, u32[]{:S(2)}, u32[]{:S(2)}) collective-permute-start(bf16[528,128]{1,0:T(8,128)(2,1)S(1)} %get-tuple-element.45.refs_1_), channel_id=1, source_target_pairs={{0,32},{16,240},{32,64},{48,16},{64,96},{80,48},{96,128},{112,80},... | collective-permute-start | bytes 405512 | tf_op jit(solution)/shard_map/ppermute | solution.py:447
  51.4 2.5 %collective-permute-done.12.refs_0_ = bf16[528,128]{1,0:T(8,128)(2,1)S(1)} collective-permute-done((bf16[528,128]{1,0:T(8,128)(2,1)S(1)}, bf16[528,128]{1,0:T(8,128)(2,1)S(1)}, u32[]{:S(2)}, u32[]{:S(2)}) %collective-permute-start.12) | collective-permute-done | bytes 135200 | tf_op jit(solution)/shard_map/ppermute | solution.py:447
  53.9 1.2 %collective-permute-start.13 = (bf16[528,128]{1,0:T(8,128)(2,1)S(1)}, bf16[528,128]{1,0:T(8,128)(2,1)S(1)}, u32[]{:S(2)}, u32[]{:S(2)}) collective-permute-start(bf16[528,128]{1,0:T(8,128)(2,1)S(1)} %collective-permute-done.12.refs_0_), channel_id=1, source_target_pairs={{0,32},{16,240},{32,64},{48,16},{64,96},{80,48},{96,128},{112,80},... | collective-permute-start | bytes 405512 | tf_op jit(solution)/shard_map/ppermute | solution.py:447
  55.1 0.5 collective-permute-done.15.refs_1_
  55.7 0.9 %collective-permute-start.16 = (bf16[528,128]{1,0:T(8,128)(2,1)S(1)}, bf16[528,128]{1,0:T(8,128)(2,1)S(1)}, u32[]{:S(2)}, u32[]{:S(2)}) collective-permute-start(bf16[528,128]{1,0:T(8,128)(2,1)S(1)} %collective-permute-done.15.refs_1_), channel_id=1, source_target_pairs={{0,32},{16,240},{32,64},{48,16},{64,96},{80,48},{96,128},{112,80},... | collective-permute-start | bytes 405512 | tf_op jit(solution)/shard_map/ppermute | solution.py:447
  56.6 1.8 %shard_map.69 = (bf16[8,256,512]{2,1,0:T(8,128)(2,1)}, bf16[8,256,512]{2,1,0:T(8,128)(2,1)}, bf16[1,128]{1,0:T(2,128)(2,1)}) custom-call(s32[2]{0:T(128)S(1)} %pad_add_fusion.7.place_ref, f32[1,128]{1,0:T(1,128)S(1)} %get-tuple-element.42.ratio_ref, bf16[8,256,512]{2,1,0:T(8,128)(2,1)S(1)} %copy-done.2, bf16[8,256,512]{2,1,0:T(8,128)(2,1)S(1)} %bitcast.17, ...), custom_call_target="tpu_custom_call" | custom-call | flops 134217728 | bytes 1318912 | tf_op jit(solution)/shard_map/pallas_call | solution.py:370
  58.3 1.8 %shard_map.70 = (bf16[8,256,512]{2,1,0:T(8,128)(2,1)}, bf16[8,256,512]{2,1,0:T(8,128)(2,1)}, bf16[1,128]{1,0:T(2,128)(2,1)S(1)}) custom-call(s32[2]{0:T(128)S(1)} %pad_add_fusion.7.place_ref, f32[1,128]{1,0:T(1,128)S(1)} %get-tuple-element.42.ratio_ref, bf16[8,256,512]{2,1,0:T(8,128)(2,1)S(1)} %copy-done.2, ...), custom_call_target="tpu_custom_call", output_to_operand_aliasing={{0}: (6, {}), {1}: (7, {})} | custom-call | flops 134217728 | bytes 1318912 | tf_op jit(solution)/shard_map/pallas_call | solution.py:370
  60.1 0.1 maximum_add_fusion
  60.2 4.2 %collective-permute-start.19 = (bf16[2112,128]{1,0:T(8,128)(2,1)S(1)}, bf16[2112,128]{1,0:T(8,128)(2,1)S(1)}, u32[]{:S(2)}, u32[]{:S(2)}) collective-permute-start(bf16[2112,128]{1,0:T(8,128)(2,1)S(1)} %maximum_add_fusion), channel_id=1, source_target_pairs={{0,16},{16,0},{32,48},{48,32},{64,80},{80,64},{96,112},{112,96},{1... | collective-permute-start | bytes 1622024 | tf_op jit(solution)/shard_map/ppermute | solution.py:443
  64.4 0.3 collective-permute-start.14
  64.7 0.3 collective-permute-start.17
  65.0 4.7 %collective-permute-start.18 = (bf16[528,128]{1,0:T(8,128)(2,1)S(1)}, bf16[528,128]{1,0:T(8,128)(2,1)S(1)}, u32[]{:S(2)}, u32[]{:S(2)}) collective-permute-start(bf16[528,128]{1,0:T(8,128)(2,1)S(1)} %collective-permute-done.13.refs_1_), channel_id=1, source_target_pairs={{0,64},{16,208},{32,96},{48,240},{64,128},{80,16},{96,160},{112,48... | collective-permute-start | bytes 405512 | tf_op jit(solution)/shard_map/ppermute | solution.py:447
  69.7 3.2 %shard_map.71 = (bf16[8,256,512]{2,1,0:T(8,128)(2,1)}, bf16[8,256,512]{2,1,0:T(8,128)(2,1)}, bf16[1,128]{1,0:T(2,128)(2,1)S(1)}) custom-call(s32[2]{0:T(128)S(1)} %pad_add_fusion.7.place_ref, f32[1,128]{1,0:T(1,128)S(1)} %get-tuple-element.42.ratio_ref, bf16[8,256,512]{2,1,0:T(8,128)(2,1)S(1)} %copy-done.2, ...), custom_call_target="tpu_custom_call", output_to_operand_aliasing={{0}: (7, {}), {1}: (8, {})} | custom-call | flops 402653184 | bytes 3956736 | tf_op jit(solution)/shard_map/pallas_call | solution.py:370
  72.9 0.1 maximum_add_fusion.1
  73.0 2.3 %collective-permute-start.20 = (bf16[1584,128]{1,0:T(8,128)(2,1)S(1)}, bf16[1584,128]{1,0:T(8,128)(2,1)S(1)}, u32[]{:S(2)}, u32[]{:S(2)}) collective-permute-start(bf16[1584,128]{1,0:T(8,128)(2,1)S(1)} %maximum_add_fusion.1), channel_id=1, source_target_pairs={{0,16},{16,0},{32,48},{48,32},{64,80},{80,64},{96,112},{112,96},{1... | collective-permute-start | bytes 1216520 | tf_op jit(solution)/shard_map/ppermute | solution.py:443
  75.4 1.8 %shard_map.72 = (bf16[8,256,512]{2,1,0:T(8,128)(2,1)}, bf16[8,256,512]{2,1,0:T(8,128)(2,1)}, bf16[1,128]{1,0:T(2,128)(2,1)}) custom-call(s32[2]{0:T(128)S(1)} %pad_add_fusion.7.place_ref, f32[1,128]{1,0:T(1,128)S(1)} %get-tuple-element.42.ratio_ref, bf16[8,256,512]{2,1,0:T(8,128)(2,1)S(1)} %copy-done.2, ...), custom_call_target="tpu_custom_call", output_to_operand_aliasing={{0}: (6, {}), {1}: (7, {})} | custom-call | flops 134217728 | bytes 1318912 | tf_op jit(solution)/shard_map/pallas_call | solution.py:370
  77.1 2.4 %shard_map.73 = (bf16[8,256,512]{2,1,0:T(8,128)(2,1)}, bf16[8,256,512]{2,1,0:T(8,128)(2,1)}, bf16[1,128]{1,0:T(2,128)(2,1)}) custom-call(s32[2]{0:T(128)S(1)} %pad_add_fusion.7.place_ref, f32[1,128]{1,0:T(1,128)S(1)} %get-tuple-element.42.ratio_ref, bf16[8,256,512]{2,1,0:T(8,128)(2,1)S(1)} %copy-done.2, ...), custom_call_target="tpu_custom_call", output_to_operand_aliasing={{0}: (6, {}), {1}: (7, {})} | custom-call | flops 268435456 | bytes 2637824 | tf_op jit(solution)/shard_map/pallas_call | solution.py:370
  (25 shorter events, 0.3 us)
Async XLA Ops:
  0.6 0.7 copy-start
  1.5 12.3 %collective-permute-start = (f32[4,32]{1,0:T(4,128)S(1)}, f32[4,32]{1,0:T(4,128)S(1)}, u32[]{:S(2)}, u32[]{:S(2)}) collective-permute-start(f32[4,32]{1,0:T(4,128)S(1)} %bitcast.28), channel_id=1, source_target_pairs={{0,10},{1,11},{2,8},{3,9},{4,14},{5,15},{6,12},{7,13},{8,2},{9,3},... | collective-permute-start | bytes 1544 | tf_op jit(solution)/shard_map/ppermute | solution.py:416
  13.9 4.8 %collective-permute-start.1 = (bf16[3808,128]{1,0:T(8,128)(2,1)S(1)}, bf16[3808,128]{1,0:T(8,128)(2,1)S(1)}, u32[]{:S(2)}, u32[]{:S(2)}) collective-permute-start(bf16[3808,128]{1,0:T(8,128)(2,1)S(1)} %get-tuple-element.33), channel_id=1, source_target_pairs={{0,16},{16,0},{32,48},{48,32},{64,80},{80,64},{96,112},{112,96},{1... | collective-permute-start | bytes 2924552 | tf_op jit(solution)/shard_map/ppermute | solution.py:443
  16.5 2.1 %collective-permute-start.2 = (bf16[64,128]{1,0:T(8,128)(2,1)S(1)}, bf16[64,128]{1,0:T(8,128)(2,1)S(1)}, u32[]{:S(2)}, u32[]{:S(2)}) collective-permute-start(bf16[64,128]{1,0:T(8,128)(2,1)S(1)} %select_convert_fusion), channel_id=1, source_target_pairs={{0,16},{16,0},{32,48},{48,32},{64,80},{80,64},{96,112},{112,96},{1... | collective-permute-start | bytes 49160 | tf_op jit(solution)/shard_map/ppermute | solution.py:443
  18.9 6.5 %collective-permute-start.3 = (bf16[544,128]{1,0:T(8,128)(2,1)S(1)}, bf16[544,128]{1,0:T(8,128)(2,1)S(1)}, u32[]{:S(2)}, u32[]{:S(2)}) collective-permute-start(bf16[544,128]{1,0:T(8,128)(2,1)S(1)} %get-tuple-element.37), channel_id=1, source_target_pairs={{0,32},{16,240},{32,64},{48,16},{64,96},{80,48},{96,128},{112,80},... | collective-permute-start | bytes 417800 | tf_op jit(solution)/shard_map/ppermute | solution.py:447
  21.7 6.0 %collective-permute-start.4 = (bf16[544,128]{1,0:T(8,128)(2,1)S(1)}, bf16[544,128]{1,0:T(8,128)(2,1)S(1)}, u32[]{:S(2)}, u32[]{:S(2)}) collective-permute-start(bf16[544,128]{1,0:T(8,128)(2,1)S(1)} %get-tuple-element.38), channel_id=1, source_target_pairs={{0,64},{16,208},{32,96},{48,240},{64,128},{80,16},{96,160},{112,48... | collective-permute-start | bytes 417800 | tf_op jit(solution)/shard_map/ppermute | solution.py:447
  25.3 5.1 %collective-permute-start.7 = (bf16[544,128]{1,0:T(8,128)(2,1)S(1)}, bf16[544,128]{1,0:T(8,128)(2,1)S(1)}, u32[]{:S(2)}, u32[]{:S(2)}) collective-permute-start(bf16[544,128]{1,0:T(8,128)(2,1)S(1)} %get-tuple-element.41), channel_id=1, source_target_pairs={{0,32},{16,240},{32,64},{48,16},{64,96},{80,48},{96,128},{112,80},... | collective-permute-start | bytes 417800 | tf_op jit(solution)/shard_map/ppermute | solution.py:447
  27.8 4.7 %collective-permute-start.5 = (bf16[544,128]{1,0:T(8,128)(2,1)S(1)}, bf16[544,128]{1,0:T(8,128)(2,1)S(1)}, u32[]{:S(2)}, u32[]{:S(2)}) collective-permute-start(bf16[544,128]{1,0:T(8,128)(2,1)S(1)} %add_convert_fusion.5), channel_id=1, source_target_pairs={{0,32},{16,240},{32,64},{48,16},{64,96},{80,48},{96,128},{112,80},... | collective-permute-start | bytes 417800 | tf_op jit(solution)/shard_map/ppermute | solution.py:447
  30.5 5.2 %collective-permute-start.8 = (bf16[544,128]{1,0:T(8,128)(2,1)S(1)}, bf16[544,128]{1,0:T(8,128)(2,1)S(1)}, u32[]{:S(2)}, u32[]{:S(2)}) collective-permute-start(bf16[544,128]{1,0:T(8,128)(2,1)S(1)} %add_convert_fusion.2), channel_id=1, source_target_pairs={{0,32},{16,240},{32,64},{48,16},{64,96},{80,48},{96,128},{112,80},... | collective-permute-start | bytes 417800 | tf_op jit(solution)/shard_map/ppermute | solution.py:447
  32.5 5.2 %collective-permute-start.6 = (bf16[544,128]{1,0:T(8,128)(2,1)S(1)}, bf16[544,128]{1,0:T(8,128)(2,1)S(1)}, u32[]{:S(2)}, u32[]{:S(2)}) collective-permute-start(bf16[544,128]{1,0:T(8,128)(2,1)S(1)} %add_convert_fusion.4), channel_id=1, source_target_pairs={{0,32},{16,240},{32,64},{48,16},{64,96},{80,48},{96,128},{112,80},... | collective-permute-start | bytes 417800 | tf_op jit(solution)/shard_map/ppermute | solution.py:447
  35.7 4.3 %collective-permute-start.9 = (bf16[544,128]{1,0:T(8,128)(2,1)S(1)}, bf16[544,128]{1,0:T(8,128)(2,1)S(1)}, u32[]{:S(2)}, u32[]{:S(2)}) collective-permute-start(bf16[544,128]{1,0:T(8,128)(2,1)S(1)} %add_convert_fusion.1), channel_id=1, source_target_pairs={{0,32},{16,240},{32,64},{48,16},{64,96},{80,48},{96,128},{112,80},... | collective-permute-start | bytes 417800 | tf_op jit(solution)/shard_map/ppermute | solution.py:447
  40.1 5.4 %collective-permute-start.10 = (bf16[544,128]{1,0:T(8,128)(2,1)S(1)}, bf16[544,128]{1,0:T(8,128)(2,1)S(1)}, u32[]{:S(2)}, u32[]{:S(2)}) collective-permute-start(bf16[544,128]{1,0:T(8,128)(2,1)S(1)} %get-tuple-element.67.mine_first), channel_id=1, source_target_pairs={{0,16},{16,0},{32,48},{48,32},{64,80},{80,64},{96,112},{112,96},{1... | collective-permute-start | bytes 417800 | tf_op jit(solution)/shard_map/ppermute | solution.py:443
  44.5 1.4 %collective-permute-start.11 = (bf16[544,128]{1,0:T(8,128)(2,1)S(1)}, bf16[544,128]{1,0:T(8,128)(2,1)S(1)}, u32[]{:S(2)}, u32[]{:S(2)}) collective-permute-start(bf16[544,128]{1,0:T(8,128)(2,1)S(1)} %get-tuple-element.66.mine_second), channel_id=1, source_target_pairs={{0,16},{16,0},{32,48},{48,32},{64,80},{80,64},{96,112},{112,96},{1... | collective-permute-start | bytes 417800 | tf_op jit(solution)/shard_map/ppermute | solution.py:443
  44.8 11.7 %copy-start.1 = (bf16[4,2,256,512]{3,2,1,0:T(8,128)(2,1)S(1)}, bf16[4,2,256,512]{3,2,1,0:T(8,128)(2,1)}, u32[]{:S(2)}) copy-start(bf16[4,2,256,512]{3,2,1,0:T(8,128)(2,1)} %param.6) | copy-start | bytes 6291460
  44.8 11.7 %copy-start.2 = (bf16[8,256,512]{2,1,0:T(8,128)(2,1)S(1)}, bf16[8,256,512]{2,1,0:T(8,128)(2,1)}, u32[]{:S(2)}) copy-start(bf16[8,256,512]{2,1,0:T(8,128)(2,1)} %get-tuple-element.43.advance_ref) | copy-start | bytes 6291460
  50.0 3.9 %collective-permute-start.12 = (bf16[528,128]{1,0:T(8,128)(2,1)S(1)}, bf16[528,128]{1,0:T(8,128)(2,1)S(1)}, u32[]{:S(2)}, u32[]{:S(2)}) collective-permute-start(bf16[528,128]{1,0:T(8,128)(2,1)S(1)} %get-tuple-element.44.refs_0_), channel_id=1, source_target_pairs={{0,32},{16,240},{32,64},{48,16},{64,96},{80,48},{96,128},{112,80},... | collective-permute-start | bytes 405512 | tf_op jit(solution)/shard_map/ppermute | solution.py:447
  50.1 5.6 %collective-permute-start.15 = (bf16[528,128]{1,0:T(8,128)(2,1)S(1)}, bf16[528,128]{1,0:T(8,128)(2,1)S(1)}, u32[]{:S(2)}, u32[]{:S(2)}) collective-permute-start(bf16[528,128]{1,0:T(8,128)(2,1)S(1)} %get-tuple-element.45.refs_1_), channel_id=1, source_target_pairs={{0,32},{16,240},{32,64},{48,16},{64,96},{80,48},{96,128},{112,80},... | collective-permute-start | bytes 405512 | tf_op jit(solution)/shard_map/ppermute | solution.py:447
  53.9 6.2 %collective-permute-start.13 = (bf16[528,128]{1,0:T(8,128)(2,1)S(1)}, bf16[528,128]{1,0:T(8,128)(2,1)S(1)}, u32[]{:S(2)}, u32[]{:S(2)}) collective-permute-start(bf16[528,128]{1,0:T(8,128)(2,1)S(1)} %collective-permute-done.12.refs_0_), channel_id=1, source_target_pairs={{0,32},{16,240},{32,64},{48,16},{64,96},{80,48},{96,128},{112,80},... | collective-permute-start | bytes 405512 | tf_op jit(solution)/shard_map/ppermute | solution.py:447
  55.7 4.5 %collective-permute-start.16 = (bf16[528,128]{1,0:T(8,128)(2,1)S(1)}, bf16[528,128]{1,0:T(8,128)(2,1)S(1)}, u32[]{:S(2)}, u32[]{:S(2)}) collective-permute-start(bf16[528,128]{1,0:T(8,128)(2,1)S(1)} %collective-permute-done.15.refs_1_), channel_id=1, source_target_pairs={{0,32},{16,240},{32,64},{48,16},{64,96},{80,48},{96,128},{112,80},... | collective-permute-start | bytes 405512 | tf_op jit(solution)/shard_map/ppermute | solution.py:447
  60.2 9.5 %collective-permute-start.19 = (bf16[2112,128]{1,0:T(8,128)(2,1)S(1)}, bf16[2112,128]{1,0:T(8,128)(2,1)S(1)}, u32[]{:S(2)}, u32[]{:S(2)}) collective-permute-start(bf16[2112,128]{1,0:T(8,128)(2,1)S(1)} %maximum_add_fusion), channel_id=1, source_target_pairs={{0,16},{16,0},{32,48},{48,32},{64,80},{80,64},{96,112},{112,96},{1... | collective-permute-start | bytes 1622024 | tf_op jit(solution)/shard_map/ppermute | solution.py:443
  64.4 8.5 %collective-permute-start.14 = (bf16[528,128]{1,0:T(8,128)(2,1)S(1)}, bf16[528,128]{1,0:T(8,128)(2,1)S(1)}, u32[]{:S(2)}, u32[]{:S(2)}) collective-permute-start(bf16[528,128]{1,0:T(8,128)(2,1)S(1)} %collective-permute-done.13.refs_1_), channel_id=1, source_target_pairs={{0,32},{16,240},{32,64},{48,16},{64,96},{80,48},{96,128},{112,80},... | collective-permute-start | bytes 405512 | tf_op jit(solution)/shard_map/ppermute | solution.py:447
  64.7 8.2 %collective-permute-start.17 = (bf16[528,128]{1,0:T(8,128)(2,1)S(1)}, bf16[528,128]{1,0:T(8,128)(2,1)S(1)}, u32[]{:S(2)}, u32[]{:S(2)}) collective-permute-start(bf16[528,128]{1,0:T(8,128)(2,1)S(1)} %collective-permute-done.16.refs_2_), channel_id=1, source_target_pairs={{0,32},{16,240},{32,64},{48,16},{64,96},{80,48},{96,128},{112,80},... | collective-permute-start | bytes 405512 | tf_op jit(solution)/shard_map/ppermute | solution.py:447
  65.0 8.0 %collective-permute-start.18 = (bf16[528,128]{1,0:T(8,128)(2,1)S(1)}, bf16[528,128]{1,0:T(8,128)(2,1)S(1)}, u32[]{:S(2)}, u32[]{:S(2)}) collective-permute-start(bf16[528,128]{1,0:T(8,128)(2,1)S(1)} %collective-permute-done.13.refs_1_), channel_id=1, source_target_pairs={{0,64},{16,208},{32,96},{48,240},{64,128},{80,16},{96,160},{112,48... | collective-permute-start | bytes 405512 | tf_op jit(solution)/shard_map/ppermute | solution.py:447
  73.0 4.1 %collective-permute-start.20 = (bf16[1584,128]{1,0:T(8,128)(2,1)S(1)}, bf16[1584,128]{1,0:T(8,128)(2,1)S(1)}, u32[]{:S(2)}, u32[]{:S(2)}) collective-permute-start(bf16[1584,128]{1,0:T(8,128)(2,1)S(1)} %maximum_add_fusion.1), channel_id=1, source_target_pairs={{0,16},{16,0},{32,48},{48,32},{64,80},{80,64},{96,112},{112,96},{1... | collective-permute-start | bytes 1216520 | tf_op jit(solution)/shard_map/ppermute | solution.py:443

commit v6 on v3

--- a/solution.py
+++ b/solution.py
@@ -119,7 +119,7 @@
 
 def gram_kernel(
     grad_hbm, moment_hbm,
-    new_moment_hbm, advance_hbm, mine_hbm, theirs_hbm, far_mine_hbm, far_theirs_hbm, own_hbm,
+    new_moment_hbm, advance_hbm, mine_hbm, theirs_hbm, far_mine_hbm, their_first_hbm, own_hbm,
     grad_ref, moment_ref, new_moment_ref, advance_ref, packed_ref, in_sems, out_sems,
 ):
     matrices, rows, width = grad_ref.shape
@@ -184,15 +184,18 @@
             first, second = packed_ref.at[0, :GRAM_HALF], packed_ref.at[0, GRAM_HALF:]
             copies.append(packed_copy(first, far_mine_hbm, out_sems.at[2, 0]))
             copies[-1].start()
-            copies.append(packed_copy(second, far_theirs_hbm, out_sems.at[3, 0]))
+            their_far = their_first_hbm.at[pl.ds(0, GRAM_HALF)]
+            copies.append(packed_copy(second, their_far, out_sems.at[3, 0]))
             copies[-1].start()
             continue
         if step == matrices - 1:
             target = own_hbm
         elif mine:
             target = mine_hbm.at[(step - 1) // 2]
+        elif step == 2:
+            target = their_first_hbm.at[pl.ds(GRAM_HALF, GRAM_ROWS)]
         else:
-            target = theirs_hbm.at[(step - 1) // 2]
+            target = theirs_hbm.at[(step - 1) // 2 - 1]
         copies.append(packed_copy(packed_ref.at[step], target, out_sems.at[2, step]))
         copies[-1].start()
     for copy in copies:
@@ -211,8 +214,8 @@
     return pl.pallas_call(
         gram_kernel,
         out_shape=(
-            full, full, shape(3, GRAM_ROWS, SIDE), shape(3, GRAM_ROWS, SIDE),
-            shape(GRAM_HALF, SIDE), shape(GRAM_HALF, SIDE), shape(GRAM_ROWS, SIDE),
+            full, full, shape(3, GRAM_ROWS, SIDE), shape(2, GRAM_ROWS, SIDE),
+            shape(GRAM_HALF, SIDE), shape(GRAM_HALF + GRAM_ROWS, SIDE), shape(GRAM_ROWS, SIDE),
         ),
         in_specs=[there, there],
         out_specs=(there, there) + (anywhere,) * 5,
@@ -366,7 +369,7 @@
             factor = jnp.where(row // DK == k, ratio, factor)
         factor = jnp.where(which % 2 == 0, factor, 1.0)
         off = matrix_ref[:middle, middle:]
-        left, right = advance_ref[0, :, :middle], advance_ref[0, :, middle:]
+        left, right = advance_ref[which, :, :middle], advance_ref[which, :, middle:]
         halves = (
             jnp.dot(left, matrix_ref[:middle, :middle], preferred_element_type=jnp.float32)
             + lax.dot_general(
@@ -380,10 +383,11 @@
             rest = wide(matrix_ref[width : width + 1, columns])
             scaled = scaling * (halves[k] + wide(values) * rest)
             update_ref[0, :, columns] = low(scaled)
-            new_weight = (wide(weight_ref[0, :, columns]) * SHRINK - LEARN_RATE * scaled) * factor
+            new_weight = (wide(weight_ref[which, :, columns]) * SHRINK - LEARN_RATE * scaled) * factor
             new_weight_ref[0, :, columns] = low(new_weight)
 
     full = pl.BlockSpec((1, rows, width), lambda step, place: (index(step, place), 0, 0))
+    held = pl.BlockSpec(memory_space=pltpu.VMEM)
     one_row = pl.BlockSpec((1, SIDE), lambda step, place: (0, 0))
     anywhere = pl.BlockSpec(memory_space=pl.ANY)
     shape = jax.ShapeDtypeStruct(advance.shape, jnp.bfloat16)
@@ -400,7 +404,7 @@
         grid_spec=pltpu.PrefetchScalarGridSpec(
             num_scalar_prefetch=1,
             grid=(count,),
-            in_specs=[one_row, full, full]
+            in_specs=[one_row, held, held]
             + [pl.BlockSpec(half.shape, lambda step, place: (0, 0)) for half in pieces]
              + [anywhere] * len(carry),
             out_specs=(full, full, one_row, one_row),
@@ -464,18 +468,16 @@
         pairs = [(i, (i + 2 * distance * (1 - 2 * (i % 2))) % parties) for i in range(parties)]
         return lax.ppermute(value, "dp", pairs)
 
-    new_moments, advance, mine, theirs, far_mine, far_theirs, own = grams(
+    new_moments, advance, mine, theirs, far_mine, their_first, own = grams(
         gradients.reshape(stacked), moments.reshape(stacked)
     )
-    far_arrived, arrived = swap(far_theirs), swap(theirs)
+    arrived_first, arrived = swap(their_first), swap(theirs)
 
     def first_half(distance):
-        slot = 3 - distance
-        return wide(mine[slot, :GRAM_HALF]) + wide(arrived[slot, :GRAM_HALF])
+        return wide(mine[3 - distance, :GRAM_HALF]) + wide(arrived[2 - distance, :GRAM_HALF])
 
     def second_half(distance):
-        slot = 3 - distance
-        return wide(mine[slot, GRAM_HALF:]) + wide(arrived[slot, GRAM_HALF:])
+        return wide(mine[3 - distance, GRAM_HALF:]) + wide(arrived[2 - distance, GRAM_HALF:])
 
     def in_first(rows):
         rows = jnp.where(core == 0, 0.0, wide(rows))
@@ -488,26 +490,26 @@
     def hop(value):
         return wide(onward(low(value), 1))
 
-    far = low(wide(far_mine) + wide(far_arrived))
-    firsts = [first_half(distance) for distance in (3, 2, 1)]
-    seconds = [second_half(distance) for distance in (3, 2, 1)]
-    firsts[0], seconds[0] = low(firsts[0]), low(seconds[0])
-    far, firsts, seconds, head_logits = lax.optimization_barrier(
-        (far, firsts, seconds, head_logits)
+    far = low(wide(far_mine) + wide(arrived_first[:GRAM_HALF]))
+    first = low(wide(mine[0, :GRAM_HALF]) + wide(arrived_first[GRAM_HALF : 2 * GRAM_HALF]))
+    second = low(wide(mine[0, GRAM_HALF:]) + wide(arrived_first[2 * GRAM_HALF :]))
+    far, first, second, head_logits = lax.optimization_barrier((far, first, second, head_logits))
+    firsts, seconds = lax.optimization_barrier(
+        ([first_half(2), first_half(1)], [second_half(2), second_half(1)])
     )
     values = observed(head_logits, layers)
     far = wide(onward(far, 2))
-    first, second = wide(onward(firsts[0], 1)), wide(onward(seconds[0], 1))
+    first, second = wide(onward(first, 1)), wide(onward(second, 1))
     values, far, first, second = lax.optimization_barrier((values, far, first, second))
     rows = gram_rows(values)
     first, second = (
-        hop(firsts[1] + first + far + in_first(rows)),
-        hop(seconds[1] + second + in_second(rows)),
+        hop(firsts[0] + first + far + in_first(rows)),
+        hop(seconds[0] + second + in_second(rows)),
     )
     both_rows = lax.optimization_barrier(rows) + lax.optimization_barrier(swap(rows))
     first, second = (
-        hop(firsts[2] + first + in_first(both_rows)),
-        hop(seconds[2] + second + in_second(both_rows)),
+        hop(firsts[1] + first + in_first(both_rows)),
+        hop(seconds[1] + second + in_second(both_rows)),
     )
     second = low(second + wide(own[GRAM_HALF:]) + in_second(rows))
     first = low(first + wide(own[:GRAM_HALF]) + in_first(rows))
@@ -539,10 +541,10 @@
         None,
     )
     other_remote = swap(jnp.concatenate([*pieces[3], far], axis=0) + after)
+    results, _, _ = final(peaks, [([(half, 0) for half in pieces[3]], 3, True)], results)
     (new_weights, updates), _, _ = final(
         peaks,
         [
-            ([(half, 0) for half in pieces[3]], 3, True),
             ([(other_remote, 0), (other_remote, HALF)], 3, False),
             ([(far, 0), (other_remote, 2 * HALF)], 4, True),
         ],

time: 74.9 us -> 75.1 us (level)
  waiting for transfers between devices: 17.6 us -> 15.1 us
  starting transfers between devices: 37.7 us -> 39.4 us
  Pallas kernels: 17.5 us -> 18.5 us
    ppermute x7, waiting for transfers between devices: 4.45 us -> 2.29 us  [swap(): return lax.ppermute(value, 'dp', swap_pairs)]
    ppermute x7, starting transfers between devices: 12.9 us -> 14.6 us  [swap(): return lax.ppermute(value, 'dp', swap_pairs)]
    pallas_call x2 -> x3, Pallas kernels: 7.72 us -> 8.7 us  [finish(): pl.pallas_call(kernel, out_shape=(shape, shape, jax.ShapeDtypeStruct((1,...]
  transfers between devices with their start and end apart: 22 -> 22, of which waited for: 14 -> 12; matrix products, arithmetic and copies ran while one was open for 1% -> 1% of each run, Pallas kernels for 6% -> 8%
where the time goes in v6:
time: 75.1 us; the launch traced here: 75 us
  starting transfers between devices  39.4 us (52%)
  Pallas kernels  18.5 us (25%)
  waiting for transfers between devices  15.1 us (20%)
  other arithmetic  0.92 us (1%)
  between operations  0.82 us (1%)
    ppermute x14, starting transfers between devices, onward(): return lax.ppermute(value, 'dp', pairs)  21.5 us
    ppermute x7, starting transfers between devices, swap(): return lax.ppermute(value, 'dp', swap_pairs)  14.6 us
    ppermute x14, waiting for transfers between devices, onward(): return lax.ppermute(value, 'dp', pairs)  11.4 us
    pallas_call x3, Pallas kernels, finish(): pl.pallas_call(kernel, out_shape=(shape, shape, jax.ShapeDtypeStruct((1,...  8.7 us
    pallas_call x1, Pallas kernels, grams(): pl.pallas_call(gram_kernel, out_shape=(full, full, shape(3, GRAM_ROWS, SI...  5.69 us
    pallas_call x1, Pallas kernels, polynomial(): pl.pallas_call(polynomial_kernel, out_shape=(half, half), in_specs=[pl.Bl...  4.12 us
    ppermute x1, starting transfers between devices, observed(): return lax.ppermute(sent, ('dp', 'mp'), pairs).reshape(1, -1)  3.2 us
    ppermute x7, waiting for transfers between devices, swap(): return lax.ppermute(value, 'dp', swap_pairs)  2.29 us
  transfers between devices with their start and end apart: 22, of which 12 were waited for; matrix products, arithmetic and copies ran while one was open for 1% of the time, Pallas kernels for 8%

profile of v6, /device:TPU:1, one launch (start us, length us, event | category | flops | bytes accessed | tf_op | source)
XLA Modules:
  0.0 75.0 jit_solution(4615658115710340719)
XLA Ops:
  0.6 5.7 %shard_map.67 = (bf16[8,256,512]{2,1,0:T(8,128)(2,1)}, bf16[8,256,512]{2,1,0:T(8,128)(2,1)}, bf16[3,1088,128]{2,1,0:T(8,128)(2,1)S(1)}, bf16[2,1088,128]{2,1,0:T...) custom-call(bf16[8,256,512]{2,1,0:T(8,128)(2,1)} %bitcast.36, ...), custom_call_target="tpu_custom_call" | custom-call | flops 1073741824 | bytes 10485760 | tf_op jit(solution)/shard_map/pallas_call | solution.py:214
  6.3 3.3 %collective-permute-start.1 = (bf16[1632,128]{1,0:T(8,128)(2,1)S(1)}, bf16[1632,128]{1,0:T(8,128)(2,1)S(1)}, u32[]{:S(2)}, u32[]{:S(2)}) collective-permute-start(bf16[1632,128]{1,0:T(8,128)(2,1)S(1)} %get-tuple-element.38), channel_id=1, source_target_pairs={{0,16},{16,0},{32,48},{48,32},{64,80},{80,64},{96,112},{112,96},{1... | collective-permute-start | bytes 1253384 | tf_op jit(solution)/shard_map/ppermute | solution.py:465
  9.7 0.1 collective-permute-start
  9.8 1.3 %collective-permute-done.1 = bf16[1632,128]{1,0:T(8,128)(2,1)S(1)} collective-permute-done((bf16[1632,128]{1,0:T(8,128)(2,1)S(1)}, bf16[1632,128]{1,0:T(8,128)(2,1)S(1)}, u32[]{:S(2)}, u32[]{:S(2)}) %collective-permute-start.1) | collective-permute-done | bytes 417824 | tf_op jit(solution)/shard_map/ppermute | solution.py:465
  11.1 0.1 fusion.4
  11.2 4.4 %collective-permute-start.3 = (bf16[544,128]{1,0:T(8,128)(2,1)S(1)}, bf16[544,128]{1,0:T(8,128)(2,1)S(1)}, u32[]{:S(2)}, u32[]{:S(2)}) collective-permute-start(bf16[544,128]{1,0:T(8,128)(2,1)S(1)} %get-tuple-element.40), channel_id=1, source_target_pairs={{0,64},{16,208},{32,96},{48,240},{64,128},{80,16},{96,160},{112,48... | collective-permute-start | bytes 417800 | tf_op jit(solution)/shard_map/ppermute | solution.py:469
  15.5 0.7 collective-permute-start.4
  16.3 0.7 collective-permute-start.5
  17.0 0.1 constant_dynamic-slice_fusion
  17.1 0.1 copy.11
  17.1 3.2 %collective-permute-start.2 = (f32[4,32]{1,0:T(4,128)S(1)}, f32[4,32]{1,0:T(4,128)S(1)}, u32[]{:S(2)}, u32[]{:S(2)}) collective-permute-start(f32[4,32]{1,0:T(4,128)S(1)} %bitcast.38), channel_id=1, source_target_pairs={{0,0},{1,1},{2,2},{3,3},{4,4},{5,5},{6,6},{7,7},{8,8},{9,9},{10,10... | collective-permute-start | bytes 1544 | tf_op jit(solution)/shard_map/ppermute | solution.py:438
  20.4 1.4 %collective-permute-done.2 = f32[4,32]{1,0:T(4,128)S(1)} collective-permute-done((f32[4,32]{1,0:T(4,128)S(1)}, f32[4,32]{1,0:T(4,128)S(1)}, u32[]{:S(2)}, u32[]{:S(2)}) %collective-permute-start.2) | collective-permute-done | bytes 544 | tf_op jit(solution)/shard_map/ppermute | solution.py:438
  21.8 0.1 reshape.112
  21.9 0.4 collective-permute-done.5
  22.4 0.1 select_convert_fusion
  22.5 1.0 %collective-permute-start.7 = (bf16[64,128]{1,0:T(8,128)(2,1)S(1)}, bf16[64,128]{1,0:T(8,128)(2,1)S(1)}, u32[]{:S(2)}, u32[]{:S(2)}) collective-permute-start(bf16[64,128]{1,0:T(8,128)(2,1)S(1)} %select_convert_fusion), channel_id=1, source_target_pairs={{0,16},{16,0},{32,48},{48,32},{64,80},{80,64},{96,112},{112,96},{1... | collective-permute-start | bytes 49160 | tf_op jit(solution)/shard_map/ppermute | solution.py:465
  23.5 0.1 convert_select_fusion.2
  23.6 0.1 add_bitcast_fusion
  23.8 4.3 %collective-permute-start.6 = (bf16[544,128]{1,0:T(8,128)(2,1)S(1)}, bf16[544,128]{1,0:T(8,128)(2,1)S(1)}, u32[]{:S(2)}, u32[]{:S(2)}) collective-permute-start(bf16[544,128]{1,0:T(8,128)(2,1)S(1)} %fusion), channel_id=1, source_target_pairs={{0,32},{16,240},{32,64},{48,16},{64,96},{80,48},{96,128},{112,80},... | collective-permute-start | bytes 417800 | tf_op jit(solution)/shard_map/ppermute | solution.py:469
  28.1 0.1 collective-permute-start.9
  28.2 1.9 %collective-permute-done.6 = bf16[544,128]{1,0:T(8,128)(2,1)S(1)} collective-permute-done((bf16[544,128]{1,0:T(8,128)(2,1)S(1)}, bf16[544,128]{1,0:T(8,128)(2,1)S(1)}, u32[]{:S(2)}, u32[]{:S(2)}) %collective-permute-start.6) | collective-permute-done | bytes 139296 | tf_op jit(solution)/shard_map/ppermute | solution.py:469
  30.1 3.2 %collective-permute-start.8 = (bf16[544,128]{1,0:T(8,128)(2,1)S(1)}, bf16[544,128]{1,0:T(8,128)(2,1)S(1)}, u32[]{:S(2)}, u32[]{:S(2)}) collective-permute-start(bf16[544,128]{1,0:T(8,128)(2,1)S(1)} %add_convert_fusion.1), channel_id=1, source_target_pairs={{0,32},{16,240},{32,64},{48,16},{64,96},{80,48},{96,128},{112,80},... | collective-permute-start | bytes 417800 | tf_op jit(solution)/shard_map/ppermute | solution.py:469
  33.3 1.5 %collective-permute-start.10 = (bf16[544,128]{1,0:T(8,128)(2,1)S(1)}, bf16[544,128]{1,0:T(8,128)(2,1)S(1)}, u32[]{:S(2)}, u32[]{:S(2)}) collective-permute-start(bf16[544,128]{1,0:T(8,128)(2,1)S(1)} %add_convert_fusion), channel_id=1, source_target_pairs={{0,32},{16,240},{32,64},{48,16},{64,96},{80,48},{96,128},{112,80},... | collective-permute-start | bytes 417800 | tf_op jit(solution)/shard_map/ppermute | solution.py:469
  34.7 0.5 collective-permute-done.8
  35.3 2.1 %collective-permute-done.10 = bf16[544,128]{1,0:T(8,128)(2,1)S(1)} collective-permute-done((bf16[544,128]{1,0:T(8,128)(2,1)S(1)}, bf16[544,128]{1,0:T(8,128)(2,1)S(1)}, u32[]{:S(2)}, u32[]{:S(2)}) %collective-permute-start.10) | collective-permute-done | bytes 139296 | tf_op jit(solution)/shard_map/ppermute | solution.py:469
  37.3 0.1 fusion.3
  37.4 2.6 %collective-permute-start.11 = (bf16[544,128]{1,0:T(8,128)(2,1)S(1)}, bf16[544,128]{1,0:T(8,128)(2,1)S(1)}, u32[]{:S(2)}, u32[]{:S(2)}) collective-permute-start(bf16[544,128]{1,0:T(8,128)(2,1)S(1)} %get-tuple-element.69.mine_first), channel_id=1, source_target_pairs={{0,16},{16,0},{32,48},{48,32},{64,80},{80,64},{96,112},{112,96},{1... | collective-permute-start | bytes 417800 | tf_op jit(solution)/shard_map/ppermute | solution.py:465
  40.1 0.3 collective-permute-start.12
  40.3 0.1 pad_add_fusion.4.place_ref
  40.4 0.6 collective-permute-done.11.theirs_first
  41.1 0.4 collective-permute-done.12.theirs_second
  41.4 4.1 %shard_map.68 = (bf16[528,128]{1,0:T(8,128)(2,1)S(1)}, bf16[528,128]{1,0:T(8,128)(2,1)S(1)}) custom-call(s32[2]{0:T(128)S(1)} %pad_add_fusion.4.place_ref, bf16[544,128]{1,0:T(8,128)(2,1)S(1)} %get-tuple-element.69.mine_first, bf16[544,128]{1,0:T(8,128)(2,1)S(1)} %get-tuple-element.68.mine_second, bf16[544,128]{1,0:T(8,128)(2,1)S(1)} %collective-permute-done.11.theirs_first, ...), custom_call_target="tpu_custom_call" | custom-call | flops 2415919104 | bytes 811008 | tf_op jit(solution)/shard_map/pallas_call | solution.py:289
  45.5 0.3 collective-permute-start.13
  45.9 0.1 collective-permute-start.14
  46.0 3.5 %collective-permute-done.13.refs_2_ = bf16[528,128]{1,0:T(8,128)(2,1)S(1)} collective-permute-done((bf16[528,128]{1,0:T(8,128)(2,1)S(1)}, bf16[528,128]{1,0:T(8,128)(2,1)S(1)}, u32[]{:S(2)}, u32[]{:S(2)}) %collective-permute-start.13) | collective-permute-done | bytes 135200 | tf_op jit(solution)/shard_map/ppermute | solution.py:469
  49.5 1.5 %collective-permute-start.15 = (bf16[528,128]{1,0:T(8,128)(2,1)S(1)}, bf16[528,128]{1,0:T(8,128)(2,1)S(1)}, u32[]{:S(2)}, u32[]{:S(2)}) collective-permute-start(bf16[528,128]{1,0:T(8,128)(2,1)S(1)} %collective-permute-done.13.refs_2_), channel_id=1, source_target_pairs={{0,32},{16,240},{32,64},{48,16},{64,96},{80,48},{96,128},{112,80},... | collective-permute-start | bytes 405512 | tf_op jit(solution)/shard_map/ppermute | solution.py:469
  51.0 0.3 collective-permute-done.14.refs_3_
  51.2 1.2 %collective-permute-start.16 = (bf16[528,128]{1,0:T(8,128)(2,1)S(1)}, bf16[528,128]{1,0:T(8,128)(2,1)S(1)}, u32[]{:S(2)}, u32[]{:S(2)}) collective-permute-start(bf16[528,128]{1,0:T(8,128)(2,1)S(1)} %collective-permute-done.14.refs_3_), channel_id=1, source_target_pairs={{0,32},{16,240},{32,64},{48,16},{64,96},{80,48},{96,128},{112,80},... | collective-permute-start | bytes 405512 | tf_op jit(solution)/shard_map/ppermute | solution.py:469
  52.4 1.0 %collective-permute-done.15.refs_5_ = bf16[528,128]{1,0:T(8,128)(2,1)S(1)} collective-permute-done((bf16[528,128]{1,0:T(8,128)(2,1)S(1)}, bf16[528,128]{1,0:T(8,128)(2,1)S(1)}, u32[]{:S(2)}, u32[]{:S(2)}) %collective-permute-start.15) | collective-permute-done | bytes 135200 | tf_op jit(solution)/shard_map/ppermute | solution.py:469
  53.4 1.7 %collective-permute-done.16.refs_6_ = bf16[528,128]{1,0:T(8,128)(2,1)S(1)} collective-permute-done((bf16[528,128]{1,0:T(8,128)(2,1)S(1)}, bf16[528,128]{1,0:T(8,128)(2,1)S(1)}, u32[]{:S(2)}, u32[]{:S(2)}) %collective-permute-start.16) | collective-permute-done | bytes 135200 | tf_op jit(solution)/shard_map/ppermute | solution.py:469
  55.1 4.8 %collective-permute-start.17 = (bf16[2112,128]{1,0:T(8,128)(2,1)S(1)}, bf16[2112,128]{1,0:T(8,128)(2,1)S(1)}, u32[]{:S(2)}, u32[]{:S(2)}) collective-permute-start(bf16[2112,128]{1,0:T(8,128)(2,1)S(1)} %pad_maximum_fusion), channel_id=1, source_target_pairs={{0,16},{16,0},{32,48},{48,32},{64,80},{80,64},{96,112},{112,96},{1... | collective-permute-start | bytes 1622024 | tf_op jit(solution)/shard_map/ppermute | solution.py:465
  59.9 0.3 collective-permute-start.18
  60.3 3.4 %collective-permute-start.20 = (bf16[528,128]{1,0:T(8,128)(2,1)S(1)}, bf16[528,128]{1,0:T(8,128)(2,1)S(1)}, u32[]{:S(2)}, u32[]{:S(2)}) collective-permute-start(bf16[528,128]{1,0:T(8,128)(2,1)S(1)} %collective-permute-done.15.refs_5_), channel_id=1, source_target_pairs={{0,64},{16,208},{32,96},{48,240},{64,128},{80,16},{96,160},{112,48... | collective-permute-start | bytes 405512 | tf_op jit(solution)/shard_map/ppermute | solution.py:469
  63.6 4.5 %shard_map.69 = (bf16[8,256,512]{2,1,0:T(8,128)(2,1)}, bf16[8,256,512]{2,1,0:T(8,128)(2,1)}, f32[1,128]{1,0:T(1,128)S(1)}, bf16[1,128]{1,0:T(2,128)(2,1)S(1)}) custom-call(s32[2]{0:T(128)S(1)} %pad_add_fusion.4.place_ref, f32[1,128]{1,0:T(1,128)S(1)} %broadcast_in_dim.69.peaks_ref, bf16[8,256,512]{2,1,0:T(8,128)(2,1)S(1)} %copy-done.2, ...), custom_call_target="tpu_custom_call" | custom-call | flops 671088640 | bytes 6594560 | tf_op jit(solution)/shard_map/pallas_call | solution.py:396
  68.2 0.1 maximum_add_fusion
  68.2 2.5 %collective-permute-start.21 = (bf16[1584,128]{1,0:T(8,128)(2,1)S(1)}, bf16[1584,128]{1,0:T(8,128)(2,1)S(1)}, u32[]{:S(2)}, u32[]{:S(2)}) collective-permute-start(bf16[1584,128]{1,0:T(8,128)(2,1)S(1)} %maximum_add_fusion), channel_id=1, source_target_pairs={{0,16},{16,0},{32,48},{48,32},{64,80},{80,64},{96,112},{112,96},{1... | collective-permute-start | bytes 1216520 | tf_op jit(solution)/shard_map/ppermute | solution.py:465
  70.8 1.8 %shard_map.70 = (bf16[8,256,512]{2,1,0:T(8,128)(2,1)}, bf16[8,256,512]{2,1,0:T(8,128)(2,1)}, f32[1,128]{1,0:T(1,128)}, bf16[1,128]{1,0:T(2,128)(2,1)}) custom-call(s32[2]{0:T(128)S(1)} %pad_add_fusion.4.place_ref, f32[1,128]{1,0:T(1,128)S(1)} %get-tuple-element.52.peaks_ref, ...), custom_call_target="tpu_custom_call", output_to_operand_aliasing={{0}: (6, {}), {1}: (7, {})} | custom-call | flops 134217728 | bytes 1318912 | tf_op jit(solution)/shard_map/pallas_call | solution.py:396
  72.5 2.4 %shard_map.71 = (bf16[8,256,512]{2,1,0:T(8,128)(2,1)}, bf16[8,256,512]{2,1,0:T(8,128)(2,1)}, f32[1,128]{1,0:T(1,128)}, bf16[1,128]{1,0:T(2,128)(2,1)}) custom-call(s32[2]{0:T(128)S(1)} %pad_add_fusion.4.place_ref, f32[1,128]{1,0:T(1,128)S(1)} %get-tuple-element.52.peaks_ref, ...), custom_call_target="tpu_custom_call", output_to_operand_aliasing={{0}: (6, {}), {1}: (7, {})} | custom-call | flops 268435456 | bytes 2637824 | tf_op jit(solution)/shard_map/pallas_call | solution.py:396
  (30 shorter events, 0.4 us)
Async XLA Ops:
  0.6 16.4 %copy-start = (f32[1,64,32]{1,2,0:T(8,128)S(1)}, f32[1,64,32]{1,2,0:T(8,128)}, u32[]{:S(2)}) copy-start(f32[1,64,32]{1,2,0:T(8,128)} %param.7) | copy-start | bytes 24580
  6.3 4.7 %collective-permute-start.1 = (bf16[1632,128]{1,0:T(8,128)(2,1)S(1)}, bf16[1632,128]{1,0:T(8,128)(2,1)S(1)}, u32[]{:S(2)}, u32[]{:S(2)}) collective-permute-start(bf16[1632,128]{1,0:T(8,128)(2,1)S(1)} %get-tuple-element.38), channel_id=1, source_target_pairs={{0,16},{16,0},{32,48},{48,32},{64,80},{80,64},{96,112},{112,96},{1... | collective-permute-start | bytes 1253384 | tf_op jit(solution)/shard_map/ppermute | solution.py:465
  9.7 13.9 %collective-permute-start = (bf16[2,1088,128]{2,1,0:T(8,128)(2,1)S(1)}, bf16[2,1088,128]{2,1,0:T(8,128)(2,1)S(1)}, u32[]{:S(2)}, u32[]{:S(2)}) collective-permute-start(bf16[2,1088,128]{2,1,0:T(8,128)(2,1)S(1)} %get-tuple-element.34), channel_id=1, source_target_pairs={{0,16},{16,0},{32,48},{48,32},{64,80},{80,64},{96,112},{112,96},{1... | collective-permute-start | bytes 1671176 | tf_op jit(solution)/shard_map/ppermute | solution.py:465
  11.2 10.7 %collective-permute-start.3 = (bf16[544,128]{1,0:T(8,128)(2,1)S(1)}, bf16[544,128]{1,0:T(8,128)(2,1)S(1)}, u32[]{:S(2)}, u32[]{:S(2)}) collective-permute-start(bf16[544,128]{1,0:T(8,128)(2,1)S(1)} %get-tuple-element.40), channel_id=1, source_target_pairs={{0,64},{16,208},{32,96},{48,240},{64,128},{80,16},{96,160},{112,48... | collective-permute-start | bytes 417800 | tf_op jit(solution)/shard_map/ppermute | solution.py:469
  15.5 6.4 %collective-permute-start.4 = (bf16[544,128]{1,0:T(8,128)(2,1)S(1)}, bf16[544,128]{1,0:T(8,128)(2,1)S(1)}, u32[]{:S(2)}, u32[]{:S(2)}) collective-permute-start(bf16[544,128]{1,0:T(8,128)(2,1)S(1)} %get-tuple-element.41), channel_id=1, source_target_pairs={{0,32},{16,240},{32,64},{48,16},{64,96},{80,48},{96,128},{112,80},... | collective-permute-start | bytes 417800 | tf_op jit(solution)/shard_map/ppermute | solution.py:469
  16.3 6.1 %collective-permute-start.5 = (bf16[544,128]{1,0:T(8,128)(2,1)S(1)}, bf16[544,128]{1,0:T(8,128)(2,1)S(1)}, u32[]{:S(2)}, u32[]{:S(2)}) collective-permute-start(bf16[544,128]{1,0:T(8,128)(2,1)S(1)} %get-tuple-element.42), channel_id=1, source_target_pairs={{0,32},{16,240},{32,64},{48,16},{64,96},{80,48},{96,128},{112,80},... | collective-permute-start | bytes 417800 | tf_op jit(solution)/shard_map/ppermute | solution.py:469
  17.1 4.6 %collective-permute-start.2 = (f32[4,32]{1,0:T(4,128)S(1)}, f32[4,32]{1,0:T(4,128)S(1)}, u32[]{:S(2)}, u32[]{:S(2)}) collective-permute-start(f32[4,32]{1,0:T(4,128)S(1)} %bitcast.38), channel_id=1, source_target_pairs={{0,0},{1,1},{2,2},{3,3},{4,4},{5,5},{6,6},{7,7},{8,8},{9,9},{10,10... | collective-permute-start | bytes 1544 | tf_op jit(solution)/shard_map/ppermute | solution.py:438
  22.5 5.7 %collective-permute-start.7 = (bf16[64,128]{1,0:T(8,128)(2,1)S(1)}, bf16[64,128]{1,0:T(8,128)(2,1)S(1)}, u32[]{:S(2)}, u32[]{:S(2)}) collective-permute-start(bf16[64,128]{1,0:T(8,128)(2,1)S(1)} %select_convert_fusion), channel_id=1, source_target_pairs={{0,16},{16,0},{32,48},{48,32},{64,80},{80,64},{96,112},{112,96},{1... | collective-permute-start | bytes 49160 | tf_op jit(solution)/shard_map/ppermute | solution.py:465
  23.8 6.3 %collective-permute-start.6 = (bf16[544,128]{1,0:T(8,128)(2,1)S(1)}, bf16[544,128]{1,0:T(8,128)(2,1)S(1)}, u32[]{:S(2)}, u32[]{:S(2)}) collective-permute-start(bf16[544,128]{1,0:T(8,128)(2,1)S(1)} %fusion), channel_id=1, source_target_pairs={{0,32},{16,240},{32,64},{48,16},{64,96},{80,48},{96,128},{112,80},... | collective-permute-start | bytes 417800 | tf_op jit(solution)/shard_map/ppermute | solution.py:469
  28.1 5.2 %collective-permute-start.9 = (bf16[544,128]{1,0:T(8,128)(2,1)S(1)}, bf16[544,128]{1,0:T(8,128)(2,1)S(1)}, u32[]{:S(2)}, u32[]{:S(2)}) collective-permute-start(bf16[544,128]{1,0:T(8,128)(2,1)S(1)} %fusion.2), channel_id=1, source_target_pairs={{0,32},{16,240},{32,64},{48,16},{64,96},{80,48},{96,128},{112,80},... | collective-permute-start | bytes 417800 | tf_op jit(solution)/shard_map/ppermute | solution.py:469
  30.1 5.2 %collective-permute-start.8 = (bf16[544,128]{1,0:T(8,128)(2,1)S(1)}, bf16[544,128]{1,0:T(8,128)(2,1)S(1)}, u32[]{:S(2)}, u32[]{:S(2)}) collective-permute-start(bf16[544,128]{1,0:T(8,128)(2,1)S(1)} %add_convert_fusion.1), channel_id=1, source_target_pairs={{0,32},{16,240},{32,64},{48,16},{64,96},{80,48},{96,128},{112,80},... | collective-permute-start | bytes 417800 | tf_op jit(solution)/shard_map/ppermute | solution.py:469
  33.3 4.0 %collective-permute-start.10 = (bf16[544,128]{1,0:T(8,128)(2,1)S(1)}, bf16[544,128]{1,0:T(8,128)(2,1)S(1)}, u32[]{:S(2)}, u32[]{:S(2)}) collective-permute-start(bf16[544,128]{1,0:T(8,128)(2,1)S(1)} %add_convert_fusion), channel_id=1, source_target_pairs={{0,32},{16,240},{32,64},{48,16},{64,96},{80,48},{96,128},{112,80},... | collective-permute-start | bytes 417800 | tf_op jit(solution)/shard_map/ppermute | solution.py:469
  37.4 3.6 %collective-permute-start.11 = (bf16[544,128]{1,0:T(8,128)(2,1)S(1)}, bf16[544,128]{1,0:T(8,128)(2,1)S(1)}, u32[]{:S(2)}, u32[]{:S(2)}) collective-permute-start(bf16[544,128]{1,0:T(8,128)(2,1)S(1)} %get-tuple-element.69.mine_first), channel_id=1, source_target_pairs={{0,16},{16,0},{32,48},{48,32},{64,80},{80,64},{96,112},{112,96},{1... | collective-permute-start | bytes 417800 | tf_op jit(solution)/shard_map/ppermute | solution.py:465
  40.1 1.4 %collective-permute-start.12 = (bf16[544,128]{1,0:T(8,128)(2,1)S(1)}, bf16[544,128]{1,0:T(8,128)(2,1)S(1)}, u32[]{:S(2)}, u32[]{:S(2)}) collective-permute-start(bf16[544,128]{1,0:T(8,128)(2,1)S(1)} %get-tuple-element.68.mine_second), channel_id=1, source_target_pairs={{0,16},{16,0},{32,48},{48,32},{64,80},{80,64},{96,112},{112,96},{1... | collective-permute-start | bytes 417800 | tf_op jit(solution)/shard_map/ppermute | solution.py:465
  41.4 22.2 %copy-start.1 = (bf16[4,2,256,512]{3,2,1,0:T(8,128)(2,1)S(1)}, bf16[4,2,256,512]{3,2,1,0:T(8,128)(2,1)}, u32[]{:S(2)}) copy-start(bf16[4,2,256,512]{3,2,1,0:T(8,128)(2,1)} %param.6) | copy-start | bytes 6291460
  41.4 22.2 %copy-start.2 = (bf16[8,256,512]{2,1,0:T(8,128)(2,1)S(1)}, bf16[8,256,512]{2,1,0:T(8,128)(2,1)}, u32[]{:S(2)}) copy-start(bf16[8,256,512]{2,1,0:T(8,128)(2,1)} %get-tuple-element.32.advance_ref) | copy-start | bytes 6291460
  45.5 3.9 %collective-permute-start.13 = (bf16[528,128]{1,0:T(8,128)(2,1)S(1)}, bf16[528,128]{1,0:T(8,128)(2,1)S(1)}, u32[]{:S(2)}, u32[]{:S(2)}) collective-permute-start(bf16[528,128]{1,0:T(8,128)(2,1)S(1)} %get-tuple-element.50.refs_0_), channel_id=1, source_target_pairs={{0,32},{16,240},{32,64},{48,16},{64,96},{80,48},{96,128},{112,80},... | collective-permute-start | bytes 405512 | tf_op jit(solution)/shard_map/ppermute | solution.py:469
  45.9 5.4 %collective-permute-start.14 = (bf16[528,128]{1,0:T(8,128)(2,1)S(1)}, bf16[528,128]{1,0:T(8,128)(2,1)S(1)}, u32[]{:S(2)}, u32[]{:S(2)}) collective-permute-start(bf16[528,128]{1,0:T(8,128)(2,1)S(1)} %get-tuple-element.51.refs_1_), channel_id=1, source_target_pairs={{0,32},{16,240},{32,64},{48,16},{64,96},{80,48},{96,128},{112,80},... | collective-permute-start | bytes 405512 | tf_op jit(solution)/shard_map/ppermute | solution.py:469
  49.5 3.9 %collective-permute-start.15 = (bf16[528,128]{1,0:T(8,128)(2,1)S(1)}, bf16[528,128]{1,0:T(8,128)(2,1)S(1)}, u32[]{:S(2)}, u32[]{:S(2)}) collective-permute-start(bf16[528,128]{1,0:T(8,128)(2,1)S(1)} %collective-permute-done.13.refs_2_), channel_id=1, source_target_pairs={{0,32},{16,240},{32,64},{48,16},{64,96},{80,48},{96,128},{112,80},... | collective-permute-start | bytes 405512 | tf_op jit(solution)/shard_map/ppermute | solution.py:469
  51.2 3.9 %collective-permute-start.16 = (bf16[528,128]{1,0:T(8,128)(2,1)S(1)}, bf16[528,128]{1,0:T(8,128)(2,1)S(1)}, u32[]{:S(2)}, u32[]{:S(2)}) collective-permute-start(bf16[528,128]{1,0:T(8,128)(2,1)S(1)} %collective-permute-done.14.refs_3_), channel_id=1, source_target_pairs={{0,32},{16,240},{32,64},{48,16},{64,96},{80,48},{96,128},{112,80},... | collective-permute-start | bytes 405512 | tf_op jit(solution)/shard_map/ppermute | solution.py:469
  55.1 8.5 %collective-permute-start.17 = (bf16[2112,128]{1,0:T(8,128)(2,1)S(1)}, bf16[2112,128]{1,0:T(8,128)(2,1)S(1)}, u32[]{:S(2)}, u32[]{:S(2)}) collective-permute-start(bf16[2112,128]{1,0:T(8,128)(2,1)S(1)} %pad_maximum_fusion), channel_id=1, source_target_pairs={{0,16},{16,0},{32,48},{48,32},{64,80},{80,64},{96,112},{112,96},{1... | collective-permute-start | bytes 1622024 | tf_op jit(solution)/shard_map/ppermute | solution.py:465
  59.9 8.2 %collective-permute-start.18 = (bf16[528,128]{1,0:T(8,128)(2,1)S(1)}, bf16[528,128]{1,0:T(8,128)(2,1)S(1)}, u32[]{:S(2)}, u32[]{:S(2)}) collective-permute-start(bf16[528,128]{1,0:T(8,128)(2,1)S(1)} %collective-permute-done.15.refs_5_), channel_id=1, source_target_pairs={{0,32},{16,240},{32,64},{48,16},{64,96},{80,48},{96,128},{112,80},... | collective-permute-start | bytes 405512 | tf_op jit(solution)/shard_map/ppermute | solution.py:469
  60.2 7.9 %collective-permute-start.19 = (bf16[528,128]{1,0:T(8,128)(2,1)S(1)}, bf16[528,128]{1,0:T(8,128)(2,1)S(1)}, u32[]{:S(2)}, u32[]{:S(2)}) collective-permute-start(bf16[528,128]{1,0:T(8,128)(2,1)S(1)} %collective-permute-done.16.refs_6_), channel_id=1, source_target_pairs={{0,32},{16,240},{32,64},{48,16},{64,96},{80,48},{96,128},{112,80},... | collective-permute-start | bytes 405512 | tf_op jit(solution)/shard_map/ppermute | solution.py:469
  60.3 7.9 %collective-permute-start.20 = (bf16[528,128]{1,0:T(8,128)(2,1)S(1)}, bf16[528,128]{1,0:T(8,128)(2,1)S(1)}, u32[]{:S(2)}, u32[]{:S(2)}) collective-permute-start(bf16[528,128]{1,0:T(8,128)(2,1)S(1)} %collective-permute-done.15.refs_5_), channel_id=1, source_target_pairs={{0,64},{16,208},{32,96},{48,240},{64,128},{80,16},{96,160},{112,48... | collective-permute-start | bytes 405512 | tf_op jit(solution)/shard_map/ppermute | solution.py:469
  68.2 4.3 %collective-permute-start.21 = (bf16[1584,128]{1,0:T(8,128)(2,1)S(1)}, bf16[1584,128]{1,0:T(8,128)(2,1)S(1)}, u32[]{:S(2)}, u32[]{:S(2)}) collective-permute-start(bf16[1584,128]{1,0:T(8,128)(2,1)S(1)} %maximum_add_fusion), channel_id=1, source_target_pairs={{0,16},{16,0},{32,48},{48,32},{64,80},{80,64},{96,112},{112,96},{1... | collective-permute-start | bytes 1216520 | tf_op jit(solution)/shard_map/ppermute | solution.py:465

commit v7 on v6

--- a/solution.py
+++ b/solution.py
@@ -540,13 +540,14 @@
         ],
         None,
     )
-    other_remote = swap(jnp.concatenate([*pieces[3], far], axis=0) + after)
-    results, _, _ = final(peaks, [([(half, 0) for half in pieces[3]], 3, True)], results)
+    other_remote = swap(jnp.concatenate(pieces[3], axis=0) + after)
+    results, _, after = final(peaks, [([(half, 0) for half in pieces[3]], 3, True)], results)
+    other_far = swap(far + after)
     (new_weights, updates), _, _ = final(
         peaks,
         [
             ([(other_remote, 0), (other_remote, HALF)], 3, False),
-            ([(far, 0), (other_remote, 2 * HALF)], 4, True),
+            ([(far, 0), (other_far, 0)], 4, True),
         ],
         results,
     )

time: 75.1 us -> 75 us (level)
  starting transfers between devices: 39.4 us -> 38 us
  waiting for transfers between devices: 15.1 us -> 16.4 us
    ppermute x7 -> x8, starting transfers between devices: 14.6 us -> 13.2 us  [swap(): return lax.ppermute(value, 'dp', swap_pairs)]
    ppermute x7 -> x8, waiting for transfers between devices: 2.29 us -> 3.62 us  [swap(): return lax.ppermute(value, 'dp', swap_pairs)]
  transfers between devices with their start and end apart: 22 -> 23, of which waited for: 12 -> 13; matrix products, arithmetic and copies ran while one was open for 1% -> 1% of each run, Pallas kernels for 8% -> 8%
where the time goes in v7:
time: 75 us; the launch traced here: 74.9 us
  starting transfers between devices  38 us (51%)
  Pallas kernels  18.5 us (25%)
  waiting for transfers between devices  16.4 us (22%)
  other arithmetic  0.91 us (1%)
  between operations  0.82 us (1%)
    ppermute x14, starting transfers between devices, onward(): return lax.ppermute(value, 'dp', pairs)  21.5 us
    ppermute x8, starting transfers between devices, swap(): return lax.ppermute(value, 'dp', swap_pairs)  13.2 us
    ppermute x14, waiting for transfers between devices, onward(): return lax.ppermute(value, 'dp', pairs)  11.4 us
    pallas_call x3, Pallas kernels, finish(): pl.pallas_call(kernel, out_shape=(shape, shape, jax.ShapeDtypeStruct((1,...  8.69 us
    pallas_call x1, Pallas kernels, grams(): pl.pallas_call(gram_kernel, out_shape=(full, full, shape(3, GRAM_ROWS, SI...  5.69 us
    pallas_call x1, Pallas kernels, polynomial(): pl.pallas_call(polynomial_kernel, out_shape=(half, half), in_specs=[pl.Bl...  4.12 us
    ppermute x8, waiting for transfers between devices, swap(): return lax.ppermute(value, 'dp', swap_pairs)  3.62 us
    ppermute x1, starting transfers between devices, observed(): return lax.ppermute(sent, ('dp', 'mp'), pairs).reshape(1, -1)  3.2 us
  transfers between devices with their start and end apart: 23, of which 13 were waited for; matrix products, arithmetic and copies ran while one was open for 1% of the time, Pallas kernels for 8%

profile of v7, /device:TPU:1, one launch (start us, length us, event | category | flops | bytes accessed | tf_op | source)
XLA Modules:
  0.0 74.9 jit_solution(416372205545336764)
XLA Ops:
  0.6 5.7 %shard_map.67 = (bf16[8,256,512]{2,1,0:T(8,128)(2,1)}, bf16[8,256,512]{2,1,0:T(8,128)(2,1)}, bf16[3,1088,128]{2,1,0:T(8,128)(2,1)S(1)}, bf16[2,1088,128]{2,1,0:T...) custom-call(bf16[8,256,512]{2,1,0:T(8,128)(2,1)} %bitcast.38, ...), custom_call_target="tpu_custom_call" | custom-call | flops 1073741824 | bytes 10485760 | tf_op jit(solution)/shard_map/pallas_call | solution.py:214
  6.3 3.3 %collective-permute-start.1 = (bf16[1632,128]{1,0:T(8,128)(2,1)S(1)}, bf16[1632,128]{1,0:T(8,128)(2,1)S(1)}, u32[]{:S(2)}, u32[]{:S(2)}) collective-permute-start(bf16[1632,128]{1,0:T(8,128)(2,1)S(1)} %get-tuple-element.39), channel_id=1, source_target_pairs={{0,16},{16,0},{32,48},{48,32},{64,80},{80,64},{96,112},{112,96},{1... | collective-permute-start | bytes 1253384 | tf_op jit(solution)/shard_map/ppermute | solution.py:465
  9.7 0.1 collective-permute-start
  9.8 1.3 %collective-permute-done.1 = bf16[1632,128]{1,0:T(8,128)(2,1)S(1)} collective-permute-done((bf16[1632,128]{1,0:T(8,128)(2,1)S(1)}, bf16[1632,128]{1,0:T(8,128)(2,1)S(1)}, u32[]{:S(2)}, u32[]{:S(2)}) %collective-permute-start.1) | collective-permute-done | bytes 417824 | tf_op jit(solution)/shard_map/ppermute | solution.py:465
  11.1 0.1 fusion.4
  11.2 4.4 %collective-permute-start.3 = (bf16[544,128]{1,0:T(8,128)(2,1)S(1)}, bf16[544,128]{1,0:T(8,128)(2,1)S(1)}, u32[]{:S(2)}, u32[]{:S(2)}) collective-permute-start(bf16[544,128]{1,0:T(8,128)(2,1)S(1)} %get-tuple-element.41), channel_id=1, source_target_pairs={{0,64},{16,208},{32,96},{48,240},{64,128},{80,16},{96,160},{112,48... | collective-permute-start | bytes 417800 | tf_op jit(solution)/shard_map/ppermute | solution.py:469
  15.5 0.7 collective-permute-start.4
  16.3 0.7 collective-permute-start.5
  17.1 0.1 copy.11
  17.1 3.2 %collective-permute-start.2 = (f32[4,32]{1,0:T(4,128)S(1)}, f32[4,32]{1,0:T(4,128)S(1)}, u32[]{:S(2)}, u32[]{:S(2)}) collective-permute-start(f32[4,32]{1,0:T(4,128)S(1)} %bitcast.40), channel_id=1, source_target_pairs={{0,0},{1,1},{2,2},{3,3},{4,4},{5,5},{6,6},{7,7},{8,8},{9,9},{10,10... | collective-permute-start | bytes 1544 | tf_op jit(solution)/shard_map/ppermute | solution.py:438
  20.4 1.4 %collective-permute-done.2 = f32[4,32]{1,0:T(4,128)S(1)} collective-permute-done((f32[4,32]{1,0:T(4,128)S(1)}, f32[4,32]{1,0:T(4,128)S(1)}, u32[]{:S(2)}, u32[]{:S(2)}) %collective-permute-start.2) | collective-permute-done | bytes 544 | tf_op jit(solution)/shard_map/ppermute | solution.py:438
  21.8 0.1 reshape.112
  21.9 0.4 collective-permute-done.5
  22.4 0.1 select_convert_fusion
  22.5 1.0 %collective-permute-start.7 = (bf16[64,128]{1,0:T(8,128)(2,1)S(1)}, bf16[64,128]{1,0:T(8,128)(2,1)S(1)}, u32[]{:S(2)}, u32[]{:S(2)}) collective-permute-start(bf16[64,128]{1,0:T(8,128)(2,1)S(1)} %select_convert_fusion), channel_id=1, source_target_pairs={{0,16},{16,0},{32,48},{48,32},{64,80},{80,64},{96,112},{112,96},{1... | collective-permute-start | bytes 49160 | tf_op jit(solution)/shard_map/ppermute | solution.py:465
  23.5 0.1 convert_select_fusion.2
  23.6 0.1 add_bitcast_fusion
  23.8 4.3 %collective-permute-start.6 = (bf16[544,128]{1,0:T(8,128)(2,1)S(1)}, bf16[544,128]{1,0:T(8,128)(2,1)S(1)}, u32[]{:S(2)}, u32[]{:S(2)}) collective-permute-start(bf16[544,128]{1,0:T(8,128)(2,1)S(1)} %fusion), channel_id=1, source_target_pairs={{0,32},{16,240},{32,64},{48,16},{64,96},{80,48},{96,128},{112,80},... | collective-permute-start | bytes 417800 | tf_op jit(solution)/shard_map/ppermute | solution.py:469
  28.1 0.1 collective-permute-start.9
  28.2 1.9 %collective-permute-done.6 = bf16[544,128]{1,0:T(8,128)(2,1)S(1)} collective-permute-done((bf16[544,128]{1,0:T(8,128)(2,1)S(1)}, bf16[544,128]{1,0:T(8,128)(2,1)S(1)}, u32[]{:S(2)}, u32[]{:S(2)}) %collective-permute-start.6) | collective-permute-done | bytes 139296 | tf_op jit(solution)/shard_map/ppermute | solution.py:469
  30.1 3.2 %collective-permute-start.8 = (bf16[544,128]{1,0:T(8,128)(2,1)S(1)}, bf16[544,128]{1,0:T(8,128)(2,1)S(1)}, u32[]{:S(2)}, u32[]{:S(2)}) collective-permute-start(bf16[544,128]{1,0:T(8,128)(2,1)S(1)} %add_convert_fusion.1), channel_id=1, source_target_pairs={{0,32},{16,240},{32,64},{48,16},{64,96},{80,48},{96,128},{112,80},... | collective-permute-start | bytes 417800 | tf_op jit(solution)/shard_map/ppermute | solution.py:469
  33.3 1.5 %collective-permute-start.10 = (bf16[544,128]{1,0:T(8,128)(2,1)S(1)}, bf16[544,128]{1,0:T(8,128)(2,1)S(1)}, u32[]{:S(2)}, u32[]{:S(2)}) collective-permute-start(bf16[544,128]{1,0:T(8,128)(2,1)S(1)} %add_convert_fusion), channel_id=1, source_target_pairs={{0,32},{16,240},{32,64},{48,16},{64,96},{80,48},{96,128},{112,80},... | collective-permute-start | bytes 417800 | tf_op jit(solution)/shard_map/ppermute | solution.py:469
  34.7 0.5 collective-permute-done.8
  35.3 2.1 %collective-permute-done.10 = bf16[544,128]{1,0:T(8,128)(2,1)S(1)} collective-permute-done((bf16[544,128]{1,0:T(8,128)(2,1)S(1)}, bf16[544,128]{1,0:T(8,128)(2,1)S(1)}, u32[]{:S(2)}, u32[]{:S(2)}) %collective-permute-start.10) | collective-permute-done | bytes 139296 | tf_op jit(solution)/shard_map/ppermute | solution.py:469
  37.3 0.1 fusion.3
  37.4 2.6 %collective-permute-start.11 = (bf16[544,128]{1,0:T(8,128)(2,1)S(1)}, bf16[544,128]{1,0:T(8,128)(2,1)S(1)}, u32[]{:S(2)}, u32[]{:S(2)}) collective-permute-start(bf16[544,128]{1,0:T(8,128)(2,1)S(1)} %get-tuple-element.71.mine_first), channel_id=1, source_target_pairs={{0,16},{16,0},{32,48},{48,32},{64,80},{80,64},{96,112},{112,96},{1... | collective-permute-start | bytes 417800 | tf_op jit(solution)/shard_map/ppermute | solution.py:465
  40.1 0.3 collective-permute-start.12
  40.3 0.1 pad_add_fusion.4.place_ref
  40.4 0.6 collective-permute-done.11.theirs_first
  41.1 0.4 collective-permute-done.12.theirs_second
  41.4 4.1 %shard_map.68 = (bf16[528,128]{1,0:T(8,128)(2,1)S(1)}, bf16[528,128]{1,0:T(8,128)(2,1)S(1)}) custom-call(s32[2]{0:T(128)S(1)} %pad_add_fusion.4.place_ref, bf16[544,128]{1,0:T(8,128)(2,1)S(1)} %get-tuple-element.71.mine_first, bf16[544,128]{1,0:T(8,128)(2,1)S(1)} %get-tuple-element.70.mine_second, bf16[544,128]{1,0:T(8,128)(2,1)S(1)} %collective-permute-done.11.theirs_first, ...), custom_call_target="tpu_custom_call" | custom-call | flops 2415919104 | bytes 811008 | tf_op jit(solution)/shard_map/pallas_call | solution.py:289
  45.5 0.3 collective-permute-start.13
  45.9 0.1 collective-permute-start.14
  46.0 3.5 %collective-permute-done.13.refs_2_ = bf16[528,128]{1,0:T(8,128)(2,1)S(1)} collective-permute-done((bf16[528,128]{1,0:T(8,128)(2,1)S(1)}, bf16[528,128]{1,0:T(8,128)(2,1)S(1)}, u32[]{:S(2)}, u32[]{:S(2)}) %collective-permute-start.13) | collective-permute-done | bytes 135200 | tf_op jit(solution)/shard_map/ppermute | solution.py:469
  49.5 1.5 %collective-permute-start.15 = (bf16[528,128]{1,0:T(8,128)(2,1)S(1)}, bf16[528,128]{1,0:T(8,128)(2,1)S(1)}, u32[]{:S(2)}, u32[]{:S(2)}) collective-permute-start(bf16[528,128]{1,0:T(8,128)(2,1)S(1)} %collective-permute-done.13.refs_2_), channel_id=1, source_target_pairs={{0,32},{16,240},{32,64},{48,16},{64,96},{80,48},{96,128},{112,80},... | collective-permute-start | bytes 405512 | tf_op jit(solution)/shard_map/ppermute | solution.py:469
  51.0 0.3 collective-permute-done.14.refs_3_
  51.2 1.2 %collective-permute-start.16 = (bf16[528,128]{1,0:T(8,128)(2,1)S(1)}, bf16[528,128]{1,0:T(8,128)(2,1)S(1)}, u32[]{:S(2)}, u32[]{:S(2)}) collective-permute-start(bf16[528,128]{1,0:T(8,128)(2,1)S(1)} %collective-permute-done.14.refs_3_), channel_id=1, source_target_pairs={{0,32},{16,240},{32,64},{48,16},{64,96},{80,48},{96,128},{112,80},... | collective-permute-start | bytes 405512 | tf_op jit(solution)/shard_map/ppermute | solution.py:469
  52.4 1.0 %collective-permute-done.15.refs_5_ = bf16[528,128]{1,0:T(8,128)(2,1)S(1)} collective-permute-done((bf16[528,128]{1,0:T(8,128)(2,1)S(1)}, bf16[528,128]{1,0:T(8,128)(2,1)S(1)}, u32[]{:S(2)}, u32[]{:S(2)}) %collective-permute-start.15) | collective-permute-done | bytes 135200 | tf_op jit(solution)/shard_map/ppermute | solution.py:469
  53.4 1.7 %collective-permute-done.16.refs_6_ = bf16[528,128]{1,0:T(8,128)(2,1)S(1)} collective-permute-done((bf16[528,128]{1,0:T(8,128)(2,1)S(1)}, bf16[528,128]{1,0:T(8,128)(2,1)S(1)}, u32[]{:S(2)}, u32[]{:S(2)}) %collective-permute-start.16) | collective-permute-done | bytes 135200 | tf_op jit(solution)/shard_map/ppermute | solution.py:469
  55.1 4.8 %collective-permute-start.17 = (bf16[2112,128]{1,0:T(8,128)(2,1)S(1)}, bf16[2112,128]{1,0:T(8,128)(2,1)S(1)}, u32[]{:S(2)}, u32[]{:S(2)}) collective-permute-start(bf16[2112,128]{1,0:T(8,128)(2,1)S(1)} %pad_maximum_fusion), channel_id=1, source_target_pairs={{0,16},{16,0},{32,48},{48,32},{64,80},{80,64},{96,112},{112,96},{1... | collective-permute-start | bytes 1622024 | tf_op jit(solution)/shard_map/ppermute | solution.py:465
  59.9 0.3 collective-permute-start.18
  60.3 3.4 %collective-permute-start.21 = (bf16[528,128]{1,0:T(8,128)(2,1)S(1)}, bf16[528,128]{1,0:T(8,128)(2,1)S(1)}, u32[]{:S(2)}, u32[]{:S(2)}) collective-permute-start(bf16[528,128]{1,0:T(8,128)(2,1)S(1)} %collective-permute-done.15.refs_5_), channel_id=1, source_target_pairs={{0,64},{16,208},{32,96},{48,240},{64,128},{80,16},{96,160},{112,48... | collective-permute-start | bytes 405512 | tf_op jit(solution)/shard_map/ppermute | solution.py:469
  63.6 4.5 %shard_map.69 = (bf16[8,256,512]{2,1,0:T(8,128)(2,1)}, bf16[8,256,512]{2,1,0:T(8,128)(2,1)}, f32[1,128]{1,0:T(1,128)S(1)}, bf16[1,128]{1,0:T(2,128)(2,1)S(1)}) custom-call(s32[2]{0:T(128)S(1)} %pad_add_fusion.4.place_ref, f32[1,128]{1,0:T(1,128)S(1)} %broadcast_in_dim.69.peaks_ref, bf16[8,256,512]{2,1,0:T(8,128)(2,1)S(1)} %copy-done.2, ...), custom_call_target="tpu_custom_call" | custom-call | flops 671088640 | bytes 6594560 | tf_op jit(solution)/shard_map/pallas_call | solution.py:396
  68.2 1.0 %collective-permute-start.20 = (bf16[1056,128]{1,0:T(8,128)(2,1)S(1)}, bf16[1056,128]{1,0:T(8,128)(2,1)S(1)}, u32[]{:S(2)}, u32[]{:S(2)}) collective-permute-start(bf16[1056,128]{1,0:T(8,128)(2,1)S(1)} %maximum_add_fusion), channel_id=1, source_target_pairs={{0,16},{16,0},{32,48},{48,32},{64,80},{80,64},{96,112},{112,96},{1... | collective-permute-start | bytes 811016 | tf_op jit(solution)/shard_map/ppermute | solution.py:465
  69.2 1.8 %shard_map.70 = (bf16[8,256,512]{2,1,0:T(8,128)(2,1)}, bf16[8,256,512]{2,1,0:T(8,128)(2,1)}, f32[1,128]{1,0:T(1,128)}, bf16[1,128]{1,0:T(2,128)(2,1)S(1)}) custom-call(s32[2]{0:T(128)S(1)} %pad_add_fusion.4.place_ref, f32[1,128]{1,0:T(1,128)S(1)} %get-tuple-element.53.peaks_ref, ...), custom_call_target="tpu_custom_call", output_to_operand_aliasing={{0}: (6, {}), {1}: (7, {})} | custom-call | flops 134217728 | bytes 1318912 | tf_op jit(solution)/shard_map/pallas_call | solution.py:396
  71.0 0.1 collective-permute-start.22
  71.1 1.3 %collective-permute-done.22.refs_2_ = bf16[528,128]{1,0:T(8,128)(2,1)S(1)} collective-permute-done((bf16[528,128]{1,0:T(8,128)(2,1)S(1)}, bf16[528,128]{1,0:T(8,128)(2,1)S(1)}, u32[]{:S(2)}, u32[]{:S(2)}) %collective-permute-start.22) | collective-permute-done | bytes 135200 | tf_op jit(solution)/shard_map/ppermute | solution.py:465
  72.5 2.4 %shard_map.71 = (bf16[8,256,512]{2,1,0:T(8,128)(2,1)}, bf16[8,256,512]{2,1,0:T(8,128)(2,1)}, f32[1,128]{1,0:T(1,128)}, bf16[1,128]{1,0:T(2,128)(2,1)}) custom-call(s32[2]{0:T(128)S(1)} %pad_add_fusion.4.place_ref, f32[1,128]{1,0:T(1,128)S(1)} %get-tuple-element.53.peaks_ref, ...), custom_call_target="tpu_custom_call", output_to_operand_aliasing={{0}: (7, {}), {1}: (8, {})} | custom-call | flops 268435456 | bytes 2637824 | tf_op jit(solution)/shard_map/pallas_call | solution.py:396
  (33 shorter events, 0.5 us)
Async XLA Ops:
  0.6 16.4 %copy-start = (f32[1,64,32]{1,2,0:T(8,128)S(1)}, f32[1,64,32]{1,2,0:T(8,128)}, u32[]{:S(2)}) copy-start(f32[1,64,32]{1,2,0:T(8,128)} %param.7) | copy-start | bytes 24580
  6.3 4.7 %collective-permute-start.1 = (bf16[1632,128]{1,0:T(8,128)(2,1)S(1)}, bf16[1632,128]{1,0:T(8,128)(2,1)S(1)}, u32[]{:S(2)}, u32[]{:S(2)}) collective-permute-start(bf16[1632,128]{1,0:T(8,128)(2,1)S(1)} %get-tuple-element.39), channel_id=1, source_target_pairs={{0,16},{16,0},{32,48},{48,32},{64,80},{80,64},{96,112},{112,96},{1... | collective-permute-start | bytes 1253384 | tf_op jit(solution)/shard_map/ppermute | solution.py:465
  9.7 13.9 %collective-permute-start = (bf16[2,1088,128]{2,1,0:T(8,128)(2,1)S(1)}, bf16[2,1088,128]{2,1,0:T(8,128)(2,1)S(1)}, u32[]{:S(2)}, u32[]{:S(2)}) collective-permute-start(bf16[2,1088,128]{2,1,0:T(8,128)(2,1)S(1)} %get-tuple-element.35), channel_id=1, source_target_pairs={{0,16},{16,0},{32,48},{48,32},{64,80},{80,64},{96,112},{112,96},{1... | collective-permute-start | bytes 1671176 | tf_op jit(solution)/shard_map/ppermute | solution.py:465
  11.2 10.7 %collective-permute-start.3 = (bf16[544,128]{1,0:T(8,128)(2,1)S(1)}, bf16[544,128]{1,0:T(8,128)(2,1)S(1)}, u32[]{:S(2)}, u32[]{:S(2)}) collective-permute-start(bf16[544,128]{1,0:T(8,128)(2,1)S(1)} %get-tuple-element.41), channel_id=1, source_target_pairs={{0,64},{16,208},{32,96},{48,240},{64,128},{80,16},{96,160},{112,48... | collective-permute-start | bytes 417800 | tf_op jit(solution)/shard_map/ppermute | solution.py:469
  15.5 6.4 %collective-permute-start.4 = (bf16[544,128]{1,0:T(8,128)(2,1)S(1)}, bf16[544,128]{1,0:T(8,128)(2,1)S(1)}, u32[]{:S(2)}, u32[]{:S(2)}) collective-permute-start(bf16[544,128]{1,0:T(8,128)(2,1)S(1)} %get-tuple-element.42), channel_id=1, source_target_pairs={{0,32},{16,240},{32,64},{48,16},{64,96},{80,48},{96,128},{112,80},... | collective-permute-start | bytes 417800 | tf_op jit(solution)/shard_map/ppermute | solution.py:469
  16.3 6.1 %collective-permute-start.5 = (bf16[544,128]{1,0:T(8,128)(2,1)S(1)}, bf16[544,128]{1,0:T(8,128)(2,1)S(1)}, u32[]{:S(2)}, u32[]{:S(2)}) collective-permute-start(bf16[544,128]{1,0:T(8,128)(2,1)S(1)} %get-tuple-element.43), channel_id=1, source_target_pairs={{0,32},{16,240},{32,64},{48,16},{64,96},{80,48},{96,128},{112,80},... | collective-permute-start | bytes 417800 | tf_op jit(solution)/shard_map/ppermute | solution.py:469
  17.1 4.6 %collective-permute-start.2 = (f32[4,32]{1,0:T(4,128)S(1)}, f32[4,32]{1,0:T(4,128)S(1)}, u32[]{:S(2)}, u32[]{:S(2)}) collective-permute-start(f32[4,32]{1,0:T(4,128)S(1)} %bitcast.40), channel_id=1, source_target_pairs={{0,0},{1,1},{2,2},{3,3},{4,4},{5,5},{6,6},{7,7},{8,8},{9,9},{10,10... | collective-permute-start | bytes 1544 | tf_op jit(solution)/shard_map/ppermute | solution.py:438
  22.5 5.7 %collective-permute-start.7 = (bf16[64,128]{1,0:T(8,128)(2,1)S(1)}, bf16[64,128]{1,0:T(8,128)(2,1)S(1)}, u32[]{:S(2)}, u32[]{:S(2)}) collective-permute-start(bf16[64,128]{1,0:T(8,128)(2,1)S(1)} %select_convert_fusion), channel_id=1, source_target_pairs={{0,16},{16,0},{32,48},{48,32},{64,80},{80,64},{96,112},{112,96},{1... | collective-permute-start | bytes 49160 | tf_op jit(solution)/shard_map/ppermute | solution.py:465
  23.8 6.3 %collective-permute-start.6 = (bf16[544,128]{1,0:T(8,128)(2,1)S(1)}, bf16[544,128]{1,0:T(8,128)(2,1)S(1)}, u32[]{:S(2)}, u32[]{:S(2)}) collective-permute-start(bf16[544,128]{1,0:T(8,128)(2,1)S(1)} %fusion), channel_id=1, source_target_pairs={{0,32},{16,240},{32,64},{48,16},{64,96},{80,48},{96,128},{112,80},... | collective-permute-start | bytes 417800 | tf_op jit(solution)/shard_map/ppermute | solution.py:469
  28.1 5.2 %collective-permute-start.9 = (bf16[544,128]{1,0:T(8,128)(2,1)S(1)}, bf16[544,128]{1,0:T(8,128)(2,1)S(1)}, u32[]{:S(2)}, u32[]{:S(2)}) collective-permute-start(bf16[544,128]{1,0:T(8,128)(2,1)S(1)} %fusion.2), channel_id=1, source_target_pairs={{0,32},{16,240},{32,64},{48,16},{64,96},{80,48},{96,128},{112,80},... | collective-permute-start | bytes 417800 | tf_op jit(solution)/shard_map/ppermute | solution.py:469
  30.1 5.2 %collective-permute-start.8 = (bf16[544,128]{1,0:T(8,128)(2,1)S(1)}, bf16[544,128]{1,0:T(8,128)(2,1)S(1)}, u32[]{:S(2)}, u32[]{:S(2)}) collective-permute-start(bf16[544,128]{1,0:T(8,128)(2,1)S(1)} %add_convert_fusion.1), channel_id=1, source_target_pairs={{0,32},{16,240},{32,64},{48,16},{64,96},{80,48},{96,128},{112,80},... | collective-permute-start | bytes 417800 | tf_op jit(solution)/shard_map/ppermute | solution.py:469
  33.3 4.0 %collective-permute-start.10 = (bf16[544,128]{1,0:T(8,128)(2,1)S(1)}, bf16[544,128]{1,0:T(8,128)(2,1)S(1)}, u32[]{:S(2)}, u32[]{:S(2)}) collective-permute-start(bf16[544,128]{1,0:T(8,128)(2,1)S(1)} %add_convert_fusion), channel_id=1, source_target_pairs={{0,32},{16,240},{32,64},{48,16},{64,96},{80,48},{96,128},{112,80},... | collective-permute-start | bytes 417800 | tf_op jit(solution)/shard_map/ppermute | solution.py:469
  37.4 3.6 %collective-permute-start.11 = (bf16[544,128]{1,0:T(8,128)(2,1)S(1)}, bf16[544,128]{1,0:T(8,128)(2,1)S(1)}, u32[]{:S(2)}, u32[]{:S(2)}) collective-permute-start(bf16[544,128]{1,0:T(8,128)(2,1)S(1)} %get-tuple-element.71.mine_first), channel_id=1, source_target_pairs={{0,16},{16,0},{32,48},{48,32},{64,80},{80,64},{96,112},{112,96},{1... | collective-permute-start | bytes 417800 | tf_op jit(solution)/shard_map/ppermute | solution.py:465
  40.1 1.4 %collective-permute-start.12 = (bf16[544,128]{1,0:T(8,128)(2,1)S(1)}, bf16[544,128]{1,0:T(8,128)(2,1)S(1)}, u32[]{:S(2)}, u32[]{:S(2)}) collective-permute-start(bf16[544,128]{1,0:T(8,128)(2,1)S(1)} %get-tuple-element.70.mine_second), channel_id=1, source_target_pairs={{0,16},{16,0},{32,48},{48,32},{64,80},{80,64},{96,112},{112,96},{1... | collective-permute-start | bytes 417800 | tf_op jit(solution)/shard_map/ppermute | solution.py:465
  41.4 22.2 %copy-start.1 = (bf16[4,2,256,512]{3,2,1,0:T(8,128)(2,1)S(1)}, bf16[4,2,256,512]{3,2,1,0:T(8,128)(2,1)}, u32[]{:S(2)}) copy-start(bf16[4,2,256,512]{3,2,1,0:T(8,128)(2,1)} %param.6) | copy-start | bytes 6291460
  41.4 22.2 %copy-start.2 = (bf16[8,256,512]{2,1,0:T(8,128)(2,1)S(1)}, bf16[8,256,512]{2,1,0:T(8,128)(2,1)}, u32[]{:S(2)}) copy-start(bf16[8,256,512]{2,1,0:T(8,128)(2,1)} %get-tuple-element.33.advance_ref) | copy-start | bytes 6291460
  45.5 3.9 %collective-permute-start.13 = (bf16[528,128]{1,0:T(8,128)(2,1)S(1)}, bf16[528,128]{1,0:T(8,128)(2,1)S(1)}, u32[]{:S(2)}, u32[]{:S(2)}) collective-permute-start(bf16[528,128]{1,0:T(8,128)(2,1)S(1)} %get-tuple-element.51.refs_0_), channel_id=1, source_target_pairs={{0,32},{16,240},{32,64},{48,16},{64,96},{80,48},{96,128},{112,80},... | collective-permute-start | bytes 405512 | tf_op jit(solution)/shard_map/ppermute | solution.py:469
  45.9 5.4 %collective-permute-start.14 = (bf16[528,128]{1,0:T(8,128)(2,1)S(1)}, bf16[528,128]{1,0:T(8,128)(2,1)S(1)}, u32[]{:S(2)}, u32[]{:S(2)}) collective-permute-start(bf16[528,128]{1,0:T(8,128)(2,1)S(1)} %get-tuple-element.52.refs_1_), channel_id=1, source_target_pairs={{0,32},{16,240},{32,64},{48,16},{64,96},{80,48},{96,128},{112,80},... | collective-permute-start | bytes 405512 | tf_op jit(solution)/shard_map/ppermute | solution.py:469
  49.5 3.9 %collective-permute-start.15 = (bf16[528,128]{1,0:T(8,128)(2,1)S(1)}, bf16[528,128]{1,0:T(8,128)(2,1)S(1)}, u32[]{:S(2)}, u32[]{:S(2)}) collective-permute-start(bf16[528,128]{1,0:T(8,128)(2,1)S(1)} %collective-permute-done.13.refs_2_), channel_id=1, source_target_pairs={{0,32},{16,240},{32,64},{48,16},{64,96},{80,48},{96,128},{112,80},... | collective-permute-start | bytes 405512 | tf_op jit(solution)/shard_map/ppermute | solution.py:469
  51.2 3.9 %collective-permute-start.16 = (bf16[528,128]{1,0:T(8,128)(2,1)S(1)}, bf16[528,128]{1,0:T(8,128)(2,1)S(1)}, u32[]{:S(2)}, u32[]{:S(2)}) collective-permute-start(bf16[528,128]{1,0:T(8,128)(2,1)S(1)} %collective-permute-done.14.refs_3_), channel_id=1, source_target_pairs={{0,32},{16,240},{32,64},{48,16},{64,96},{80,48},{96,128},{112,80},... | collective-permute-start | bytes 405512 | tf_op jit(solution)/shard_map/ppermute | solution.py:469
  55.1 8.5 %collective-permute-start.17 = (bf16[2112,128]{1,0:T(8,128)(2,1)S(1)}, bf16[2112,128]{1,0:T(8,128)(2,1)S(1)}, u32[]{:S(2)}, u32[]{:S(2)}) collective-permute-start(bf16[2112,128]{1,0:T(8,128)(2,1)S(1)} %pad_maximum_fusion), channel_id=1, source_target_pairs={{0,16},{16,0},{32,48},{48,32},{64,80},{80,64},{96,112},{112,96},{1... | collective-permute-start | bytes 1622024 | tf_op jit(solution)/shard_map/ppermute | solution.py:465
  59.9 8.2 %collective-permute-start.18 = (bf16[528,128]{1,0:T(8,128)(2,1)S(1)}, bf16[528,128]{1,0:T(8,128)(2,1)S(1)}, u32[]{:S(2)}, u32[]{:S(2)}) collective-permute-start(bf16[528,128]{1,0:T(8,128)(2,1)S(1)} %collective-permute-done.15.refs_5_), channel_id=1, source_target_pairs={{0,32},{16,240},{32,64},{48,16},{64,96},{80,48},{96,128},{112,80},... | collective-permute-start | bytes 405512 | tf_op jit(solution)/shard_map/ppermute | solution.py:469
  60.2 7.9 %collective-permute-start.19 = (bf16[528,128]{1,0:T(8,128)(2,1)S(1)}, bf16[528,128]{1,0:T(8,128)(2,1)S(1)}, u32[]{:S(2)}, u32[]{:S(2)}) collective-permute-start(bf16[528,128]{1,0:T(8,128)(2,1)S(1)} %collective-permute-done.16.refs_6_), channel_id=1, source_target_pairs={{0,32},{16,240},{32,64},{48,16},{64,96},{80,48},{96,128},{112,80},... | collective-permute-start | bytes 405512 | tf_op jit(solution)/shard_map/ppermute | solution.py:469
  60.3 10.7 %collective-permute-start.21 = (bf16[528,128]{1,0:T(8,128)(2,1)S(1)}, bf16[528,128]{1,0:T(8,128)(2,1)S(1)}, u32[]{:S(2)}, u32[]{:S(2)}) collective-permute-start(bf16[528,128]{1,0:T(8,128)(2,1)S(1)} %collective-permute-done.15.refs_5_), channel_id=1, source_target_pairs={{0,64},{16,208},{32,96},{48,240},{64,128},{80,16},{96,160},{112,48... | collective-permute-start | bytes 405512 | tf_op jit(solution)/shard_map/ppermute | solution.py:469
  68.2 4.2 %collective-permute-start.20 = (bf16[1056,128]{1,0:T(8,128)(2,1)S(1)}, bf16[1056,128]{1,0:T(8,128)(2,1)S(1)}, u32[]{:S(2)}, u32[]{:S(2)}) collective-permute-start(bf16[1056,128]{1,0:T(8,128)(2,1)S(1)} %maximum_add_fusion), channel_id=1, source_target_pairs={{0,16},{16,0},{32,48},{48,32},{64,80},{80,64},{96,112},{112,96},{1... | collective-permute-start | bytes 811016 | tf_op jit(solution)/shard_map/ppermute | solution.py:465
  71.0 1.4 %collective-permute-start.22 = (bf16[528,128]{1,0:T(8,128)(2,1)S(1)}, bf16[528,128]{1,0:T(8,128)(2,1)S(1)}, u32[]{:S(2)}, u32[]{:S(2)}) collective-permute-start(bf16[528,128]{1,0:T(8,128)(2,1)S(1)} %broadcast_add_fusion), channel_id=1, source_target_pairs={{0,16},{16,0},{32,48},{48,32},{64,80},{80,64},{96,112},{112,96},{1... | collective-permute-start | bytes 405512 | tf_op jit(solution)/shard_map/ppermute | solution.py:465
